TPU v7x, 32 devices: a whole 2x2x4 slice. The times are simulated.
32 devices in a mesh: seq: 8 (over z, x), doc: 4 (over y, core).
Axes of the slice: x: 2, y: 2, z: 4, core: 2. Of those that a mesh axis runs over, the one named last changes fastest.
Arguments:
- arriving_features: bfloat16 [8, 1024, 1024], P('doc', 'seq'), may hold values from -6 to 6
- valid_extents: int32 [8], P('doc'), may hold values from 256 to 1024, as said below
- sampled_target_tiles: int32 [8, 16, 16, 3], P('doc'), may hold values from 0 to 15
- query_context_mapping: bfloat16 [1024, 3072], P(('seq', 'doc')), may hold values from -0.1875 to 0.1875
- attention_outflow_weights: bfloat16 [1024, 1024], P(('seq', 'doc')), may hold values from -1.5 to 1.5
- expansion_weights: bfloat16 [1024, 4096], P(('seq', 'doc')), may hold values from -0.1875 to 0.1875
- contraction_weights: bfloat16 [4096, 1024], P(('seq', 'doc')), may hold values from -0.09375 to 0.09375
- opening_scale_vector: bfloat16 [1024], P(('seq', 'doc')), may hold values from 0.5 to 1.5
- opening_shift_vector: bfloat16 [1024], P(('seq', 'doc')), may hold values from -1 to 1
- closing_scale_vector: bfloat16 [1024], P(('seq', 'doc')), may hold values from 0.5 to 1.5
- closing_shift_vector: bfloat16 [1024], P(('seq', 'doc')), may hold values from -1 to 1
- expansion_shift: bfloat16 [4096], P(('seq', 'doc')), may hold values from -1 to 1
- contraction_shift: bfloat16 [1024], P(('seq', 'doc')), may hold values from -1.5 to 1.5
- output_sensitivity: bfloat16 [8, 1024, 1024], P('doc', 'seq'), may hold values from -6 to 6
Outputs:
- output: bfloat16 [8, 1024, 1024], P('doc', 'seq')
- grad_inputs: float32 [8, 1024, 1024], P('doc', 'seq')
- inward_grad: float32 [1024, 3072], P(('seq', 'doc'))
- outward_grad: float32 [1024, 1024], P(('seq', 'doc'))
- expand_grad: float32 [1024, 4096], P(('seq', 'doc'))
- contract_grad: float32 [4096, 1024], P(('seq', 'doc'))
- leading_gain_sensitivity: float32 [1024], P(('seq', 'doc'))
- leading_offset_sensitivity: float32 [1024], P(('seq', 'doc'))
- midscale_grad: float32 [1024], P(('seq', 'doc'))
- midshift_grad: float32 [1024], P(('seq', 'doc'))
- upshift_grad: float32 [4096], P(('seq', 'doc'))
- downshift_grad: float32 [1024], P(('seq', 'doc'))
Inputs may be any that keep to these rules, and one draw needn't show every extreme that they name: `valid_extents`: of the 2 documents on each index of doc (that many in a row), one has length 1024.
All inputs are finite; a program needn't handle non-finite values.
Results may differ from a plain program's by a relative error of at most 0.014.
Values may be sent and summed in bfloat16 or wider, within the bound.
A program may use at most 512 MiB of HBM per device.

v0:
```python
import jax
import jax.numpy as jnp
from jax import lax
from jax.sharding import PartitionSpec as P

group_heads = 4
epsilon = 1e-05
negative = -1e30


def normalise_each_line(values, scaling, shifting):
    centered = values - jnp.mean(values, axis=-1, keepdims=True)
    inverse = lax.rsqrt(jnp.mean(centered * centered, axis=-1, keepdims=True) + epsilon)
    scaled = centered * inverse
    return (scaled * scaling + shifting, scaled, inverse)


def standardize_rows_pullback(grad_norm, scaled, inverse, scaling):
    grad_scaled = grad_norm * scaling
    centred_grad = grad_scaled - jnp.mean(grad_scaled, axis=-1, keepdims=True)
    centred_grad = centred_grad - scaled * jnp.mean(grad_scaled * scaled, axis=-1, keepdims=True)
    return (centred_grad * inverse, jnp.sum(grad_norm * scaled, axis=0), jnp.sum(grad_norm, axis=0))


def exact_gelu(values):
    return jax.nn.gelu(values, approximate=False)


def dense_width():
    return 8


def split_heads(array):
    return array.reshape((array.shape[0] // group_heads, group_heads) + array.shape[1:])


def join_heads(array):
    return array.reshape((array.shape[0] * array.shape[1],) + array.shape[2:])


def candidate_table(span_number, drawn_ordering, first_block, local_blocks, block_size):
    head_count, slot_blocks, random_count = drawn_ordering.shape
    query_blocks = first_block + jnp.arange(local_blocks, dtype=jnp.int32)
    last_block = (span_number - 1) // block_size
    picked = lax.dynamic_slice_in_dim(drawn_ordering, first_block, local_blocks, 1)
    window = jnp.stack([query_blocks - 1, query_blocks, query_blocks + 1], axis=1)
    edges = jnp.stack(
        [jnp.zeros_like(query_blocks), jnp.zeros_like(query_blocks) + last_block], axis=1
    )
    window = jnp.broadcast_to(window[None], (head_count, local_blocks, 3))
    edges = jnp.broadcast_to(edges[None], (head_count, local_blocks, 2))
    candidates = jnp.concatenate([window, picked, edges], axis=2)
    candidate_count = candidates.shape[2]
    inside = (candidates >= 0) & (candidates < slot_blocks)
    earlier = jnp.arange(candidate_count)[:, None] > jnp.arange(candidate_count)[None, :]
    repeated = jnp.any((candidates[:, :, :, None] == candidates[:, :, None, :]) & earlier, axis=3)
    usable = inside & jnp.logical_not(repeated)
    clipped = jnp.clip(candidates, 0, slot_blocks - 1)
    places = clipped[:, :, :, None] * block_size + jnp.arange(block_size, dtype=jnp.int32)
    keep = usable[:, :, :, None] & (places < span_number)
    flags = (query_blocks == 0) | (query_blocks == last_block)
    return (clipped, keep, flags)


def select_blocks(rows, clipped, block_size):
    slot_size, head_count, head_dim = rows.shape
    shaped = rows.reshape(slot_size // block_size, block_size, head_count, head_dim)
    head_index = jnp.arange(head_count, dtype=jnp.int32)[:, None, None]
    return shaped[clipped, :, head_index, :]


def sparse_forward(parts):
    query_group, key_group, value_group, keep_group = parts
    scale = query_group.shape[-1] ** (-0.5)
    scores = (
        jnp.einsum("hitd,hickd->hitck", query_group, key_group, preferred_element_type=jnp.float32)
        * scale
    )
    scores = jnp.where(keep_group[:, :, None], scores, negative)
    shape = scores.shape
    flat = scores.reshape(shape[0], shape[1], shape[2], shape[3] * shape[4])
    highest = jnp.max(flat, axis=-1, keepdims=True)
    weights_exp = jnp.exp(flat - highest)
    totals = jnp.sum(weights_exp, axis=-1, keepdims=True)
    chances_low = (weights_exp / totals).astype(jnp.bfloat16).reshape(shape)
    mixed = jnp.einsum(
        "hitck,hickd->hitd", chances_low, value_group, preferred_element_type=jnp.float32
    )
    return (mixed, (highest + jnp.log(totals))[..., 0])


def sparse_backward(parts):
    query_group, key_group, value_group, keep_group, log_group, grad_group = parts
    scale = query_group.shape[-1] ** (-0.5)
    scores = (
        jnp.einsum("hitd,hickd->hitck", query_group, key_group, preferred_element_type=jnp.float32)
        * scale
    )
    scores = jnp.where(keep_group[:, :, None], scores, negative)
    chances = jnp.exp(scores - log_group[..., None, None])
    grad_chances = jnp.einsum(
        "hitd,hickd->hitck", grad_group, value_group, preferred_element_type=jnp.float32
    )
    central = jnp.sum(chances * grad_chances, axis=(3, 4), keepdims=True)
    grad_scores = (chances * (grad_chances - central)).astype(jnp.bfloat16)
    query_term = (
        jnp.einsum("hitck,hickd->hitd", grad_scores, key_group, preferred_element_type=jnp.float32)
        * scale
    )
    key_term = (
        jnp.einsum(
            "hitck,hitd->hickd", grad_scores, query_group, preferred_element_type=jnp.float32
        )
        * scale
    )
    value_term = jnp.einsum(
        "hitck,hitd->hickd",
        chances.astype(jnp.bfloat16),
        grad_group,
        preferred_element_type=jnp.float32,
    )
    return (query_term, key_term, value_term)


def dense_forward(query_block, key_rows, value_rows, span_number):
    block_size, head_count, head_dim = query_block.shape
    width_group = dense_width()
    scale = head_dim ** (-0.5)
    valid = jnp.arange(key_rows.shape[0], dtype=jnp.int32) < span_number

    def one_group(number):
        offset = number * width_group
        query_part = lax.dynamic_slice_in_dim(query_block, offset, width_group, 1)
        key_part = lax.dynamic_slice_in_dim(key_rows, offset, width_group, 1)
        value_part = lax.dynamic_slice_in_dim(value_rows, offset, width_group, 1)
        scores = (
            jnp.einsum("tgd,kgd->gtk", query_part, key_part, preferred_element_type=jnp.float32)
            * scale
        )
        scores = jnp.where(valid[None, None, :], scores, negative)
        highest = jnp.max(scores, axis=-1, keepdims=True)
        weights_exp = jnp.exp(scores - highest)
        totals = jnp.sum(weights_exp, axis=-1, keepdims=True)
        chances_low = (weights_exp / totals).astype(jnp.bfloat16)
        mixed = jnp.einsum(
            "gtk,kgd->gtd", chances_low, value_part, preferred_element_type=jnp.float32
        )
        return (mixed, (highest + jnp.log(totals))[:, :, 0])

    mixed_all, logs_all = lax.map(one_group, jnp.arange(head_count // width_group, dtype=jnp.int32))
    mixed_all = mixed_all.reshape(head_count, block_size, head_dim).transpose(1, 0, 2)
    return (mixed_all, logs_all.reshape(head_count, block_size))


def dense_skip(query_block, key_rows, value_rows, span_number):
    block_size, head_count, head_dim = query_block.shape
    return (
        jnp.zeros((block_size, head_count, head_dim), jnp.float32),
        jnp.zeros((head_count, block_size), jnp.float32),
    )


def dense_back(query_block, grad_block, key_rows, value_rows, log_block, span_number):
    block_size, head_count, head_dim = query_block.shape
    slot_size = key_rows.shape[0]
    width_group = dense_width()
    scale = head_dim ** (-0.5)
    valid = jnp.arange(slot_size, dtype=jnp.int32) < span_number

    def one_group(number):
        offset = number * width_group
        query_part = lax.dynamic_slice_in_dim(query_block, offset, width_group, 1)
        grad_part = lax.dynamic_slice_in_dim(grad_block, offset, width_group, 1)
        key_part = lax.dynamic_slice_in_dim(key_rows, offset, width_group, 1)
        value_part = lax.dynamic_slice_in_dim(value_rows, offset, width_group, 1)
        scores = (
            jnp.einsum("tgd,kgd->gtk", query_part, key_part, preferred_element_type=jnp.float32)
            * scale
        )
        scores = jnp.where(valid[None, None, :], scores, negative)
        chances = jnp.exp(
            scores - lax.dynamic_slice_in_dim(log_block, offset, width_group, 0)[:, :, None]
        )
        grad_chances = jnp.einsum(
            "tgd,kgd->gtk", grad_part, value_part, preferred_element_type=jnp.float32
        )
        central = jnp.sum(chances * grad_chances, axis=-1, keepdims=True)
        grad_scores = (chances * (grad_chances - central)).astype(jnp.bfloat16)
        query_new = (
            jnp.einsum("gtk,kgd->gtd", grad_scores, key_part, preferred_element_type=jnp.float32)
            * scale
        )
        key_new = (
            jnp.einsum("gtk,tgd->gkd", grad_scores, query_part, preferred_element_type=jnp.float32)
            * scale
        )
        value_new = jnp.einsum(
            "gtk,tgd->gkd",
            chances.astype(jnp.bfloat16),
            grad_part,
            preferred_element_type=jnp.float32,
        )
        return (key_new, value_new, query_new)

    key_all, value_all, query_all = lax.map(
        one_group, jnp.arange(head_count // width_group, dtype=jnp.int32)
    )
    slot_terms = jnp.stack(
        [
            key_all.reshape(head_count, slot_size, head_dim),
            value_all.reshape(head_count, slot_size, head_dim),
        ]
    )
    return (slot_terms, query_all.reshape(head_count, block_size, head_dim).transpose(1, 0, 2))


def dense_pass(query_block, grad_block, key_rows, value_rows, log_block, span_number):
    block_size, head_count, head_dim = query_block.shape
    return (
        jnp.zeros((2, head_count, key_rows.shape[0], head_dim), jnp.float32),
        jnp.zeros(query_block.shape, jnp.float32),
    )


def return_grads(slot_grads):
    owned = lax.psum_scatter(
        slot_grads.astype(jnp.bfloat16), "seq", scatter_dimension=2, tiled=True
    ).astype(jnp.float32)
    pair_count, head_count, tok_count, head_dim = owned.shape
    return owned.transpose(2, 0, 1, 3).reshape(tok_count, pair_count * head_count * head_dim)


def flagged_place(flags):
    return jnp.sum(jnp.where(flags, jnp.arange(flags.shape[0], dtype=jnp.int32), 0))


def local(
    arriving_features,
    valid_extents,
    sampled_target_tiles,
    query_context_mapping,
    attention_outflow_weights,
    expansion_weights,
    contraction_weights,
    opening_scale_vector,
    opening_shift_vector,
    closing_scale_vector,
    closing_shift_vector,
    expansion_shift,
    contraction_shift,
    output_sensitivity,
):
    doc_count, tok_count, feature_breadth = arriving_features.shape
    head_count = sampled_target_tiles.shape[1]
    slot_blocks = sampled_target_tiles.shape[2]
    head_dim = feature_breadth // head_count
    slot_size = tok_count * lax.axis_size("seq")
    block_size = slot_size // slot_blocks
    local_blocks = tok_count // block_size
    first_block = lax.axis_index("seq") * local_blocks
    per_line_summation = doc_count * tok_count
    (
        full_inward,
        entire_outflow,
        full_expand,
        full_contract,
        overall_premultiplier,
        overall_shift_term,
        full_midscale,
        full_midshift,
        full_upshift,
        full_downshift,
    ) = (
        lax.all_gather(query_context_mapping, ("seq", "doc"), axis=0, tiled=True),
        lax.all_gather(attention_outflow_weights, ("seq", "doc"), axis=0, tiled=True),
        lax.all_gather(expansion_weights, ("seq", "doc"), axis=0, tiled=True),
        lax.all_gather(contraction_weights, ("seq", "doc"), axis=0, tiled=True),
        lax.all_gather(opening_scale_vector, ("seq", "doc"), axis=0, tiled=True),
        lax.all_gather(opening_shift_vector, ("seq", "doc"), axis=0, tiled=True),
        lax.all_gather(closing_scale_vector, ("seq", "doc"), axis=0, tiled=True),
        lax.all_gather(closing_shift_vector, ("seq", "doc"), axis=0, tiled=True),
        lax.all_gather(expansion_shift, ("seq", "doc"), axis=0, tiled=True),
        lax.all_gather(contraction_shift, ("seq", "doc"), axis=0, tiled=True),
    )
    shortcut_holder = arriving_features.reshape(per_line_summation, feature_breadth).astype(
        jnp.float32
    )
    opening_normalised, scaled_one, inverse_one = normalise_each_line(
        shortcut_holder,
        overall_premultiplier.astype(jnp.float32),
        overall_shift_term.astype(jnp.float32),
    )
    opening_normalised = opening_normalised.astype(jnp.bfloat16)
    projected = jnp.dot(opening_normalised, full_inward, preferred_element_type=jnp.float32).astype(
        jnp.bfloat16
    )
    query_local = projected[:, :feature_breadth].reshape(doc_count, tok_count, head_count, head_dim)
    pair_local = projected[:, feature_breadth:].reshape(doc_count, tok_count, 2 * feature_breadth)
    pair_full = lax.all_gather(pair_local, "seq", axis=1, tiled=True)

    def table_one(span_number, drawn_ordering):
        return candidate_table(span_number, drawn_ordering, first_block, local_blocks, block_size)

    clipped_all, keep_all, flags_all = jax.vmap(table_one)(valid_extents, sampled_target_tiles)
    query_heads = query_local.reshape(
        doc_count, local_blocks, block_size, head_count, head_dim
    ).transpose(0, 3, 1, 2, 4)
    block_flags = flags_all[:, :, None, None, None]

    def doc_forward(items):
        queries, pair_rows, clipped, keep = items
        key_sel = select_blocks(
            pair_rows[:, :feature_breadth].reshape(slot_size, head_count, head_dim),
            clipped,
            block_size,
        )
        value_sel = select_blocks(
            pair_rows[:, feature_breadth:].reshape(slot_size, head_count, head_dim),
            clipped,
            block_size,
        )
        mixed, log_sums = lax.map(
            sparse_forward,
            (split_heads(queries), split_heads(key_sel), split_heads(value_sel), split_heads(keep)),
        )
        return (join_heads(mixed), join_heads(log_sums))

    sparse_mixed, sparse_logs = lax.map(
        doc_forward, (query_heads, pair_full, clipped_all, keep_all)
    )
    mixed_rows = sparse_mixed.transpose(0, 2, 3, 1, 4)

    def doc_dense(items):
        queries, pair_rows, span_number, flags = items
        key_rows = pair_rows[:, :feature_breadth].reshape(slot_size, head_count, head_dim)
        value_rows = pair_rows[:, feature_breadth:].reshape(slot_size, head_count, head_dim)
        query_block = lax.dynamic_slice_in_dim(
            queries, flagged_place(flags) * block_size, block_size, 0
        )
        return lax.cond(
            jnp.any(flags),
            dense_forward,
            dense_skip,
            query_block,
            key_rows,
            value_rows,
            span_number,
        )

    dense_mixed, dense_logs = lax.map(doc_dense, (query_local, pair_full, valid_extents, flags_all))
    mixed_rows = jnp.where(block_flags, dense_mixed[:, None], mixed_rows)
    context_mixture = mixed_rows.reshape(per_line_summation, feature_breadth).astype(jnp.bfloat16)
    intermediate_state = shortcut_holder + jnp.dot(
        context_mixture, entire_outflow, preferred_element_type=jnp.float32
    )
    normed_two, scaled_two, inverse_two = normalise_each_line(
        intermediate_state, full_midscale.astype(jnp.float32), full_midshift.astype(jnp.float32)
    )
    normed_two = normed_two.astype(jnp.bfloat16)
    pre_act = jnp.dot(
        normed_two, full_expand, preferred_element_type=jnp.float32
    ) + full_upshift.astype(jnp.float32)
    activated = exact_gelu(pre_act).astype(jnp.bfloat16)
    final_rows = (
        intermediate_state
        + jnp.dot(activated, full_contract, preferred_element_type=jnp.float32)
        + full_downshift.astype(jnp.float32)
    )
    output = final_rows.astype(jnp.bfloat16).reshape(doc_count, tok_count, feature_breadth)
    back_inward, back_outward, back_expand, back_contract, back_prescale, back_midscale = (
        full_inward,
        entire_outflow,
        full_expand,
        full_contract,
        overall_premultiplier,
        full_midscale,
    )
    grad_out_rows = output_sensitivity.reshape(per_line_summation, feature_breadth)
    grad_out_wide = grad_out_rows.astype(jnp.float32)
    contract_grad = jnp.einsum(
        "rf,rd->fd", activated, grad_out_rows, preferred_element_type=jnp.float32
    )
    downshift_grad = jnp.sum(grad_out_wide, axis=0)
    grad_act = jnp.einsum(
        "rd,fd->rf", grad_out_rows, back_contract, preferred_element_type=jnp.float32
    )
    unused_value, gelu_back = jax.vjp(exact_gelu, pre_act)
    grad_pre = gelu_back(grad_act)[0].astype(jnp.bfloat16)
    expand_grad = jnp.einsum("rd,rf->df", normed_two, grad_pre, preferred_element_type=jnp.float32)
    upshift_grad = jnp.sum(grad_pre.astype(jnp.float32), axis=0)
    grad_norm_two = jnp.einsum(
        "rf,df->rd", grad_pre, back_expand, preferred_element_type=jnp.float32
    )
    middle_part, midscale_grad, midshift_grad = standardize_rows_pullback(
        grad_norm_two, scaled_two, inverse_two, back_midscale.astype(jnp.float32)
    )
    grad_middle = grad_out_wide + middle_part
    grad_branch = grad_middle.astype(jnp.bfloat16)
    outward_grad = jnp.einsum(
        "rd,re->de", context_mixture, grad_branch, preferred_element_type=jnp.float32
    )
    grad_attended = jnp.einsum(
        "re,de->rd", grad_branch, back_outward, preferred_element_type=jnp.float32
    ).astype(jnp.bfloat16)
    grad_attended = grad_attended.reshape(doc_count, tok_count, head_count, head_dim)
    grad_blocks = grad_attended.reshape(doc_count, local_blocks, block_size, head_count, head_dim)
    sparse_grads = jnp.where(block_flags, jnp.zeros_like(grad_blocks), grad_blocks).transpose(
        0, 3, 1, 2, 4
    )
    block_ids = jnp.arange(slot_blocks, dtype=jnp.int32)

    def sparse_back(queries, pair_rows, clipped, keep, log_sums, grad_part):
        key_rows = pair_rows[:, :feature_breadth].reshape(slot_size, head_count, head_dim)
        value_rows = pair_rows[:, feature_breadth:].reshape(slot_size, head_count, head_dim)
        key_sel = select_blocks(key_rows, clipped, block_size)
        value_sel = select_blocks(value_rows, clipped, block_size)
        grouped = (
            split_heads(queries),
            split_heads(key_sel),
            split_heads(value_sel),
            split_heads(keep),
            split_heads(log_sums),
            split_heads(grad_part),
        )
        query_term, key_term, value_term = lax.map(sparse_backward, grouped)
        query_term = join_heads(query_term)
        key_term = join_heads(key_term)
        value_term = join_heads(value_term)
        placing = (clipped[..., None] == block_ids).astype(jnp.float32)
        key_slot = jnp.einsum(
            "hlcn,hlcbd->hnbd",
            placing,
            key_term,
            precision=lax.Precision.HIGHEST,
            preferred_element_type=jnp.float32,
        )
        value_slot = jnp.einsum(
            "hlcn,hlcbd->hnbd",
            placing,
            value_term,
            precision=lax.Precision.HIGHEST,
            preferred_element_type=jnp.float32,
        )
        slot_grads = jnp.stack(
            [
                key_slot.reshape(head_count, slot_size, head_dim),
                value_slot.reshape(head_count, slot_size, head_dim),
            ]
        )
        return (query_term, slot_grads, key_rows, value_rows)

    def doc_backward(carry, items):
        (
            queries,
            pair_rows,
            clipped,
            keep,
            log_sums,
            grad_part,
            grad_rows,
            query_rows,
            dense_log,
            span_number,
            flags,
        ) = items
        query_term, slot_grads, key_rows, value_rows = sparse_back(
            queries, pair_rows, clipped, keep, log_sums, grad_part
        )
        start = flagged_place(flags) * block_size
        query_block = lax.dynamic_slice_in_dim(query_rows, start, block_size, 0)
        grad_block = lax.dynamic_slice_in_dim(grad_rows, start, block_size, 0)
        dense_slot, dense_term = lax.cond(
            jnp.any(flags),
            dense_back,
            dense_pass,
            query_block,
            grad_block,
            key_rows,
            value_rows,
            dense_log,
            span_number,
        )
        owned = return_grads(slot_grads + dense_slot)
        return (carry, (query_term, dense_term, owned))

    unused_carry, (sparse_query, dense_query, pair_grads) = lax.scan(
        doc_backward,
        jnp.zeros((), jnp.int32),
        (
            query_heads,
            pair_full,
            clipped_all,
            keep_all,
            sparse_logs,
            sparse_grads,
            grad_attended,
            query_local,
            dense_logs,
            valid_extents,
            flags_all,
        ),
    )
    query_grad = sparse_query.transpose(0, 2, 3, 1, 4) + jnp.where(
        block_flags, dense_query[:, None], 0.0
    )
    grad_projected = jnp.concatenate(
        [
            query_grad.reshape(per_line_summation, feature_breadth),
            pair_grads.reshape(per_line_summation, 2 * feature_breadth),
        ],
        axis=1,
    ).astype(jnp.bfloat16)
    inward_grad = jnp.einsum(
        "rd,re->de", opening_normalised, grad_projected, preferred_element_type=jnp.float32
    )
    grad_norm_one = jnp.einsum(
        "re,de->rd", grad_projected, back_inward, preferred_element_type=jnp.float32
    )
    incoming_slice, leading_gain_sensitivity, leading_offset_sensitivity = (
        standardize_rows_pullback(
            grad_norm_one, scaled_one, inverse_one, back_prescale.astype(jnp.float32)
        )
    )
    grad_inputs = (grad_middle + incoming_slice).reshape(doc_count, tok_count, feature_breadth)
    summed = (
        lax.psum_scatter(inward_grad, ("seq", "doc"), scatter_dimension=0, tiled=True),
        lax.psum_scatter(outward_grad, ("seq", "doc"), scatter_dimension=0, tiled=True),
        lax.psum_scatter(expand_grad, ("seq", "doc"), scatter_dimension=0, tiled=True),
        lax.psum_scatter(contract_grad, ("seq", "doc"), scatter_dimension=0, tiled=True),
        lax.psum_scatter(leading_gain_sensitivity, ("seq", "doc"), scatter_dimension=0, tiled=True),
        lax.psum_scatter(
            leading_offset_sensitivity, ("seq", "doc"), scatter_dimension=0, tiled=True
        ),
        lax.psum_scatter(midscale_grad, ("seq", "doc"), scatter_dimension=0, tiled=True),
        lax.psum_scatter(midshift_grad, ("seq", "doc"), scatter_dimension=0, tiled=True),
        lax.psum_scatter(upshift_grad, ("seq", "doc"), scatter_dimension=0, tiled=True),
        lax.psum_scatter(downshift_grad, ("seq", "doc"), scatter_dimension=0, tiled=True),
    )
    return (output, grad_inputs) + tuple(summed)


def solution(mesh):
    return jax.shard_map(
        local,
        mesh=mesh,
        in_specs=(
            P("doc", "seq", None),
            P("doc"),
            P("doc", None, None, None),
            P(("seq", "doc"), None),
            P(("seq", "doc"), None),
            P(("seq", "doc"), None),
            P(("seq", "doc"), None),
            P(("seq", "doc")),
            P(("seq", "doc")),
            P(("seq", "doc")),
            P(("seq", "doc")),
            P(("seq", "doc")),
            P(("seq", "doc")),
            P("doc", "seq", None),
        ),
        out_specs=(
            P("doc", "seq", None),
            P("doc", "seq", None),
            P(("seq", "doc"), None),
            P(("seq", "doc"), None),
            P(("seq", "doc"), None),
            P(("seq", "doc"), None),
            P(("seq", "doc")),
            P(("seq", "doc")),
            P(("seq", "doc")),
            P(("seq", "doc")),
            P(("seq", "doc")),
            P(("seq", "doc")),
        ),
        check_vma=False,
    )
```

profile of v0, /device:TPU:0, one launch (start us, length us, event | category | flops | bytes accessed | tf_op | source)
XLA Modules:
  0.0 1738.3 jit_solution(1673767277403234417)
XLA Ops:
  12.2 42.4 %all-reduce.13 = (bf16[1024]{0:T(1024)(128)(2,1)S(1)}, bf16[1024]{0:T(1024)(128)(2,1)S(1)}, bf16[1024]{0:T(1024)(128)(2,1)S(1)}, bf16[1024]{0:T(1024)(128)(2,1)S(1)}, bf16[1024]{0:T(1024)(128)(2,1)}) all-reduce(bf16[1024]{0:T(1024)(128)(2,1)S(1)} %dynamic-update-slice.2, ...), channel_id=1, replica_groups=mesh['seq'=8,'doc'=4] {'seq','doc'}, use_global_device_ids=true, to_apply=%add.2 | all-reduce | flops 5120 | bytes 20480
  59.1 24.3 %all-gather.7.cloned.1.call-done = bf16[1024,3072]{1,0:T(8,128)(2,1)} async-done(((bf16[32,3072]{1,0:T(8,128)(2,1)}), bf16[1024,3072]{1,0:T(8,128)(2,1)}) %all-gather.7.cloned.1.call-update) | async-done | bytes 6291472 | tf_op jit(solution)/shard_map/all_gather | solution.py:274
  95.9 39.2 %all-gather = bf16[32,1,128]{2,1,0:T(2,128)(2,1)S(1)} all-gather(bf16[1,1,128]{2,1,0:T(2,128)(2,1)S(1)} %bitcast.452), channel_id=1, replica_groups=mesh['seq'=8,'doc'=4] {'seq','doc'}, dimensions={0}, use_global_device_ids=true | all-gather | bytes 8448 | tf_op jit(solution)/shard_map/all_gather | solution.py:282
  140.1 73.5 %all-gather.9.cloned.1.call-done = bf16[2,1024,2048]{1,2,0:T(8,128)(2,1)} async-done(((bf16[2,128,2048]{1,2,0:T(8,128)(2,1)}), bf16[2,1024,2048]{1,2,0:T(8,128)(2,1)}) %all-gather.9.cloned.1.call-update) | async-done | bytes 8388624 | tf_op jit(solution)/shard_map/all_gather | solution.py:299
  213.6 42.5 %while.171 = (s32[]{:T(128)}, bf16[2,64,16,64]{3,1,2,0:T(8,128)(2,1)}, f32[2,16,64]{2,1,0:T(8,128)}, pred[2,2]{1,0:T(4,128)(4,1)S(1)}, bf16[2,128,16,64]{3,1,2,0...) while((s32[]{:T(128)}, bf16[2,64,16,64]{3,1,2,0:T(8,128)(2,1)}, ...), condition=%wide.region_11.12_spmd.clone, body=%wide.region_2.11_spmd.sunk.clone | while | flops 140509712 | bytes 34648640 | solution.py:350
  215.4 16.7 conditional.7
  221.8 10.3 while.169
  236.4 16.8 conditional.7
  242.8 10.3 while.169
  257.1 142.5 %while.173 = (s32[]{:T(128)}, bf16[2,16,2,64,64]{4,3,2,1,0:T(8,128)(2,1)}, f32[2,16,2,64]{3,2,1,0:T(2,128)}, bf16[2,16,2,64,64]{4,3,2,1,0:T(8,128)(2,1)}, bf16[2...) while((s32[]{:T(128)}, ...), condition=%wide.region_18.19_spmd.clone, body=%wide.region_13.18_spmd.sunk.clone | while | flops 70256128 | bytes 63046040 | solution.py:328
  262.9 6.5 copy.220
  273.5 6.3 reshape.755
  305.8 21.4 %while.172 = (s32[]{:T(128)}, bf16[4,4,2,64,64]{4,3,2,1,0:T(8,128)(2,1)S(1)}, f32[4,4,2,64]{3,2,1,0:T(2,128)S(1)}, pred[4,4,2,8,64]{4,3,2,1,0:T(8,128)(4,1)S(1)}...) while((s32[]{:T(128)}, ...), condition=%wide.region_17.17_spmd, body=%wide.region_14.16_spmd.sunk | while | flops 70254080 | bytes 6742117 | solution.py:322
  334.0 6.6 copy.220
  344.7 6.5 reshape.755
  377.0 21.4 %while.172 = (s32[]{:T(128)}, bf16[4,4,2,64,64]{4,3,2,1,0:T(8,128)(2,1)S(1)}, f32[4,4,2,64]{3,2,1,0:T(2,128)S(1)}, pred[4,4,2,8,64]{4,3,2,1,0:T(8,128)(4,1)S(1)}...) while((s32[]{:T(128)}, ...), condition=%wide.region_17.17_spmd, body=%wide.region_14.16_spmd.sunk | while | flops 70254080 | bytes 6742117 | solution.py:322
  405.8 7.9 convolution_add_fusion
  413.7 15.5 all-gather.15.cloned.1.call-done
  429.2 16.9 convert_reduce_fusion
  460.4 596.2 %while.175 = (s32[]{:T(128)}, f32[2,16,2,64,64]{4,3,2,1,0:T(8,128)}, f32[2,64,16,64]{3,1,2,0:T(8,128)}, bf16[2,128,2048]{2,1,0:T(8,128)(2,1)}, bf16[2,16,2,64,64...) while((s32[]{:T(128)}, f32[2,16,2,64,64]{4,3,2,1,0:T(8,128)}, ...), condition=%wide.region_35.36_spmd.clone.clone, body=%wide.region_23.35_spmd.clone.sunk.clone | while | flops 922298368 | bytes 290053376 | solution.py:486
  469.6 6.8 copy.223
  476.6 6.5 reshape.764
  483.0 6.8 copy.224
  502.2 44.4 %while.174 = (s32[]{:T(128)}, f32[4,4,2,64,64]{4,3,2,1,0:T(8,128)}, f32[4,4,2,8,64,64]{5,4,3,2,1,0:T(8,128)}, f32[4,4,2,8,64,64]{5,4,3,2,1,0:T(8,128)}, pred[4,4...) while((s32[]{:T(128)}, f32[4,4,2,64,64]{4,3,2,1,0:T(8,128)}, ...), condition=%wide.region_26.26_spmd, body=%wide.region_24.25_spmd.sunk | while | flops 170425856 | bytes 18646140 | solution.py:425
  548.6 9.8 copy.225
  558.4 9.4 convolution_bitcast_fusion.9
  567.7 7.6 reshape.765
  575.4 9.8 copy.226
  585.2 9.3 convolution_bitcast_fusion.10
  594.5 7.6 reshape.766
  602.1 31.1 %conditional.8 = (f32[2,16,1024,64]{2,3,1,0:T(8,128)}, f32[1,64,16,64]{3,1,2,0:T(8,128)}) conditional(s32[]{:T(128)} %convert_element_type.208, () %tuple.291, (s32[]{:T(128)}, pred[1,2]{1,0:T(4,128)(4,1)S(1)}, s32[2]{0:T(128)S(1)}, bf16[2,128,16,64]{3,1,2,0:T(8,128)(2,1)}, bf16[2,128,16,64]{3,1,2,0:T(8,128)(2,1)}, ...), branch_computations={%region_28.28_spmd, %region_29.33_spmd} | conditional | flops 342917632 | bytes 108290624 | solution.py:472
  605.2 19.6 %while.170 = (s32[]{:T(128)}, f32[2,8,1024,64]{2,3,1,0:T(8,128)}, f32[2,8,1024,64]{2,3,1,0:T(8,128)}, f32[2,8,64,64]{3,2,1,0:T(8,128)}, s32[2]{0:T(128)S(1)}, /*...) while((s32[]{:T(128)}, f32[2,8,1024,64]{2,3,1,0:T(8,128)}, ...), condition=%wide.region_33.32_spmd.clone.clone, body=%wide.region_31.31_spmd.clone.sunk.clone | while | flops 340820480 | bytes 90980680 | solution.py:205
  624.8 8.3 pad_maximum_fusion
  633.2 8.7 fusion.245
  641.9 12.9 copy.227
  654.8 12.3 reshape.767
  669.4 84.6 %reduce-scatter.19.cloned.1.call-done = bf16[128,2048]{1,0:T(8,128)(2,1)} async-done(((bf16[1024,2048]{1,0:T(8,128)(2,1)}), bf16[128,2048]{1,0:T(8,128)(2,1)}) %reduce-scatter.19.cloned.1.call-update) | async-done | bytes 524304 | tf_op jit(solution)/shard_map/while
  766.8 6.8 copy.223
  773.7 6.5 reshape.764
  780.2 6.8 copy.224
  799.4 44.4 %while.174 = (s32[]{:T(128)}, f32[4,4,2,64,64]{4,3,2,1,0:T(8,128)}, f32[4,4,2,8,64,64]{5,4,3,2,1,0:T(8,128)}, f32[4,4,2,8,64,64]{5,4,3,2,1,0:T(8,128)}, pred[4,4...) while((s32[]{:T(128)}, f32[4,4,2,64,64]{4,3,2,1,0:T(8,128)}, ...), condition=%wide.region_26.26_spmd, body=%wide.region_24.25_spmd.sunk | while | flops 170425856 | bytes 18646140 | solution.py:425
  845.8 9.8 copy.225
  855.5 9.4 convolution_bitcast_fusion.9
  864.9 7.6 reshape.765
  872.5 9.8 copy.226
  882.3 9.3 convolution_bitcast_fusion.10
  891.6 7.6 reshape.766
  899.2 31.1 %conditional.8 = (f32[2,16,1024,64]{2,3,1,0:T(8,128)}, f32[1,64,16,64]{3,1,2,0:T(8,128)}) conditional(s32[]{:T(128)} %convert_element_type.208, () %tuple.291, (s32[]{:T(128)}, pred[1,2]{1,0:T(4,128)(4,1)S(1)}, s32[2]{0:T(128)S(1)}, bf16[2,128,16,64]{3,1,2,0:T(8,128)(2,1)}, bf16[2,128,16,64]{3,1,2,0:T(8,128)(2,1)}, ...), branch_computations={%region_28.28_spmd, %region_29.33_spmd} | conditional | flops 342917632 | bytes 108290624 | solution.py:472
  902.4 19.6 %while.170 = (s32[]{:T(128)}, f32[2,8,1024,64]{2,3,1,0:T(8,128)}, f32[2,8,1024,64]{2,3,1,0:T(8,128)}, f32[2,8,64,64]{3,2,1,0:T(8,128)}, s32[2]{0:T(128)S(1)}, /*...) while((s32[]{:T(128)}, f32[2,8,1024,64]{2,3,1,0:T(8,128)}, ...), condition=%wide.region_33.32_spmd.clone.clone, body=%wide.region_31.31_spmd.clone.sunk.clone | while | flops 340820480 | bytes 90980680 | solution.py:205
  922.0 8.3 pad_maximum_fusion
  930.3 8.7 fusion.245
  939.1 12.9 copy.227
  952.0 12.3 reshape.767
  966.5 85.4 %reduce-scatter.19.cloned.1.call-done = bf16[128,2048]{1,0:T(8,128)(2,1)} async-done(((bf16[1024,2048]{1,0:T(8,128)(2,1)}), bf16[128,2048]{1,0:T(8,128)(2,1)}) %reduce-scatter.19.cloned.1.call-update) | async-done | bytes 524304 | tf_op jit(solution)/shard_map/while
  1061.3 6.3 fusion.99
  1068.8 9.8 fusion.110
  1084.3 8.1 fusion.118
  1093.5 6.2 multiply_reduce_fusion.3
  1099.8 41.3 %all-reduce.12 = (f32[1024]{0:T(1024)S(1)}, f32[1024]{0:T(1024)S(1)}, f32[1024]{0:T(1024)S(1)}, f32[1024]{0:T(1024)S(1)}, f32[4096]{0:T(1024)S(1)}, /*index=5*/f32[1024]{0:T(1024)S(1)}) all-reduce(f32[1024]{0:T(1024)S(1)} %get-tuple-element.1280, ...), channel_id=7, replica_groups=mesh['seq'=8,'doc'=4] {'seq','doc'}, use_global_device_ids=true, to_apply=%region_43.44.clone | all-reduce | flops 9216 | bytes 73728
  1147.2 7.2 fusion.96
  1154.4 46.6 %reduce-scatter.13.cloned.1.call-done = f32[32,1024]{1,0:T(8,128)} async-done(((f32[1024,1024]{1,0:T(8,128)}), f32[32,1024]{1,0:T(8,128)}) %reduce-scatter.13.cloned.1.call-update) | async-done | bytes 131088 | tf_op jit(solution)/shard_map/reduce_scatter | solution.py:527
  1201.0 158.0 %reduce-scatter.11.cloned.1.call-done = f32[32,3072]{1,0:T(8,128)} async-done(((f32[1024,3072]{1,0:T(8,128)}), f32[32,3072]{1,0:T(8,128)}) %reduce-scatter.11.cloned.1.call-update) | async-done | bytes 393232 | tf_op jit(solution)/shard_map/reduce_scatter | solution.py:526
  1359.0 185.0 %reduce-scatter.15.cloned.1.call-done = f32[32,4096]{1,0:T(8,128)} async-done(((f32[1024,4096]{1,0:T(8,128)}), f32[32,4096]{1,0:T(8,128)}) %reduce-scatter.15.cloned.1.call-update) | async-done | bytes 524304 | tf_op jit(solution)/shard_map/reduce_scatter | solution.py:528
  1544.0 187.6 %reduce-scatter.17.cloned.1.call-done = f32[128,1024]{1,0:T(8,128)} async-done(((f32[4096,1024]{1,0:T(8,128)}), f32[128,1024]{1,0:T(8,128)}) %reduce-scatter.17.cloned.1.call-update) | async-done | bytes 524304 | tf_op jit(solution)/shard_map/reduce_scatter | solution.py:529
  (557 shorter events, 406.2 us)
Async XLA Ops:
  7.2 87.2 %copy-start = (s32[2,16,16,3]{2,1,3,0:T(8,128)S(1)}, s32[2,16,16,3]{2,1,3,0:T(8,128)}, u32[]{:S(2)}) copy-start(s32[2,16,16,3]{2,1,3,0:T(8,128)} %param.34) | copy-start | bytes 18436
  7.2 76.2 %all-gather.7.cloned.1.call-start = ((), (), s32[]{:S(2)}) async-start(), calls=%async_computation.5 | async-start | bytes 6488064 | tf_op jit(solution)/shard_map/all_gather | solution.py:274
  7.9 205.6 %all-gather.9.cloned.1.call-start = ((), (), s32[]{:S(2)}) async-start(), calls=%async_computation.6 | async-start | bytes 9437184 | tf_op jit(solution)/shard_map/all_gather | solution.py:299
  54.6 2.6 copy-start.40
  59.1 24.4 %copy-start.22 = (bf16[256,1024]{1,0:T(8,128)(2,1)}, bf16[256,1024]{1,0:T(8,128)(2,1)S(1)}, u32[]{:S(2)}) copy-start(bf16[256,1024]{1,0:T(8,128)(2,1)S(1)} %add_convert_fusion.2) | copy-start | bytes 1572868
  88.0 5.5 copy-start.54
  88.0 7.9 copy-start.58
  89.5 313.6 %all-gather.11.cloned.1.call-start = ((), (), s32[]{:S(2)}) async-start(), calls=%async_computation.7 | async-start | bytes 2162688 | tf_op jit(solution)/shard_map/all_gather | solution.py:275
  90.2 315.5 %all-gather.13.cloned.1.call-start = ((), (), s32[]{:S(2)}) async-start(), calls=%async_computation.8 | async-start | bytes 8650752 | tf_op jit(solution)/shard_map/all_gather | solution.py:276
  90.8 338.4 %all-gather.15.cloned.1.call-start = ((), (), s32[]{:S(2)}) async-start(), calls=%async_computation.9 | async-start | bytes 8650752 | tf_op jit(solution)/shard_map/all_gather | solution.py:277
  137.2 76.4 %copy-start.55 = (s32[2]{0:T(128)S(1)}, s32[2]{0:T(128)}, u32[]{:S(2)}) copy-start(s32[2]{0:T(128)} %param.33) | copy-start | bytes 28
  305.8 21.4 %copy-start.20 = (bf16[2,16,2,64,64]{4,3,2,1,0:T(8,128)(2,1)S(1)}, bf16[2,16,2,64,64]{4,3,2,1,0:T(8,128)(2,1)}, u32[]{:S(2)}) copy-start(bf16[2,16,2,64,64]{4,3,2,1,0:T(8,128)(2,1)} %get-tuple-element.2241) | copy-start | bytes 1572868 | tf_op jit(solution)/shard_map/while
  305.8 21.5 %copy-start.31 = (f32[2,16,2,64]{3,2,1,0:T(2,128)S(1)}, f32[2,16,2,64]{3,2,1,0:T(2,128)}, u32[]{:S(2)}) copy-start(f32[2,16,2,64]{3,2,1,0:T(2,128)} %get-tuple-element.2242) | copy-start | bytes 49156 | tf_op jit(solution)/shard_map/while
  377.0 21.4 %copy-start.20 = (bf16[2,16,2,64,64]{4,3,2,1,0:T(8,128)(2,1)S(1)}, bf16[2,16,2,64,64]{4,3,2,1,0:T(8,128)(2,1)}, u32[]{:S(2)}) copy-start(bf16[2,16,2,64,64]{4,3,2,1,0:T(8,128)(2,1)} %get-tuple-element.2241) | copy-start | bytes 1572868 | tf_op jit(solution)/shard_map/while
  377.0 21.5 %copy-start.31 = (f32[2,16,2,64]{3,2,1,0:T(2,128)S(1)}, f32[2,16,2,64]{3,2,1,0:T(2,128)}, u32[]{:S(2)}) copy-start(f32[2,16,2,64]{3,2,1,0:T(2,128)} %get-tuple-element.2242) | copy-start | bytes 49156 | tf_op jit(solution)/shard_map/while
  399.6 3.4 copy-start.12
  401.6 4.2 copy-start.29
  401.6 4.2 copy-start.34
  401.6 4.2 copy-start.47
  405.4 43.9 %copy-start.8 = (f32[256,1024]{1,0:T(8,128)}, f32[256,1024]{1,0:T(8,128)S(1)}, u32[]{:S(2)}) copy-start(f32[256,1024]{1,0:T(8,128)S(1)} %get-tuple-element.1458) | copy-start | bytes 3145732
  405.4 43.9 %copy-start.42 = (f32[256]{0:T(256)}, f32[256]{0:T(256)S(1)}, u32[]{:S(2)}) copy-start(f32[256]{0:T(256)S(1)} %broadcast_multiply_fusion.5) | copy-start | bytes 3076
  405.7 43.6 %copy-start.44 = (f32[256]{0:T(256)}, f32[256]{0:T(256)S(1)}, u32[]{:S(2)}) copy-start(f32[256]{0:T(256)S(1)} %add_rsqrt_fusion) | copy-start | bytes 3076
  405.8 23.4 %copy-start.17 = (bf16[2,128,1024]{2,1,0:T(8,128)(2,1)S(1)}, bf16[2,128,1024]{2,1,0:T(8,128)(2,1)}, u32[]{:S(2)}) copy-start(bf16[2,128,1024]{2,1,0:T(8,128)(2,1)} %param.45) | copy-start | bytes 1572868
  429.2 16.9 copy-start.59
  446.1 3.2 copy-start.26
  446.1 3.6 copy-start.16
  449.7 7.0 copy-start.10
  450.5 6.2 copy-start.38
  453.9 2.8 copy-start.19
  453.9 6.5 copy-start.33
  453.9 6.5 copy-start.36
  453.9 6.5 copy-start.56
  461.0 293.0 %reduce-scatter.19.cloned.1.call-start = ((), (), s32[]{:S(2)}) async-start(), calls=%async_computation.14 | async-start | bytes 4718592 | tf_op jit(solution)/shard_map/while
  608.8 2.2 copy-start.2
  609.7 2.8 copy-start.4
  611.5 3.1 copy-start.3
  618.6 2.2 copy-start.2
  619.5 2.8 copy-start.4
  621.3 3.1 copy-start.3
  667.2 91.0 %copy-start.39 = (pred[2,2]{1,0:T(4,128)(4,1)S(1)}, pred[2,2]{1,0:T(4,128)(4,1)}, u32[]{:S(2)}) copy-start(pred[2,2]{1,0:T(4,128)(4,1)} %get-tuple-element.2385) | copy-start | bytes 16 | tf_op jit(solution)/shard_map/while
  669.4 86.6 %copy-start.25 = (f32[2,16,2,64,64]{4,3,2,1,0:T(8,128)}, f32[2,16,2,64,64]{4,3,2,1,0:T(8,128)S(1)}, u32[]{:S(2)}) copy-start(f32[2,16,2,64,64]{4,3,2,1,0:T(8,128)S(1)} %bitcast_dynamic-update-slice_fusion.32) | copy-start | bytes 3145732 | tf_op jit(solution)/shard_map/while
  758.2 293.7 %reduce-scatter.19.cloned.1.call-start = ((), (), s32[]{:S(2)}) async-start(), calls=%async_computation.14 | async-start | bytes 4718592 | tf_op jit(solution)/shard_map/while
  905.9 2.2 copy-start.2
  906.8 2.8 copy-start.4
  908.6 3.1 copy-start.3
  915.7 2.2 copy-start.2
  916.6 2.8 copy-start.4
  918.4 3.1 copy-start.3
  964.3 2.1 copy-start.7
  964.3 2.1 copy-start.24
  964.3 91.9 %copy-start.39 = (pred[2,2]{1,0:T(4,128)(4,1)S(1)}, pred[2,2]{1,0:T(4,128)(4,1)}, u32[]{:S(2)}) copy-start(pred[2,2]{1,0:T(4,128)(4,1)} %get-tuple-element.2385) | copy-start | bytes 16 | tf_op jit(solution)/shard_map/while
  966.5 87.5 %copy-start.25 = (f32[2,16,2,64,64]{4,3,2,1,0:T(8,128)}, f32[2,16,2,64,64]{4,3,2,1,0:T(8,128)S(1)}, u32[]{:S(2)}) copy-start(f32[2,16,2,64,64]{4,3,2,1,0:T(8,128)S(1)} %bitcast_dynamic-update-slice_fusion.32) | copy-start | bytes 3145732 | tf_op jit(solution)/shard_map/while
  1056.6 144.4 %reduce-scatter.13.cloned.1.call-start = ((), (), s32[]{:S(2)}) async-start(), calls=%async_computation.11 | async-start | bytes 4325376 | tf_op jit(solution)/shard_map/reduce_scatter | solution.py:527
  1057.3 3.9 copy-start.23
  1057.4 3.9 copy-start.28
  1057.4 301.7 %reduce-scatter.11.cloned.1.call-start = ((), (), s32[]{:S(2)}) async-start(), calls=%async_computation.10 | async-start | bytes 12976128 | tf_op jit(solution)/shard_map/reduce_scatter | solution.py:526
  1067.6 476.4 %reduce-scatter.15.cloned.1.call-start = ((), (), s32[]{:S(2)}) async-start(), calls=%async_computation.12 | async-start | bytes 17301504 | tf_op jit(solution)/shard_map/reduce_scatter | solution.py:528
  1078.7 652.9 %reduce-scatter.17.cloned.1.call-start = ((), (), s32[]{:S(2)}) async-start(), calls=%async_computation.13 | async-start | bytes 17301504 | tf_op jit(solution)/shard_map/reduce_scatter | solution.py:529
  1078.7 5.6 copy-start.18
  1093.5 6.2 copy-start.46
  1093.5 6.2 copy-start.52
  1093.5 6.2 copy-start.53
  1093.5 51.1 %copy-start.11 = (f32[256,1024]{1,0:T(8,128)S(1)}, f32[256,1024]{1,0:T(8,128)}, u32[]{:S(2)}) copy-start(f32[256,1024]{1,0:T(8,128)} %copy-done.10) | copy-start | bytes 3145732
  1147.2 584.4 %copy-start.1 = (s32[2,16,16,3]{2,1,3,0:T(8,128)S(1)}, s32[2,16,16,3]{2,1,3,0:T(8,128)}, u32[]{:S(2)}) copy-start(s32[2,16,16,3]{2,1,3,0:T(8,128)} %param.34) | copy-start | bytes 18436
  (30 other events, 41.0 us)
Sparse Core Ops, SparseCore 0:
  10.9 72.4 all-gather.6
  89.6 123.9 all-gather.8
  216.4 54.6 all-gather.10
  273.8 76.4 all-gather.12
  353.0 76.1 all-gather.14
  667.3 86.5 reduce-scatter.18
  964.5 87.4 reduce-scatter.18
  1060.3 140.6 reduce-scatter.12
  1207.6 151.3 reduce-scatter.10
  1361.9 182.1 reduce-scatter.14
  1547.0 184.5 reduce-scatter.16
where the time goes:
time: 1750 us; the launch traced here: 1740 us
  waiting for transfers between devices  864 us (49%)
  local copies, waits for them, and re-layouts  377 us (22%)
  matrix products  262 us (15%)
  blocking collectives  123 us (7%)
  other arithmetic  83.9 us (5%)
    reduce_scatter x1, waiting for transfers between devices, local(): lax.psum_scatter(contract_grad, ('seq', 'doc'), scatter_dimension=0, tile...  188 us
    reduce_scatter x1, waiting for transfers between devices, local(): lax.psum_scatter(expand_grad, ('seq', 'doc'), scatter_dimension=0, tiled=...  185 us
    while x4, waiting for transfers between devices  170 us
    reduce_scatter x1, waiting for transfers between devices, local(): lax.psum_scatter(inward_grad, ('seq', 'doc'), scatter_dimension=0, tiled=...  158 us
    reshape x16, local copies, waits for them, and re-layouts, select_blocks(): rows.reshape(slot_size // block_size, block_size, head_count, head_dim)  90.5 us
    unnamed x2, blocking collectives  83.8 us
    all_gather x1, waiting for transfers between devices, local(): pair_full = lax.all_gather(pair_local, 'seq', axis=1, tiled=True)  73.5 us
    while x80, local copies, waits for them, and re-layouts  68.5 us
  transfers between devices with their start and end apart: 11, of which 9 were waited for; matrix products, arithmetic and copies ran while one was open for 15% of the time, Pallas kernels for 0%

commit v1 on v0

--- a/solution.py
+++ b/solution.py
@@ -1,6 +1,10 @@
+import types
+
 import jax
 import jax.numpy as jnp
 from jax import lax
+from jax.experimental import pallas as pl
+from jax.experimental.pallas import tpu as pltpu
 from jax.sharding import PartitionSpec as P
 
 group_heads = 4
@@ -539,39 +543,991 @@
     return (output, grad_inputs) + tuple(summed)
 
 
+ROUTE = pl.DeviceIdType.MESH
+NZ, NX, NY, NC = 4, 2, 2, 2
+bf16, f32 = jnp.bfloat16, jnp.float32
+
+
+def nn(left, right):
+    return lax.dot_general(left, right, (((1,), (0,)), ((), ())), preferred_element_type=f32)
+
+
+def nt(left, right):
+    return lax.dot_general(left, right, (((1,), (1,)), ((), ())), preferred_element_type=f32)
+
+
+def tn(left, right):
+    return lax.dot_general(left, right, (((0,), (0,)), ((), ())), preferred_element_type=f32)
+
+
+class Net:
+    def __init__(self, send_sems, recv_sems, here):
+        self.send_sems, self.recv_sems, self.here = send_sems, recv_sems, here
+        self.sent, self.taken = 0, 0
+        self.open = []
+
+    def slots(self, count):
+        first = self.taken
+        self.taken += count
+        assert self.taken <= RECVS
+        return first
+
+    def send(self, src, dst, device, slot, group=None):
+        index = self.sent
+        self.sent += 1
+        assert self.sent <= SENDS
+
+        def make():
+            return pltpu.make_async_remote_copy(
+                src_ref=src,
+                dst_ref=dst,
+                send_sem=self.send_sems.at[index],
+                recv_sem=self.recv_sems.at[slot],
+                device_id=device,
+                device_id_type=ROUTE,
+            )
+
+        make().start()
+        self.open.append((group, None, make))
+
+    def send_or_keep(self, src, dst, device, slot, is_self, group=None):
+        index = self.sent
+        self.sent += 1
+        assert self.sent <= SENDS
+
+        def make():
+            return pltpu.make_async_remote_copy(
+                src_ref=src,
+                dst_ref=dst,
+                send_sem=self.send_sems.at[index],
+                recv_sem=self.recv_sems.at[slot],
+                device_id=device,
+                device_id_type=ROUTE,
+            )
+
+        @pl.when(jnp.logical_not(is_self))
+        def away():
+            make().start()
+
+        @pl.when(is_self)
+        def keep():
+            pltpu.make_async_copy(src, dst, self.recv_sems.at[slot]).start()
+
+        self.open.append((group, is_self, make))
+
+    def settle(self, group=None, everything=False):
+        rest = []
+        for entry in self.open:
+            name, is_self, make = entry
+            if not everything and name != group:
+                rest.append(entry)
+            elif is_self is None:
+                make().wait_send()
+            else:
+                pl.when(jnp.logical_not(is_self))(lambda make=make: make().wait_send())
+        self.open = rest
+
+    def arrive(self, dst, slot):
+        pltpu.make_async_remote_copy(
+            src_ref=dst,
+            dst_ref=dst,
+            send_sem=self.send_sems.at[0],
+            recv_sem=self.recv_sems.at[slot],
+            device_id=self.here,
+            device_id_type=ROUTE,
+        ).wait_recv()
+
+
+def row_stats(values):
+    mean = jnp.mean(values, axis=-1, keepdims=True)
+    centered = values - mean
+    inverse = lax.rsqrt(jnp.mean(centered * centered, axis=-1, keepdims=True) + epsilon)
+    return centered * inverse, inverse
+
+
+def norm_pullback(grad, scaled, inverse, gain):
+    wide = grad * gain
+    first = jnp.mean(wide, axis=-1, keepdims=True)
+    second = jnp.mean(wide * scaled, axis=-1, keepdims=True)
+    return (wide - first - scaled * second) * inverse
+
+
+def column_sum(values):
+    return jnp.sum(values, axis=0, keepdims=True)
+
+
+SCRATCH = dict(
+    xr=((8, 2, 64, 1024), bf16),
+    n1=((8, 128, 1024), bf16),
+    aux=((64, 128), jnp.int32),
+    bias=((16, 4, 1024), f32),
+    sv=((4, 2, 2, 2, 8, 128), f32),
+    vec=((8, 1024), f32),
+    b1=((1, 2048), f32),
+    wqs=((4, 32, 768), bf16),
+    wq=((4, 2, 2, 2, 32, 768), bf16),
+    wo=((4, 2, 2, 2, 32, 1024), bf16),
+    w1s=((32, 2048), bf16),
+    w1=((4, 2, 2, 2, 32, 2048), bf16),
+    w2=((4, 2, 2, 128, 1024), bf16),
+    qkv=((1024, 768), bf16),
+    lse=((1024, 128), f32),
+    at=((8, 128, 256), bf16),
+    att=((2, 4, 128, 256), bf16),
+    mid=((256, 1024), f32),
+    nt2=((2, 256, 1024), bf16),
+    dyx=((2, 256, 1024), bf16),
+    act=((512, 2048), bf16),
+    gp=((512, 2048), bf16),
+    dw2=((4, 2, 2, 128, 1024), bf16),
+    xs=((256, 1024), f32),
+    xg=((256, 1024), f32),
+    own=((256, 1024), f32),
+    gb=((256, 1024), bf16),
+    gm=((256, 1024), f32),
+    da=((2, 4, 128, 256), bf16),
+    do=((8, 128, 256), bf16),
+    dk=((1024, 128), f32),
+    dv=((1024, 128), f32),
+    rgs=((8, 64, 1024), bf16),
+    rgx=((4, 64, 1024), bf16),
+    gnr=((2, 2, 64, 1024), bf16),
+    r1y=((4, 2, 2, 32, 2048), bf16),
+    r1x=((4, 2, 32, 2048), bf16),
+    r1z=((4, 2, 32, 2048), bf16),
+    f1=((2, 32, 2048), f32),
+    r1f=((32, 2048), f32),
+    r2y=((4, 2, 128, 1024), bf16),
+    r2x=((4, 128, 1024), bf16),
+    r2z=((4, 128, 1024), bf16),
+    ros=((4, 2, 2, 32, 1024), bf16),
+    roy=((4, 2, 32, 1024), bf16),
+    rox=((4, 32, 1024), bf16),
+    roz=((4, 32, 1024), bf16),
+    rqy=((4, 2, 2, 32, 768), bf16),
+    rqz=((4, 2, 2, 32, 768), bf16),
+    fq=((2, 2, 32, 768), f32),
+    rqf=((4, 32, 768), f32),
+    sg=((8, 8, 128), f32),
+    rsg=((8, 8, 128), f32),
+    sgt=((2, 8, 128), f32),
+    rsy=((2, 8, 128), f32),
+)
+SENDS, RECVS = 256, 256
+VMEM_BYTES = 64 * 2**20
+
+
+def layer_kernel(
+    x_in, dy_in, aux_in, wq_in, wo_in, w1_in, w2_in, sv_in,
+    out_ref, gx_ref, dwq_ref, dwo_ref, dw1_ref, dw2_ref, sg_ref,
+    *rest,
+):
+    names = list(SCRATCH)
+    R = types.SimpleNamespace(**dict(zip(names, rest[: len(names)])))
+    send_sems, recv_sems, ready_sem = rest[len(names):]
+    s, d = lax.axis_index("seq"), lax.axis_index("doc")
+    z, x, y, c = s // NX, s % NX, d // NC, d % NC
+    hd = 2 * x + c
+    flip = 1 - c
+
+    def at(zz, xx, yy, cc):
+        return (zz * NX + xx, yy * NC + cc)
+
+    here = (s, d)
+    sib, xn, yn = at(z, x, y, flip), at(z, 1 - x, y, c), at(z, x, 1 - y, c)
+    net = Net(send_sems, recv_sems, here)
+    turn = [(z + k) % NZ for k in range(NZ)]
+
+    barrier = pltpu.get_barrier_semaphore()
+
+    def greet(step, _):
+        other = (s * NC + c + step) % 16
+        pl.semaphore_signal(
+            barrier, inc=1, device_id=(other // NC, y * NC + other % NC), device_id_type=ROUTE
+        )
+        return 0
+
+    lax.fori_loop(1, 16, greet, 0)
+    pl.semaphore_signal(barrier, inc=1, device_id=yn, device_id_type=ROUTE)
+    pl.semaphore_wait(barrier, 16)
+
+    half = pl.ds(pl.multiple_of(c * 512, 512), 512)
+    other_half = pl.ds(pl.multiple_of(flip * 512, 512), 512)
+    xz = net.slots(4)
+    for b in range(2):
+        for ch in range(2):
+            zt = 2 * c + b
+            net.send_or_keep(
+                x_in.at[b, :, :, ch * 512:(ch + 1) * 512],
+                R.xr.at[s, :, :, ch * 512:(ch + 1) * 512],
+                at(zt, x, y, ch),
+                xz + z,
+                jnp.logical_and(zt == z, c == ch),
+            )
+
+    sv_s = net.slots(1)
+    R.sv[z, x, y, c] = sv_in[...]
+    net.send(R.sv.at[z, x, y, c], R.sv.at[z, x, y, c], sib, sv_s)
+
+    for h in range(4):
+        for t in range(3):
+            R.wqs[h, :, t * 256:(t + 1) * 256] = wq_in[
+                :, t * 1024 + h * 256:t * 1024 + (h + 1) * 256
+            ]
+    R.wq[z, x, y, c] = R.wqs[hd]
+    wqa = net.slots(4)
+    for xx, cc, dev in ((x, flip, sib), (1 - x, c, xn), (1 - x, flip, at(z, 1 - x, y, flip))):
+        net.send(R.wqs.at[2 * xx + cc], R.wq.at[z, x, y, c], dev, wqa + hd)
+
+    aux_s = net.slots(1)
+    has_table = c == z // 2
+
+    @pl.when(has_table)
+    def table():
+        R.aux[...] = aux_in[z % 2, hd]
+
+    def table_copy():
+        return pltpu.make_async_remote_copy(
+            src_ref=aux_in.at[z % 2, 2 * x + flip],
+            dst_ref=R.aux,
+            send_sem=send_sems.at[SENDS - 1],
+            recv_sem=recv_sems.at[aux_s],
+            device_id=sib,
+            device_id_type=ROUTE,
+        )
+
+    @pl.when(has_table)
+    def table_away():
+        table_copy().start()
+
+    w1_sib = net.slots(1)
+
+    def parity(ref_value, which):
+        return jnp.concatenate(
+            [ref_value[:, (2 * k + which) * 128:(2 * k + which + 1) * 128] for k in range(16)],
+            axis=1,
+        )
+
+    w1_all = w1_in[...]
+    even, odd = parity(w1_all, 0), parity(w1_all, 1)
+    R.w1[z, x, y, c] = jnp.where(c == 0, even, odd)
+    R.w1s[...] = jnp.where(c == 0, odd, even)
+    net.send(R.w1s, R.w1.at[z, x, y, c], sib, w1_sib)
+    R.wo[z, x, y, c] = wo_in[...]
+    R.w2[z, x, y] = w2_in[...]
+    dy_s = net.slots(1)
+    R.dyx[c] = dy_in[...].reshape(256, 1024)
+    net.send(R.dyx.at[c], R.dyx.at[c], sib, dy_s)
+
+    for xx, cc, dev in ((x, flip, sib), (1 - x, c, xn), (1 - x, flip, at(z, 1 - x, y, flip))):
+        net.arrive(R.wq.at[z, xx, y, cc], wqa + 2 * xx + cc)
+    wqz = net.slots(4)
+    for zt in turn[1:]:
+        net.send(R.wq.at[z, :, y], R.wq.at[z, :, y], at(zt, x, y, c), wqz + z, "w")
+    wqy = net.slots(4)
+    net.send(R.wq.at[z, :, y], R.wq.at[z, :, y], yn, wqy + z, "w")
+
+    net.arrive(R.sv.at[z, x, y, flip], sv_s)
+    sv_z, sv_x, sv_y = net.slots(4), net.slots(1), net.slots(1)
+    for zt in turn[1:]:
+        net.send(R.sv.at[z, x, y], R.sv.at[z, x, y], at(zt, x, y, c), sv_z + z)
+
+    xx_r, xs_r = net.slots(4), net.slots(8)
+    for zt in turn:
+        net.arrive(R.xr.at[zt * 2 + x, :, :, half], xz + zt)
+        part = R.xr.at[zt * 2 + x, :, :, half]
+        net.send(part, part, xn, xx_r + zt, "xr")
+        net.send(part, part, sib, xs_r + zt * 2 + x, "xr")
+    for zt in turn[1:]:
+        net.arrive(R.sv.at[zt, x, y], sv_z + zt)
+    net.send(R.sv.at[:, x, y], R.sv.at[:, x, y], xn, sv_x)
+    for zt in turn[1:]:
+        part = R.wq.at[zt, :, y]
+        net.arrive(part, wqz + zt)
+        net.send(part, part, yn, wqy + zt, "w")
+
+    def gather_start(ref, piece, group):
+        base_z, base_a, base_b = net.slots(4), net.slots(4), net.slots(8)
+        own = piece(z, x, y)
+        for zt in turn[1:]:
+            net.send(own, own, at(zt, x, y, c), base_z + z, group)
+        return base_z, base_a, base_b
+
+    def piece_of(ref):
+        return lambda zz, xx, yy: ref.at[zz, xx, yy]
+
+    wo_piece = lambda zz, xx, yy: R.wo.at[zz, xx, yy, c]
+    w1_piece, w2_piece = piece_of(R.w1), piece_of(R.w2)
+    net.arrive(R.w1.at[z, x, y, flip], w1_sib)
+    wo_sl = gather_start(R.wo, wo_piece, "w")
+    w1_sl = gather_start(R.w1, w1_piece, "w")
+    w2_sl = gather_start(R.w2, w2_piece, "w")
+
+    def spread(piece, slots, group, x_first):
+        base_z, base_a, base_b = slots
+        first, second = (xn, yn) if x_first else (yn, xn)
+
+        def from_first(zz):
+            return piece(zz, 1 - x, y) if x_first else piece(zz, x, 1 - y)
+
+        def step_column(k):
+            zt = turn[k]
+            part = piece(zt, x, y)
+            if k:
+                net.arrive(part, base_z + zt)
+            net.send(part, part, first, base_a + zt, group)
+            net.send(part, part, second, base_b + 2 * zt, group)
+
+        def step_first(k):
+            zt = turn[k]
+            part = from_first(zt)
+            net.arrive(part, base_a + zt)
+            net.send(part, part, second, base_b + 2 * zt + 1, group)
+
+        def step_last():
+            for zt in turn:
+                if x_first:
+                    net.arrive(piece(zt, x, 1 - y), base_b + 2 * zt)
+                    net.arrive(piece(zt, 1 - x, 1 - y), base_b + 2 * zt + 1)
+                else:
+                    net.arrive(piece(zt, 1 - x, y), base_b + 2 * zt)
+                    net.arrive(piece(zt, 1 - x, 1 - y), base_b + 2 * zt + 1)
+
+        steps = [lambda k=k: step_column(k) for k in range(4)] + [lambda k=k: step_first(k) for k in range(4)]
+        return steps, step_last
+
+    wo_steps, wo_last = spread(wo_piece, wo_sl, "w", True)
+    w1_steps, w1_last = spread(w1_piece, w1_sl, "w", True)
+    w2_steps, w2_last = spread(w2_piece, w2_sl, "w", False)
+
+    net.arrive(R.sv.at[:, 1 - x, y], sv_x)
+    net.send(R.sv.at[:, :, y], R.sv.at[:, :, y], yn, sv_y)
+    for zt in turn:
+        part = R.xr.at[zt * 2 + (1 - x), :, :, half]
+        net.arrive(part, xx_r + zt)
+        net.send(part, part, sib, xs_r + zt * 2 + 1 - x, "xr")
+
+    @pl.when(has_table)
+    def table_sent():
+        table_copy().wait_send()
+
+    @pl.when(jnp.logical_not(has_table))
+    def table_here():
+        net.arrive(R.aux, aux_s)
+
+    for g in range(16):
+        tiles = R.aux[g * 4:(g + 1) * 4, :]
+        place = lax.broadcasted_iota(jnp.int32, (4, 1024), 1)
+        block = place >> 6
+        row = lax.broadcasted_iota(jnp.int32, (4, 1024), 0) + (g % 4) * 4
+        extent = tiles[:, 3:4]
+        last = (extent - 1) >> 6
+        seen = jnp.abs(row - block) <= 1
+        for k in range(3):
+            seen = seen | (block == tiles[:, k:k + 1])
+        seen = seen | (block == 0) | (block == last) | (row == 0) | (row == last)
+        seen = seen & (place < extent)
+        R.bias[g] = jnp.where(seen, 0.0, negative).astype(f32)
+
+    net.arrive(R.sv.at[:, :, 1 - y], sv_y)
+    lane = lax.broadcasted_iota(jnp.int32, (1, 128), 1) >> 5
+    for r in range(8):
+        for k in range(5):
+            total = jnp.zeros((1, 128), f32)
+            for q in range(4):
+                line = R.sv[r // 2, r % 2, q // 2, q % 2, k // 4:k // 4 + 1, :]
+                shift = (32 * (q - k % 4)) % 128
+                if shift:
+                    line = pltpu.roll(line, shift, 1)
+                total = jnp.where(lane == q, line, total)
+            R.vec[k:k + 1, r * 128:(r + 1) * 128] = total
+    for p in range(16):
+        R.b1[:, p * 128:(p + 1) * 128] = R.sv[p // 4, p // 2 % 2, p % 2, c, 2:3, :]
+
+    for k in range(8):
+        net.arrive(R.xr.at[k, :, :, other_half], xs_r + k)
+    for zt in turn:
+        part = R.wq.at[zt, :, 1 - y]
+        net.arrive(part, wqy + zt)
+
+    def project(step, _):
+        for k in range(2):
+            scaled, _inverse = row_stats(R.xr[2 * step + k].reshape(128, 1024).astype(f32))
+            R.n1[2 * step + k] = (scaled * R.vec[0:1, :] + R.vec[1:2, :]).astype(bf16)
+        rows = R.n1[pl.ds(2 * step, 2)].reshape(256, 1024)
+        made = nn(rows, R.wq[...].reshape(1024, 768)).astype(bf16)
+        where = pl.ds(pl.multiple_of(step * 256, 256), 256)
+        R.qkv[where, :] = jnp.concatenate([made[:, :256] * jnp.asarray(0.125, bf16), made[:, 256:]], axis=1)
+        return 0
+
+    lax.fori_loop(0, 4, project, 0)
+
+    low_lane = lax.broadcasted_iota(jnp.int32, (1, 128), 1) < 64
+
+    def only(values, e):
+        return jnp.where(low_lane if e == 0 else jnp.logical_not(low_lane), values, jnp.zeros_like(values))
+
+    def attend(pair):
+        cols = slice(pair * 128, pair * 128 + 128)
+        kcols = slice(256 + pair * 128, 256 + pair * 128 + 128)
+        vcols = slice(512 + pair * 128, 512 + pair * 128 + 128)
+
+        def tile(t, _):
+            where = pl.ds(pl.multiple_of(t * 256, 256), 256)
+            q = R.qkv[where, cols]
+            mixed = None
+            for e in range(2):
+                h = pair * 2 + e
+                scores = nt(only(q, e), R.qkv[:, kcols])
+                scores = (scores.reshape(4, 64, 1024) + R.bias[h * 4 + t][:, None, :]).reshape(256, 1024)
+                top = jnp.max(scores, axis=-1, keepdims=True)
+                grown = jnp.exp(scores - top)
+                total = jnp.sum(grown, axis=-1, keepdims=True)
+                low = (grown * (1.0 / total)).astype(bf16)
+                R.lse[where, h:h + 1] = top + jnp.log(total)
+                got = nn(low, R.qkv[:, vcols])
+                mixed = got if e == 0 else jnp.where(low_lane, mixed, got)
+            R.at[pl.ds(2 * t, 2), :, cols] = mixed.astype(bf16).reshape(2, 128, 128)
+            return 0
+
+        lax.fori_loop(0, 4, tile, 0)
+
+    for k in range(4):
+        wo_steps[k]()
+    for k in range(4):
+        w1_steps[k]()
+    attend(0)
+    for k in range(4):
+        wo_steps[4 + k]()
+    for k in range(4):
+        w1_steps[4 + k]()
+    for k in range(4):
+        w2_steps[k]()
+    attend(1)
+
+    at_r = net.slots(8)
+    back_c = z // 2
+    for k in range(4):
+        for xx in (x, 1 - x):
+            zt = turn[k]
+            net.send_or_keep(
+                R.at.at[zt * 2 + xx],
+                R.att.at[z % 2, hd],
+                at(zt, xx, y, back_c),
+                at_r + (z % 2) * 4 + hd,
+                jnp.logical_and(jnp.logical_and(zt == z, xx == x), c == back_c),
+            )
+    for k in range(4):
+        w2_steps[4 + k]()
+    wo_last()
+    wo_s = net.slots(1)
+    net.send(R.wo.at[:, :, :, c], R.wo.at[:, :, :, c], sib, wo_s, "w")
+    net.arrive(R.wo.at[:, :, :, flip], wo_s)
+    for b in range(2):
+        for h in range(4):
+            net.arrive(R.att.at[b, h], at_r + b * 4 + h)
+
+    for n in range(4):
+        cols = slice(n * 256, n * 256 + 256)
+        made = x_in[:, :, :, cols].reshape(256, 256).astype(f32)
+        for h in range(4):
+            made = made + nn(
+                R.att[:, h].reshape(256, 256),
+                R.wo[h, :, :, :, :, cols].reshape(256, 256),
+            )
+        R.mid[:, cols] = made
+    for k in range(2):
+        where = slice(k * 128, k * 128 + 128)
+        scaled, _inverse = row_stats(R.mid[where, :])
+        R.nt2[c, where, :] = (scaled * R.vec[2:3, :] + R.vec[3:4, :]).astype(bf16)
+    nt_s = net.slots(1)
+    net.send(R.nt2.at[c], R.nt2.at[c], sib, nt_s)
+    net.arrive(R.dyx.at[flip], dy_s)
+
+    w1_last()
+    net.arrive(R.nt2.at[flip], nt_s)
+
+    def widen(j, _):
+        where = pl.ds(pl.multiple_of(j * 256, 256), 256)
+        for k in range(2):
+            rows = slice(k * 256, k * 256 + 256)
+            pre = nn(R.nt2[k], R.w1[:, :, :, :, :, where].reshape(1024, 256))
+            pre = pre + R.b1[:, where]
+            share = 0.5 * (1.0 + lax.erf(pre * (2.0 ** -0.5)))
+            R.act[rows, where] = (pre * share).astype(bf16)
+            slope = share + pre * (jnp.exp(-0.5 * pre * pre) * (1.0 / (2.0 * jnp.pi) ** 0.5))
+            R.gp[rows, where] = slope.astype(bf16)
+        return 0
+
+    lax.fori_loop(0, 8, widen, 0)
+
+    def outer_two(j, _):
+        where = pl.ds(pl.multiple_of(j * 256, 256), 256)
+        made = tn(R.act[:, where], R.dyx[...].reshape(512, 1024))
+        p = 2 * j
+        R.dw2[p // 4, p // 2 % 2, 0] = made[:128].astype(bf16)
+        R.dw2[p // 4, p // 2 % 2, 1] = made[128:].astype(bf16)
+        return 0
+
+    lax.fori_loop(0, 8, outer_two, 0)
+
+    def scatter_steps(piece, ra, rb, rz, slots, x_first):
+        base_a, base_b, base_z = slots
+        first, second = (xn, yn) if x_first else (yn, xn)
+
+        def spot(zz, near, far):
+            xx, yy = (near, far) if x_first else (far, near)
+            return piece(zz, jnp.where(xx, x, 1 - x), jnp.where(yy, y, 1 - y))
+
+        def begin():
+            for far in (0, 1):
+                for k in (1, 2, 3, 0):
+                    zt = turn[k]
+                    net.send(spot(zt, 0, far), ra.at[zt, far], first, base_a + 2 * zt + far)
+
+        def middle(k):
+            zt = turn[k]
+            net.arrive(ra.at[zt, 0], base_a + 2 * zt)
+            here_ = spot(zt, 1, 0)
+            here_[...] = (here_[...].astype(f32) + ra[zt, 0].astype(f32)).astype(bf16)
+            net.send(here_, rb.at[zt], second, base_b + zt)
+
+        def late(k):
+            zt = turn[k]
+            net.arrive(ra.at[zt, 1], base_a + 2 * zt + 1)
+            net.arrive(rb.at[zt], base_b + zt)
+            here_ = spot(zt, 1, 1)
+            here_[...] = (
+                here_[...].astype(f32) + ra[zt, 1].astype(f32) + rb[zt].astype(f32)
+            ).astype(bf16)
+            if k:
+                net.send(here_, rz.at[z], at(zt, x, y, c), base_z + z)
+
+        def final():
+            total = spot(z, 1, 1)[...].astype(f32)
+            for zt in turn[1:]:
+                net.arrive(rz.at[zt], base_z + zt)
+                total = total + rz[zt].astype(f32)
+            return total
+
+        return begin, middle, late, final
+
+    def scatter_slots():
+        return net.slots(8), net.slots(4), net.slots(4)
+
+    two_begin, two_middle, two_late, two_final = scatter_steps(
+        lambda zz, xx, yy: R.dw2.at[zz, xx, yy], R.r2y, R.r2x, R.r2z, scatter_slots(), True
+    )
+    two_begin()
+
+    w2_last()
+
+    def narrow_back(j, _):
+        where = pl.ds(pl.multiple_of(j * 256, 256), 256)
+        p = 2 * j
+        rows2 = R.w2[p // 4, p // 2 % 2].reshape(256, 1024)
+        made = nt(R.dyx[...].reshape(512, 1024), rows2) * R.gp[:, where].astype(f32)
+        R.gp[:, where] = made.astype(bf16)
+        return 0
+
+    lax.fori_loop(0, 8, narrow_back, 0)
+
+    gn_s = net.slots(1)
+
+    def partial_norm(n, which):
+        rows = pl.ds(pl.multiple_of(which * 256, 256), 256)
+        return nt(R.gp[rows, :], R.w1[n].reshape(256, 2048))
+
+    for n in range(4):
+        R.xs[:, n * 256:(n + 1) * 256] = partial_norm(n, flip)
+    net.send(R.xs, R.xg, sib, gn_s, "xs")
+    for n in range(4):
+        R.own[:, n * 256:(n + 1) * 256] = partial_norm(n, c)
+    net.arrive(R.xg, gn_s)
+    sums = [jnp.zeros((1, 1024), f32) for _ in range(3)]
+    for k in range(4):
+        where = slice(k * 64, k * 64 + 64)
+        grad = R.own[where, :] + R.xg[where, :]
+        scaled, inverse = row_stats(R.mid[where, :])
+        flow = dy_in[k // 2, (k % 2) * 64:(k % 2) * 64 + 64, :].astype(f32)
+        sums[0] = sums[0] + column_sum(grad * scaled)
+        sums[1] = sums[1] + column_sum(grad)
+        sums[2] = sums[2] + column_sum(flow)
+        total = flow + norm_pullback(grad, scaled, inverse, R.vec[2:3, :])
+        R.gm[where, :] = total
+        R.gb[where, :] = total.astype(bf16)
+
+    def note(row, line):
+        for r in range(8):
+            R.sg[r, row:row + 1, :] = line[:, r * 128:(r + 1) * 128]
+
+    R.sg[...] = jnp.zeros((8, 8, 128), f32)
+    for k in range(3):
+        note(2 + k, sums[k])
+
+    do_r = net.slots(8)
+    for h in range(4):
+        made = nt(R.gb[...], R.wo[h].reshape(256, 1024)).astype(bf16)
+        R.da[:, h] = made.reshape(2, 128, 256)
+    for b in range(2):
+        for xx in (x, 1 - x):
+            for cc in (c, flip):
+                zt = 2 * c + b
+                net.send_or_keep(
+                    R.da.at[b, 2 * xx + cc],
+                    R.do.at[s],
+                    at(zt, xx, y, cc),
+                    do_r + s,
+                    jnp.logical_and(zt == z, jnp.logical_and(xx == x, cc == c)),
+                )
+
+    net.settle("w")
+
+    def outer_one(n, _):
+        for m in range(2):
+            cols = slice(m * 1024, m * 1024 + 1024)
+            left = R.nt2[:, :, pl.ds(pl.multiple_of(n * 256, 256), 256)].reshape(512, 256)
+            made = tn(left, R.gp[:, cols]).astype(bf16)
+            R.w1[n, :, :, :, :, cols] = made.reshape(2, 2, 2, 32, 1024)
+        return 0
+
+    lax.fori_loop(0, 4, outer_one, 0)
+    one_begin, one_middle, one_late, one_final = scatter_steps(
+        w1_piece, R.r1y, R.r1x, R.r1z, scatter_slots(), False
+    )
+    one_begin()
+    for h in range(4):
+        made = tn(R.att[:, h].reshape(256, 256), R.gb[...]).astype(bf16)
+        R.wo[h] = made.reshape(2, 2, 2, 32, 1024)
+    ros_s = net.slots(1)
+    net.send(R.wo.at[:, :, :, flip], R.ros, sib, ros_s)
+    for k in range(4):
+        two_middle(k)
+
+    out_s = net.slots(1)
+    net.settle("xs")
+
+    def contracted(n, which):
+        cols = slice(n * 256, n * 256 + 256)
+        rows = pl.ds(pl.multiple_of(which * 256, 256), 256)
+        return nn(R.act[rows, :], R.w2[:, :, :, :, cols].reshape(2048, 256))
+
+    for n in range(4):
+        R.xs[:, n * 256:(n + 1) * 256] = contracted(n, flip)
+    pl.semaphore_signal(ready_sem, inc=1, device_id=sib, device_id_type=ROUTE)
+    pl.semaphore_wait(ready_sem, 1)
+    net.send(R.xs, R.xg, sib, out_s)
+    for n in range(4):
+        cols = slice(n * 256, n * 256 + 256)
+        R.own[:, cols] = R.mid[:, cols] + contracted(n, c) + R.vec[4:5, cols]
+    up = [jnp.zeros((1, 2048), f32)]
+    for k in range(8):
+        up[0] = up[0] + column_sum(R.gp[k * 64:(k + 1) * 64, :].astype(f32))
+    for p in range(16):
+        R.sg[p // 2, 5 + p % 2:6 + p % 2, :] = up[0][:, p * 128:(p + 1) * 128]
+    net.arrive(R.xg, out_s)
+    for k in range(2):
+        where = slice(k * 128, k * 128 + 128)
+        out_ref[k] = (R.own[where, :] + R.xg[where, :]).astype(bf16)
+    net.arrive(R.ros, ros_s)
+    for k in range(4):
+        R.wo[k, :, :, c] = (R.wo[k, :, :, c].astype(f32) + R.ros[k].astype(f32)).astype(bf16)
+    o_begin, o_middle, o_late, o_final = scatter_steps(
+        wo_piece, R.roy, R.rox, R.roz, scatter_slots(), False
+    )
+    o_begin()
+
+    for k in range(8):
+        net.arrive(R.do.at[k], do_r + k)
+    for k in range(4):
+        one_middle(k)
+
+    def attend_back(pair):
+        cols = slice(pair * 128, pair * 128 + 128)
+        kcols = slice(256 + pair * 128, 256 + pair * 128 + 128)
+        vcols = slice(512 + pair * 128, 512 + pair * 128 + 128)
+        R.dk[...] = jnp.zeros((1024, 128), f32)
+        R.dv[...] = jnp.zeros((1024, 128), f32)
+
+        def tile(t, _):
+            where = pl.ds(pl.multiple_of(t * 256, 256), 256)
+            two = pl.ds(2 * t, 2)
+            q = R.qkv[where, cols]
+            grad = R.do[two, :, cols].reshape(256, 128)
+            prod = grad.astype(f32) * R.at[two, :, cols].reshape(256, 128).astype(f32)
+            query = None
+            for e in range(2):
+                h = pair * 2 + e
+                qe, ge = only(q, e), only(grad, e)
+                scores = nt(qe, R.qkv[:, kcols])
+                scores = (scores.reshape(4, 64, 1024) + R.bias[h * 4 + t][:, None, :]).reshape(256, 1024)
+                chances = jnp.exp(scores - R.lse[where, h:h + 1])
+                central = jnp.sum(only(prod, e), axis=-1, keepdims=True)
+                moved = nt(ge, R.qkv[:, vcols])
+                back = (chances * (moved - central)).astype(bf16)
+                R.dv[...] += tn(chances.astype(bf16), ge)
+                R.dk[...] += tn(back, qe)
+                got = nn(back, R.qkv[:, kcols])
+                query = got if e == 0 else jnp.where(low_lane, query, got)
+            R.qkv[where, cols] = (query * 0.125).astype(bf16)
+            return 0
+
+        lax.fori_loop(0, 4, tile, 0)
+        R.qkv[:, kcols] = R.dk[...].astype(bf16)
+        R.qkv[:, vcols] = R.dv[...].astype(bf16)
+
+    attend_back(0)
+    for k in range(4):
+        two_late(k)
+    for k in range(4):
+        o_middle(k)
+    attend_back(1)
+    for k in range(4):
+        one_late(k)
+    for k in range(4):
+        o_late(k)
+
+    net.settle("xr")
+
+    def unproject(step, _):
+        where = pl.ds(pl.multiple_of(step * 256, 256), 256)
+        made = nt(R.qkv[where, :], R.wq[...].reshape(1024, 768)).astype(bf16)
+        R.xr[pl.ds(2 * step, 2)] = made.reshape(2, 2, 64, 1024)
+        return 0
+
+    lax.fori_loop(0, 4, unproject, 0)
+    rgs_s, rgx_s, gnr_s = net.slots(1), net.slots(4), net.slots(4)
+    net.send(R.xr.at[:, flip], R.rgs, sib, rgs_s)
+
+    def outer_in(n, _):
+        cols = pl.ds(pl.multiple_of(n * 256, 256), 256)
+        made = tn(R.n1[:, :, cols].reshape(1024, 256), R.qkv[...]).astype(bf16)
+        R.wq[n] = made.reshape(2, 2, 2, 32, 768)
+        return 0
+
+    lax.fori_loop(0, 4, outer_in, 0)
+    rqy_s, rqz_s, rqf_s = net.slots(4), net.slots(4), net.slots(4)
+    for k in (1, 2, 3, 0):
+        zt = turn[k]
+        net.send(R.wq.at[zt, :, 1 - y], R.rqy.at[zt], yn, rqy_s + zt)
+    net.arrive(R.rgs, rgs_s)
+    for k in range(4):
+        zt = turn[k]
+        i = zt * 2 + 1 - x
+        R.xr[i, c] = (R.xr[i, c].astype(f32) + R.rgs[i].astype(f32)).astype(bf16)
+        net.send(R.xr.at[i, c], R.rgx.at[zt], xn, rgx_s + zt)
+    for k in (1, 2, 3, 0):
+        zt = turn[k]
+        i = zt * 2 + x
+        net.arrive(R.rgx.at[zt], rgx_s + zt)
+        R.xr[i, c] = (
+            R.xr[i, c].astype(f32) + R.rgs[i].astype(f32) + R.rgx[zt].astype(f32)
+        ).astype(bf16)
+        net.send_or_keep(
+            R.xr.at[i, c],
+            R.gnr.at[z % 2, c],
+            at(zt, x, y, back_c),
+            gnr_s + 2 * (z % 2) + c,
+            jnp.logical_and(zt == z, c == back_c),
+        )
+    for k in (1, 2, 3, 0):
+        zt = turn[k]
+        net.arrive(R.rqy.at[zt], rqy_s + zt)
+        R.wq[zt, :, y] = (R.wq[zt, :, y].astype(f32) + R.rqy[zt].astype(f32)).astype(bf16)
+        if k:
+            net.send(R.wq.at[zt, :, y], R.rqz.at[z], at(zt, x, y, c), rqz_s + z)
+
+    dw2_ref[...] = two_final()
+    dwo_ref[...] = o_final()
+
+    for b in range(2):
+        for cc in range(2):
+            net.arrive(R.gnr.at[b, cc], gnr_s + 2 * b + cc)
+    sums = [jnp.zeros((1, 1024), f32) for _ in range(2)]
+    for k in range(4):
+        rows = slice((k % 2) * 64, (k % 2) * 64 + 64)
+        grad = R.gnr[k // 2, k % 2].astype(f32)
+        scaled, inverse = row_stats(x_in[k // 2, k % 2].astype(f32))
+        sums[0] = sums[0] + column_sum(grad * scaled)
+        sums[1] = sums[1] + column_sum(grad)
+        gx_ref[k // 2, rows, :] = R.gm[k * 64:(k + 1) * 64, :] + norm_pullback(
+            grad, scaled, inverse, R.vec[0:1, :]
+        )
+    for k in range(2):
+        note(k, sums[k])
+    sg_r = net.slots(8)
+    for k in range(4):
+        for xx in (x, 1 - x):
+            if k == 0 and xx is x:
+                continue
+            zt = turn[k]
+            net.send(R.sg.at[zt * 2 + xx], R.rsg.at[s], at(zt, xx, y, c), sg_r + s)
+
+    made = one_final()
+    R.f1[...] = made
+    r1f_s = net.slots(1)
+    net.send(R.f1.at[flip], R.r1f, sib, r1f_s)
+
+    total = R.wq[z, :, y].astype(f32)
+    for zt in turn[1:]:
+        net.arrive(R.rqz.at[zt], rqz_s + zt)
+        total = total + R.rqz[zt].astype(f32)
+    R.fq[...] = total
+    R.rqf[hd] = R.fq[x, c]
+    for xx, cc, dev in ((x, flip, sib), (1 - x, c, xn), (1 - x, flip, at(z, 1 - x, y, flip))):
+        net.send(R.fq.at[xx, cc], R.rqf.at[hd], dev, rqf_s + hd)
+
+    total = R.sg[s]
+    for k in range(4):
+        for xx in (x, 1 - x):
+            if k == 0 and xx is x:
+                continue
+            i = turn[k] * 2 + xx
+            net.arrive(R.rsg.at[i], sg_r + i)
+            total = total + R.rsg[i]
+    R.sgt[0] = total
+    sy, ss = net.slots(1), net.slots(1)
+    net.send(R.sgt.at[0], R.rsy.at[0], yn, sy)
+    net.arrive(R.rsy.at[0], sy)
+    total = total + R.rsy[0]
+    R.sgt[1] = total
+    net.send(R.sgt.at[1], R.rsy.at[1], sib, ss)
+
+    net.arrive(R.r1f, r1f_s)
+    mine, theirs = R.f1[c], R.r1f[...]
+    first = jnp.where(c == 0, mine, theirs)
+    second = jnp.where(c == 0, theirs, mine)
+    for k in range(16):
+        dw1_ref[:, 2 * k * 128:(2 * k + 1) * 128] = first[:, k * 128:(k + 1) * 128]
+        dw1_ref[:, (2 * k + 1) * 128:(2 * k + 2) * 128] = second[:, k * 128:(k + 1) * 128]
+    for xx, cc in ((x, flip), (1 - x, c), (1 - x, flip)):
+        net.arrive(R.rqf.at[2 * xx + cc], rqf_s + 2 * xx + cc)
+    for h in range(4):
+        for t in range(3):
+            dwq_ref[:, t * 1024 + h * 256:t * 1024 + (h + 1) * 256] = R.rqf[
+                h, :, t * 256:(t + 1) * 256
+            ]
+    net.arrive(R.rsy.at[1], ss)
+    row = lax.broadcasted_iota(jnp.int32, (8, 128), 0)
+    sg_ref[...] = total + jnp.where(row < 5, R.rsy[1], 0.0)
+    net.settle(everything=True)
+
+
+def local_fused(
+    arriving_features,
+    valid_extents,
+    sampled_target_tiles,
+    query_context_mapping,
+    attention_outflow_weights,
+    expansion_weights,
+    contraction_weights,
+    opening_scale_vector,
+    opening_shift_vector,
+    closing_scale_vector,
+    closing_shift_vector,
+    expansion_shift,
+    contraction_shift,
+    output_sensitivity,
+):
+    docs, heads, blocks, count = sampled_target_tiles.shape
+    tiles = sampled_target_tiles.reshape(docs, heads * blocks, count)
+    extents = jnp.broadcast_to(valid_extents[:, None, None], (docs, heads * blocks, 1))
+    aux = jnp.concatenate([tiles, extents], axis=2)
+    aux = jnp.pad(aux, ((0, 0), (0, 0), (0, 124))).reshape(docs, 4, 64, 128)
+    line_one = jnp.concatenate(
+        [opening_scale_vector, opening_shift_vector, closing_scale_vector, closing_shift_vector]
+    )
+    line_two = jnp.pad(contraction_shift, (0, 96))
+    small = jnp.pad(jnp.stack([line_one, line_two, expansion_shift]), ((0, 5), (0, 0))).astype(f32)
+    shapes = (
+        (arriving_features.shape, bf16),
+        (arriving_features.shape, f32),
+        (query_context_mapping.shape, f32),
+        (attention_outflow_weights.shape, f32),
+        (expansion_weights.shape, f32),
+        (contraction_weights.shape, f32),
+        ((8, 128), f32),
+    )
+    whole = pl.BlockSpec(memory_space=pltpu.VMEM)
+    made = pl.pallas_call(
+        layer_kernel,
+        name="layer",
+        out_shape=[jax.ShapeDtypeStruct(a, b) for a, b in shapes],
+        in_specs=[whole] * 8,
+        out_specs=[whole] * 7,
+        scratch_shapes=[pltpu.VMEM(a, b) for a, b in SCRATCH.values()]
+        + [
+            pltpu.SemaphoreType.DMA((SENDS,)),
+            pltpu.SemaphoreType.DMA((RECVS,)),
+            pltpu.SemaphoreType.REGULAR,
+        ],
+        compiler_params=pltpu.CompilerParams(
+            collective_id=0, has_side_effects=True, vmem_limit_bytes=VMEM_BYTES
+        ),
+    )(
+        arriving_features.reshape(2, 2, 64, 1024),
+        output_sensitivity,
+        aux,
+        query_context_mapping,
+        attention_outflow_weights,
+        expansion_weights,
+        contraction_weights,
+        small,
+    )
+    sums = made[6]
+    doc = lax.axis_index("doc")
+    narrow = lax.dynamic_slice(sums, (0, doc * 32), (5, 32))
+    up = lax.dynamic_slice(sums, (5 + doc // 2, 0), (1, 128))
+    return tuple(made[:6]) + (narrow[0], narrow[1], narrow[2], narrow[3], up[0], narrow[4])
+
+
+def fits_fused(mesh, arguments):
+    features, tiles, expand = arguments[0], arguments[2], arguments[5]
+    return (
+        dict(mesh.shape) == {"seq": 8, "doc": 4}
+        and features.shape == (8, 1024, 1024)
+        and tiles.shape == (8, 16, 16, 3)
+        and expand.shape == (1024, 4096)
+    )
+
+
 def solution(mesh):
-    return jax.shard_map(
-        local,
-        mesh=mesh,
-        in_specs=(
-            P("doc", "seq", None),
-            P("doc"),
-            P("doc", None, None, None),
-            P(("seq", "doc"), None),
-            P(("seq", "doc"), None),
-            P(("seq", "doc"), None),
-            P(("seq", "doc"), None),
-            P(("seq", "doc")),
-            P(("seq", "doc")),
-            P(("seq", "doc")),
-            P(("seq", "doc")),
-            P(("seq", "doc")),
-            P(("seq", "doc")),
-            P("doc", "seq", None),
-        ),
-        out_specs=(
-            P("doc", "seq", None),
-            P("doc", "seq", None),
-            P(("seq", "doc"), None),
-            P(("seq", "doc"), None),
-            P(("seq", "doc"), None),
-            P(("seq", "doc"), None),
-            P(("seq", "doc")),
-            P(("seq", "doc")),
-            P(("seq", "doc")),
-            P(("seq", "doc")),
-            P(("seq", "doc")),
-            P(("seq", "doc")),
-        ),
-        check_vma=False,
-    )
+    in_specs = (
+        P("doc", "seq", None),
+        P("doc"),
+        P("doc", None, None, None),
+        P(("seq", "doc"), None),
+        P(("seq", "doc"), None),
+        P(("seq", "doc"), None),
+        P(("seq", "doc"), None),
+        P(("seq", "doc")),
+        P(("seq", "doc")),
+        P(("seq", "doc")),
+        P(("seq", "doc")),
+        P(("seq", "doc")),
+        P(("seq", "doc")),
+        P("doc", "seq", None),
+    )
+    out_specs = (
+        P("doc", "seq", None),
+        P("doc", "seq", None),
+        P(("seq", "doc"), None),
+        P(("seq", "doc"), None),
+        P(("seq", "doc"), None),
+        P(("seq", "doc"), None),
+        P(("seq", "doc")),
+        P(("seq", "doc")),
+        P(("seq", "doc")),
+        P(("seq", "doc")),
+        P(("seq", "doc")),
+        P(("seq", "doc")),
+    )
+
+    def run(*arguments):
+        body = local_fused if fits_fused(mesh, arguments) else local
+        mapped = jax.shard_map(
+            body, mesh=mesh, in_specs=in_specs, out_specs=out_specs, check_vma=False
+        )
+        return mapped(*arguments)
+
+    return run

time: 1750 us -> 330 us (0.19)
  waiting for transfers between devices: 864 us -> 0 us
  local copies, waits for them, and re-layouts: 377 us -> 12.3 us
  Pallas kernels: 0 us -> 313 us
  matrix products: 262 us -> 0 us
  blocking collectives: 123 us -> 0 us
  other arithmetic: 83.9 us -> 0.68 us
    reduce_scatter x4 -> x0, waiting for transfers between devices: 577 us -> none  [the longest x1 188 us: local(): lax.psum_scatter(contract_grad, ('seq', 'doc'), scatter_dimension=0, tile...]
    pallas_call x0 -> x1, Pallas kernels: none -> 313 us  [local_fused(): pl.pallas_call(layer_kernel, name='layer', out_shape=[jax.ShapeDtypeStruc...]
    dot_general x100 -> x0, matrix products: 262 us -> none  [the longest x8 23.7 us: sparse_backward(): jnp.einsum('hitd,hickd->hitck', query_group, key_group, preferred_element...]
    while x4 -> x0, waiting for transfers between devices: 170 us -> none
    reshape x28 -> x2, local copies, waits for them, and re-layouts: 164 us -> 0.1 us  [local_fused(): tiles = sampled_target_tiles.reshape(docs, heads * blocks, count)]
    all_gather x5 -> x0, waiting for transfers between devices: 113 us -> none  [the longest x1 73.5 us: local(): pair_full = lax.all_gather(pair_local, 'seq', axis=1, tiled=True)]
    unnamed x2 -> x0, blocking collectives: 83.8 us -> none
    while x82 -> x0, local copies, waits for them, and re-layouts: 68.9 us -> none
  transfers between devices with their start and end apart: 11 -> 0, of which waited for: 9 -> 0; matrix products, arithmetic and copies ran while one was open for 15% -> 0% of each run, Pallas kernels for 0% -> 0%
where the time goes in v1:
time: 330 us; the launch traced here: 327 us
  Pallas kernels  313 us (95%)
  local copies, waits for them, and re-layouts  12.3 us (4%)
    pallas_call x1, Pallas kernels, local_fused(): pl.pallas_call(layer_kernel, name='layer', out_shape=[jax.ShapeDtypeStruc...  313 us
    unnamed x33, local copies, waits for them, and re-layouts  8.85 us

profile of v1, /device:TPU:0, one launch (start us, length us, event | category | flops | bytes accessed | tf_op | source)
XLA Modules:
  0.0 327.0 jit_solution(17173535107666352)
XLA Ops:
  0.6 0.0 copy-start.5
  0.7 0.0 copy-start.9
  0.7 0.0 copy-start.10
  0.7 0.0 copy-start.6
  0.7 0.0 copy-start.7
  0.7 0.0 copy-start.8
  0.7 0.6 copy-done.9
  1.3 0.0 copy-done.10
  1.3 0.0 copy-done.6
  1.4 0.0 copy-done.7
  1.4 0.0 copy-done.8
  1.4 0.1 maximum_bitcast_fusion
  1.5 0.0 copy-start.11
  1.5 0.7 copy-done.11
  2.1 0.0 copy-start.12
  2.1 0.1 broadcast_in_dim.2
  2.2 0.6 copy-done.12
  2.8 0.6 fusion.5.sv_in
  3.4 0.0 copy-done.5
  3.4 0.1 reshape.39
  3.5 0.1 copy.30
  3.7 0.7 pad.12.clone
  4.4 313.2 %layer.1 = (bf16[2,128,1024]{2,1,0:T(8,128)(2,1)}, f32[2,128,1024]{2,1,0:T(8,128)}, f32[32,3072]{1,0:T(8,128)}, f32[32,1024]{1,0:T(8,128)}, f32[32,4096]{1,0:T(8...) custom-call(bf16[2,2,64,1024]{3,2,1,0:T(8,128)(2,1)} %bitcast.24, bf16[2,128,1024]{2,1,0:T(8,128)(2,1)} %dy_in.1, ...), custom_call_target="tpu_custom_call" | custom-call | tf_op jit(solution)/shard_map/layer/pallas_call | solution.py:1452
  317.6 0.0 copy-start
  317.6 1.3 dynamic-slice_bitcast_fusion
  318.9 0.8 constant_dynamic-slice_fusion
  319.6 0.5 slice_bitcast_fusion
  320.2 1.9 copy.37
  322.0 0.0 copy-done
  322.0 0.0 copy-start.3
  322.1 1.0 copy.38
  323.0 0.3 copy-done.3
  323.3 0.0 copy-start.4
  323.3 0.0 copy-start.2
  323.3 0.7 copy.39
  324.0 0.2 copy-done.4
  324.3 0.7 copy.40
  324.9 0.0 copy-done.2
  324.9 0.0 copy-start.1
  324.9 0.8 copy.41
  325.7 0.4 copy-done.1
  326.2 0.8 copy.42
  (2 shorter events, 0.0 us)
Async XLA Ops:
  0.6 2.7 copy-start.5
  0.7 0.7 copy-start.9
  0.7 0.7 copy-start.10
  0.7 0.7 copy-start.6
  0.7 0.7 copy-start.7
  0.7 0.7 copy-start.8
  1.5 0.7 copy-start.11
  2.1 0.7 copy-start.12
  317.6 4.5 %copy-start = (f32[2,128,1024]{2,1,0:T(8,128)S(1)}, f32[2,128,1024]{2,1,0:T(8,128)}, u32[]{:S(2)}) copy-start(f32[2,128,1024]{2,1,0:T(8,128)} %get-tuple-element.46) | copy-start | bytes 3145732
  322.0 1.2 copy-start.3
  323.3 1.0 copy-start.4
  323.3 1.7 copy-start.2
  324.9 1.2 copy-start.1

commit v2 on v0

--- a/solution.py
+++ b/solution.py
@@ -1,6 +1,10 @@
+import types
+
 import jax
 import jax.numpy as jnp
 from jax import lax
+from jax.experimental import pallas as pl
+from jax.experimental.pallas import tpu as pltpu
 from jax.sharding import PartitionSpec as P
 
 group_heads = 4
@@ -539,39 +543,1037 @@
     return (output, grad_inputs) + tuple(summed)
 
 
+ROUTE = pl.DeviceIdType.MESH
+NZ, NX, NY, NC = 4, 2, 2, 2
+bf16, f32 = jnp.bfloat16, jnp.float32
+
+
+def nn(left, right):
+    return lax.dot_general(left, right, (((1,), (0,)), ((), ())), preferred_element_type=f32)
+
+
+def nt(left, right):
+    return lax.dot_general(left, right, (((1,), (1,)), ((), ())), preferred_element_type=f32)
+
+
+def tn(left, right):
+    return lax.dot_general(left, right, (((0,), (0,)), ((), ())), preferred_element_type=f32)
+
+
+def loop(count, body):
+    lax.fori_loop(0, count, body, 0)
+
+
+class Net:
+    def __init__(self, send_sems, recv_sems, here):
+        self.send_sems, self.recv_sems, self.here = send_sems, recv_sems, here
+        self.sent, self.taken = 0, 0
+        self.open = []
+
+    def slots(self, count):
+        first = self.taken
+        self.taken += count
+        assert self.taken <= RECVS
+        return first
+
+    def copy(self, src, dst, device, slot, index):
+        return pltpu.make_async_remote_copy(
+            src_ref=src,
+            dst_ref=dst,
+            send_sem=self.send_sems.at[index],
+            recv_sem=self.recv_sems.at[slot],
+            device_id=device,
+            device_id_type=ROUTE,
+        )
+
+    def series(self, count, describe, group=None):
+        base = self.sent
+        self.sent += count
+        assert self.sent <= SENDS
+
+        def start(i):
+            src, dst, device, slot, is_self, made = describe(i)
+            copy = self.copy(src, dst, device, slot, base + i)
+            if is_self is None:
+                if made is None:
+                    copy.start()
+                else:
+                    pl.when(made)(copy.start)
+            else:
+                pl.when(jnp.logical_not(is_self))(copy.start)
+                pl.when(is_self)(pltpu.make_async_copy(src, dst, self.recv_sems.at[slot]).start)
+
+        def finish():
+            for i in range(count):
+                src, dst, device, slot, is_self, made = describe(i)
+                copy = self.copy(src, dst, device, slot, base + i)
+                if is_self is not None:
+                    made = jnp.logical_not(is_self)
+                if made is None:
+                    copy.wait_send()
+                else:
+                    pl.when(made)(copy.wait_send)
+
+        self.open.append((group, finish))
+        return start
+
+    def send(self, src, dst, device, slot, group=None, is_self=None, made=None):
+        self.series(1, lambda i: (src, dst, device, slot, is_self, made), group)(0)
+
+    def settle(self, group=None, everything=False):
+        rest = []
+        for name, finish in self.open:
+            if everything or name == group:
+                finish()
+            else:
+                rest.append((name, finish))
+        self.open = rest
+
+    def arrive(self, dst, slot):
+        self.copy(dst, dst, self.here, slot, 0).wait_recv()
+
+
+def row_stats(values):
+    mean = jnp.mean(values, axis=-1, keepdims=True)
+    centered = values - mean
+    inverse = lax.rsqrt(jnp.mean(centered * centered, axis=-1, keepdims=True) + epsilon)
+    return centered * inverse, inverse
+
+
+def norm_pullback(grad, scaled, inverse, gain):
+    wide = grad * gain
+    first = jnp.mean(wide, axis=-1, keepdims=True)
+    second = jnp.mean(wide * scaled, axis=-1, keepdims=True)
+    return (wide - first - scaled * second) * inverse
+
+
+def column_sum(values):
+    return jnp.sum(values, axis=0, keepdims=True)
+
+
+SCRATCH = dict(
+    xr=((8, 2, 64, 1024), bf16),
+    n1=((8, 128, 1024), bf16),
+    aux=((64, 128), jnp.int32),
+    bias=((16, 4, 1024), f32),
+    sv=((4, 2, 2, 2, 8, 128), f32),
+    vec=((8, 1024), f32),
+    b1=((1, 1024), f32),
+    wqs=((4, 32, 768), bf16),
+    wq=((4, 2, 2, 2, 32, 768), bf16),
+    wo=((4, 2, 2, 2, 32, 1024), bf16),
+    w1s=((4, 32, 1024), bf16),
+    w1=((4, 2, 2, 2, 32, 1024), bf16),
+    w2=((4, 2, 128, 1024), bf16),
+    qkv=((1024, 768), bf16),
+    lse=((1024, 128), f32),
+    at=((8, 128, 256), bf16),
+    att=((2, 4, 128, 256), bf16),
+    mid=((256, 1024), f32),
+    nt2=((4, 256, 1024), bf16),
+    dyx=((4, 256, 1024), bf16),
+    act=((4, 256, 1024), bf16),
+    gp=((4, 256, 1024), bf16),
+    dw2=((4, 2, 128, 1024), bf16),
+    own=((256, 1024), f32),
+    gps=((4, 256, 1024), bf16),
+    gpr=((2, 256, 1024), bf16),
+    gpx=((256, 1024), bf16),
+    ops=((4, 256, 1024), bf16),
+    opr=((2, 256, 1024), bf16),
+    opx=((256, 1024), bf16),
+    gb=((256, 1024), bf16),
+    gm=((256, 1024), f32),
+    da=((2, 4, 128, 256), bf16),
+    do=((8, 128, 256), bf16),
+    dk=((1024, 256), f32),
+    dv=((1024, 256), f32),
+    rgs=((8, 64, 1024), bf16),
+    rgx=((4, 64, 1024), bf16),
+    gnr=((2, 2, 64, 1024), bf16),
+    r1y=((4, 2, 2, 32, 1024), bf16),
+    r1z=((4, 2, 2, 32, 1024), bf16),
+    r1v=((2, 2, 32, 1024), bf16),
+    f1=((2, 2, 32, 1024), f32),
+    r1f=((4, 32, 1024), f32),
+    r2y=((4, 128, 1024), bf16),
+    r2z=((4, 128, 1024), bf16),
+    r2v=((128, 1024), bf16),
+    ros=((4, 2, 2, 32, 1024), bf16),
+    roa=((4, 32, 1024), bf16),
+    rob=((4, 32, 1024), bf16),
+    rof=((4, 32, 1024), bf16),
+    roz=((4, 32, 1024), bf16),
+    rov=((32, 1024), bf16),
+    rqy=((4, 2, 2, 32, 768), bf16),
+    rqz=((4, 2, 2, 32, 768), bf16),
+    rqv=((2, 2, 32, 768), bf16),
+    fq=((2, 2, 32, 768), f32),
+    rqf=((4, 32, 768), f32),
+    sg=((2, 8, 8, 128), f32),
+    rsg=((2, 8, 8, 128), f32),
+    sgt=((2, 8, 128), f32),
+    rst=((2, 4, 8, 128), f32),
+)
+SENDS, RECVS = 256, 256
+VMEM_BYTES = 63 * 2**20
+
+
+def layer_kernel(
+    x_in, dy_in, aux_in, wq_in, wo_in, w1_in, w2_in, sv_in,
+    out_ref, gx_ref, dwq_ref, dwo_ref, dw1_ref, dw2_ref, sg_ref,
+    *rest,
+):
+    names = list(SCRATCH)
+    R = types.SimpleNamespace(**dict(zip(names, rest[: len(names)])))
+    send_sems, recv_sems = rest[len(names):]
+    s, d = lax.axis_index("seq"), lax.axis_index("doc")
+    z, x, y, c = s // NX, s % NX, d // NC, d % NC
+    g = 2 * x + c
+    flip, xo, yo = 1 - c, 1 - x, 1 - y
+
+    def at(zz, xx, yy, cc):
+        return (zz * NX + xx, yy * NC + cc)
+
+    here = (s, d)
+    sib, xn, yn, cross = at(z, x, y, flip), at(z, xo, y, c), at(z, x, yo, c), at(z, xo, y, flip)
+    group = ((x, flip, sib), (xo, c, xn), (xo, flip, cross))
+    net = Net(send_sems, recv_sems, here)
+    order = [z, z + 1 - 2 * (z // 2), (2 + 3 * z) % 5, 3 * (1 - z // 2)]
+    middle = jnp.logical_or(z == 1, z == 2)
+
+    barrier = pltpu.get_barrier_semaphore()
+
+    def greet(step, _):
+        other = (s * NC + c + step) % 16
+        pl.semaphore_signal(
+            barrier, inc=1, device_id=(other // NC, y * NC + other % NC), device_id_type=ROUTE
+        )
+        return 0
+
+    lax.fori_loop(1, 16, greet, 0)
+    for cc in (c, flip):
+        pl.semaphore_signal(barrier, inc=1, device_id=at(z, x, yo, cc), device_id_type=ROUTE)
+    pl.semaphore_wait(barrier, 17)
+
+    def z_start(piece, base, name):
+        for k in (1, 2, 3):
+            net.send(
+                piece(z), piece(z), at(order[k], x, y, c), base + z, name, made=middle if k == 3 else None
+            )
+
+    def z_take(piece, base, name, k):
+        part = piece(order[k])
+        net.arrive(part, base + order[k])
+        if k == 3:
+            net.send(part, part, at(order[2], x, y, c), base + order[3], name, made=middle)
+        return part
+
+    half = pl.ds(pl.multiple_of(c * 512, 512), 512)
+    other_half = pl.ds(pl.multiple_of(flip * 512, 512), 512)
+    xz = net.slots(4)
+    for b in range(2):
+        for ch in range(2):
+            zt = 2 * c + b
+            net.send(
+                x_in.at[b, :, :, ch * 512:(ch + 1) * 512],
+                R.xr.at[s, :, :, ch * 512:(ch + 1) * 512],
+                at(zt, x, y, ch),
+                xz + z,
+                is_self=jnp.logical_and(zt == z, c == ch),
+            )
+
+    for h in range(4):
+        for t in range(3):
+            R.wqs[h, :, t * 256:(t + 1) * 256] = wq_in[:, t * 1024 + h * 256:t * 1024 + (h + 1) * 256]
+    R.wq[z, x, y, c] = R.wqs[g]
+    wqa = net.slots(4)
+    for xx, cc, dev in group:
+        net.send(R.wqs.at[2 * xx + cc], R.wq.at[z, x, y, c], dev, wqa + g)
+
+    sv_s, sv_z, sv_x, sv_y = net.slots(1), net.slots(4), net.slots(1), net.slots(1)
+    R.sv[z, x, y, c] = sv_in[...]
+    net.send(R.sv.at[z, x, y, c], R.sv.at[z, x, y, c], sib, sv_s)
+
+    aux_s = net.slots(1)
+    has_table = c == z // 2
+
+    @pl.when(has_table)
+    def table():
+        R.aux[...] = aux_in[z % 2, g]
+
+    net.send(aux_in.at[z % 2, 2 * x + flip], R.aux, sib, aux_s, made=has_table)
+
+    for h in range(4):
+        for q in range(8):
+            block = 8 * (q // 2) + 4 * (h // 2) + 2 * (q % 2) + h % 2
+            R.w1s[h, :, q * 128:(q + 1) * 128] = w1_in[:, block * 128:(block + 1) * 128]
+    R.w1[z, x, y, c] = R.w1s[g]
+    w1a = net.slots(4)
+    for xx, cc, dev in group:
+        net.send(R.w1s.at[2 * xx + cc], R.w1.at[z, x, y, c], dev, w1a + g)
+    R.wo[z, x, y, c] = wo_in[...]
+    R.w2[z, y] = w2_in[...]
+    R.dyx[g] = dy_in[...].reshape(256, 1024)
+
+    def wq_piece(zz):
+        return R.wq.at[zz, :, y]
+
+    def w1_piece(zz):
+        return R.w1.at[zz, :, y]
+
+    def w2_piece(zz):
+        return R.w2.at[zz, y]
+
+    def wo_piece(zz):
+        return R.wo.at[zz, x, y, c]
+
+    wqz, wqy, w1z, w1y = net.slots(4), net.slots(4), net.slots(4), net.slots(4)
+    w2z, w2y, woz = net.slots(4), net.slots(4), net.slots(4)
+    for xx, cc, dev in group:
+        net.arrive(R.wq.at[z, xx, y, cc], wqa + 2 * xx + cc)
+    z_start(wq_piece, wqz, "w")
+    net.send(wq_piece(z), wq_piece(z), yn, wqy + z, "w")
+    net.arrive(R.sv.at[z, x, y, flip], sv_s)
+    z_start(lambda zz: R.sv.at[zz, x, y], sv_z, None)
+    for xx, cc, dev in group:
+        net.arrive(R.w1.at[z, xx, y, cc], w1a + 2 * xx + cc)
+    net.send(w1_piece(z), w1_piece(z), yn, w1y + z, "w")
+    net.send(w2_piece(z), w2_piece(z), yn, w2y + z, "w")
+
+    xx_r, xs_r = net.slots(4), net.slots(8)
+    for k in range(4):
+        zt = order[k]
+        part = R.xr.at[zt * 2 + x, :, :, half]
+        net.arrive(part, xz + zt)
+        net.send(part, part, xn, xx_r + zt, "xr")
+        net.send(part, part, sib, xs_r + zt * 2 + x, "xr")
+        if k:
+            part = z_take(wq_piece, wqz, "w", k)
+            net.send(part, part, yn, wqy + zt, "w")
+    z_start(w1_piece, w1z, "w")
+    z_start(wo_piece, woz, "w")
+    for k in (1, 2, 3):
+        z_take(lambda zz: R.sv.at[zz, x, y], sv_z, None, k)
+    net.send(R.sv.at[:, x, y], R.sv.at[:, x, y], xn, sv_x)
+    for k in range(4):
+        zt = order[k]
+        part = R.xr.at[zt * 2 + xo, :, :, half]
+        net.arrive(part, xx_r + zt)
+        net.send(part, part, sib, xs_r + zt * 2 + xo, "xr")
+        if k == 0:
+            net.arrive(R.sv.at[:, xo, y], sv_x)
+            net.send(R.sv.at[:, :, y], R.sv.at[:, :, y], yn, sv_y)
+
+    def group_gather(buf):
+        own_s, far_x, far_s = net.slots(1), net.slots(1), net.slots(1)
+
+        def begin():
+            net.send(buf.at[g], buf.at[g], sib, own_s)
+            net.send(buf.at[g], buf.at[g], xn, far_x)
+
+        def step():
+            net.arrive(buf.at[2 * xo + c], far_x)
+            net.send(buf.at[2 * xo + c], buf.at[2 * xo + c], sib, far_s)
+
+        def take(which):
+            if which == 1:
+                net.arrive(buf.at[2 * x + flip], own_s)
+            if which == 3:
+                net.arrive(buf.at[2 * xo + flip], far_s)
+
+        return begin, step, take
+
+    members = (g, 2 * x + flip, 2 * xo + c, 2 * xo + flip)
+    dy_begin, dy_step, dy_take = group_gather(R.dyx)
+    nt_begin, nt_step, nt_take = group_gather(R.nt2)
+
+    @pl.when(jnp.logical_not(has_table))
+    def table_here():
+        net.arrive(R.aux, aux_s)
+
+    for i in range(16):
+        tiles = R.aux[i * 4:(i + 1) * 4, :]
+        place = lax.broadcasted_iota(jnp.int32, (4, 1024), 1)
+        block = place >> 6
+        row = lax.broadcasted_iota(jnp.int32, (4, 1024), 0) + (i % 4) * 4
+        extent = tiles[:, 3:4]
+        last = (extent - 1) >> 6
+        seen = jnp.abs(row - block) <= 1
+        for k in range(3):
+            seen = seen | (block == tiles[:, k:k + 1])
+        seen = seen | (block == 0) | (block == last) | (row == 0) | (row == last)
+        seen = seen & (place < extent)
+        R.bias[i] = jnp.where(seen, 0.0, negative).astype(f32)
+
+    net.arrive(R.sv.at[:, :, yo], sv_y)
+    lane = lax.broadcasted_iota(jnp.int32, (1, 128), 1) >> 5
+    for r in range(8):
+        for k in range(5):
+            total = jnp.zeros((1, 128), f32)
+            for q in range(4):
+                line = R.sv[r // 2, r % 2, q // 2, q % 2, k // 4:k // 4 + 1, :]
+                shift = (32 * (q - k % 4)) % 128
+                if shift:
+                    line = pltpu.roll(line, shift, 1)
+                total = jnp.where(lane == q, line, total)
+            R.vec[k:k + 1, r * 128:(r + 1) * 128] = total
+    for q in range(8):
+        R.b1[:, q * 128:(q + 1) * 128] = R.sv[q // 2, x, q % 2, c, 2:3, :]
+
+    def first_norm(step, _):
+        zt = (z + step) % NZ
+        for k in range(2):
+            i = 2 * zt + k
+            net.arrive(R.xr.at[i, :, :, other_half], xs_r + i)
+            scaled, _inverse = row_stats(R.xr[i].reshape(128, 1024).astype(f32))
+            R.n1[i] = (scaled * R.vec[0:1, :] + R.vec[1:2, :]).astype(bf16)
+        return 0
+
+    loop(4, first_norm)
+    for k in range(4):
+        net.arrive(R.wq.at[order[k], :, yo], wqy + order[k])
+
+    def project(step, _):
+        rows = R.n1[pl.ds(2 * step, 2)].reshape(256, 1024)
+        made = nn(rows, R.wq[...].reshape(1024, 768)).astype(bf16)
+        where = pl.ds(pl.multiple_of(step * 256, 256), 256)
+        R.qkv[where, :] = jnp.concatenate([made[:, :256] * jnp.asarray(0.125, bf16), made[:, 256:]], axis=1)
+        return 0
+
+    loop(4, project)
+    dy_begin()
+    z_start(w2_piece, w2z, "w")
+
+    low_lane = lax.broadcasted_iota(jnp.int32, (1, 128), 1) < 64
+
+    def only(values, e):
+        return jnp.where(low_lane if e == 0 else jnp.logical_not(low_lane), values, jnp.zeros_like(values))
+
+    at_r = net.slots(8)
+    back_c = z // 2
+
+    def at_copy(i):
+        zt, xx = i // 2, i % 2
+        mine = jnp.logical_and(jnp.logical_and(zt == z, xx == x), c == back_c)
+        return R.at.at[i], R.att.at[z % 2, g], at(zt, xx, y, back_c), at_r + (z % 2) * 4 + g, mine, None
+
+    at_start = net.series(8, at_copy)
+
+    def attend_tile(step, _):
+        t = (z + step) % NZ
+        where = pl.ds(pl.multiple_of(t * 256, 256), 256)
+        for pair in range(2):
+            cols = slice(pair * 128, pair * 128 + 128)
+            kcols = slice(256 + pair * 128, 256 + pair * 128 + 128)
+            vcols = slice(512 + pair * 128, 512 + pair * 128 + 128)
+            q = R.qkv[where, cols]
+            mixed = None
+            for e in range(2):
+                h = pair * 2 + e
+                scores = nt(only(q, e), R.qkv[:, kcols])
+                scores = (scores.reshape(4, 64, 1024) + R.bias[h * 4 + t][:, None, :]).reshape(256, 1024)
+                top = jnp.max(scores, axis=-1, keepdims=True)
+                grown = jnp.exp(scores - top)
+                total = jnp.sum(grown, axis=-1, keepdims=True)
+                low = (grown * (1.0 / total)).astype(bf16)
+                R.lse[where, h:h + 1] = top + jnp.log(total)
+                got = nn(low, R.qkv[:, vcols])
+                mixed = got if e == 0 else jnp.where(low_lane, mixed, got)
+            R.at[pl.ds(2 * t, 2), :, cols] = mixed.astype(bf16).reshape(2, 128, 128)
+        at_start(2 * t)
+        at_start(2 * t + 1)
+        return 0
+
+    def attend(low, high):
+        lax.fori_loop(low, high, attend_tile, 0)
+
+    attend(1, 3)
+    for k in (1, 2):
+        part = z_take(w1_piece, w1z, "w", k)
+        net.send(part, part, yn, w1y + order[k], "w")
+    attend(3, 5)
+    part = z_take(w1_piece, w1z, "w", 3)
+    net.send(part, part, yn, w1y + order[3], "w")
+
+    ax, ay = (x + flip) % 2, (y + c) % 2
+    bx, by = (x + c) % 2, (y + flip) % 2
+    near, far = at(z, ax, ay, c), at(z, bx, by, c)
+    wo_a, wo_b, wo_d, wo_s = net.slots(1), net.slots(1), net.slots(1), net.slots(1)
+    for k in (1, 2, 3):
+        z_take(wo_piece, woz, "w", k)
+
+    def wo_column(xx, yy):
+        return R.wo.at[:, xx, yy, c]
+
+    net.send(wo_column(x, y), wo_column(x, y), near, wo_a, "w")
+    net.send(wo_column(x, y), wo_column(x, y), far, wo_b, "w")
+    dy_step()
+    part = z_take(w2_piece, w2z, "w", 1)
+    net.send(part, part, yn, w2y + order[1], "w")
+    net.arrive(wo_column(ax, ay), wo_a)
+    net.send(wo_column(ax, ay), wo_column(ax, ay), far, wo_d, "w")
+    for k in (2, 3):
+        part = z_take(w2_piece, w2z, "w", k)
+        net.send(part, part, yn, w2y + order[k], "w")
+    net.arrive(wo_column(bx, by), wo_b)
+    net.arrive(wo_column(xo, yo), wo_d)
+    net.send(R.wo.at[:, :, :, c], R.wo.at[:, :, :, c], sib, wo_s, "w")
+    net.arrive(R.wo.at[:, :, :, flip], wo_s)
+    for b in range(2):
+        for h in range(4):
+            net.arrive(R.att.at[b, h], at_r + b * 4 + h)
+
+    def outflow():
+        for n in range(4):
+            cols = slice(n * 256, n * 256 + 256)
+            made = x_in[:, :, :, cols].reshape(256, 256).astype(f32)
+            for h in range(4):
+                made = made + nn(
+                    R.att[:, h].reshape(256, 256),
+                    R.wo[h, :, :, :, :, cols].reshape(256, 256),
+                )
+            R.mid[:, cols] = made
+        for k in range(2):
+            where = slice(k * 128, k * 128 + 128)
+            scaled, _inverse = row_stats(R.mid[where, :])
+            R.nt2[g, where, :] = (scaled * R.vec[2:3, :] + R.vec[3:4, :]).astype(bf16)
+
+    outflow()
+    nt_begin()
+
+    for k in range(4):
+        net.arrive(R.w1.at[order[k], :, yo], w1y + order[k])
+
+    def widen_rows(which):
+        def widen(j, _):
+            where = pl.ds(pl.multiple_of(j * 256, 256), 256)
+            pre = nn(R.nt2[which], R.w1[:, :, :, :, :, where].reshape(1024, 256))
+            pre = pre + R.b1[:, where]
+            share = 0.5 * (1.0 + lax.erf(pre * (2.0 ** -0.5)))
+            R.act[which, :, where] = (pre * share).astype(bf16)
+            slope = share + pre * (jnp.exp(-0.5 * pre * pre) * (1.0 / (2.0 * jnp.pi) ** 0.5))
+            R.gp[which, :, where] = slope.astype(bf16)
+            return 0
+
+        loop(4, widen)
+
+    widen_rows(members[0])
+    nt_take(1)
+    widen_rows(members[1])
+    nt_step()
+    widen_rows(members[2])
+    nt_take(3)
+    widen_rows(members[3])
+    dy_take(1)
+    dy_take(3)
+
+    def outer_two(j, _):
+        where = pl.ds(pl.multiple_of(j * 256, 256), 256)
+        made = tn(R.act[:, :, where].reshape(1024, 256), R.dyx[...].reshape(1024, 1024))
+        R.dw2[j] = made.astype(bf16).reshape(2, 128, 1024)
+        return 0
+
+    loop(4, outer_two)
+
+    def scatter(piece, away, landing_y, landing_z, landing_v, name):
+        base_y, base_z, base_v = net.slots(4), net.slots(4), net.slots(1)
+
+        def begin(ks=(3, 2, 1, 0)):
+            for k in ks:
+                net.send(away(order[k]), landing_y.at[order[k]], yn, base_y + order[k], name)
+
+        def add(ref, other):
+            ref[...] = (ref[...].astype(f32) + other[...].astype(f32)).astype(bf16)
+
+        def take(k):
+            net.arrive(landing_y.at[order[k]], base_y + order[k])
+            add(piece(order[k]), landing_y.at[order[k]])
+
+        def along(k):
+            part = piece(order[k])
+            if k == 3:
+                net.send(part, landing_v, at(order[1], x, y, c), base_v, name, made=jnp.logical_not(middle))
+
+                @pl.when(middle)
+                def pass_on():
+                    net.arrive(landing_v, base_v)
+                    add(part, landing_v)
+
+                net.send(part, landing_z.at[z], at(order[3], x, y, c), base_z + z, name, made=middle)
+            else:
+                net.send(part, landing_z.at[z], at(order[k], x, y, c), base_z + z, name)
+
+        def final(out):
+            out[...] = piece(z)[...].astype(f32)
+            for k in (1, 2):
+                net.arrive(landing_z.at[order[k]], base_z + order[k])
+                out[...] += landing_z[order[k]].astype(f32)
+
+            @pl.when(middle)
+            def from_end():
+                net.arrive(landing_z.at[order[3]], base_z + order[3])
+                out[...] += landing_z[order[3]].astype(f32)
+
+        return begin, take, along, final
+
+    two_begin, two_take, two_along, two_final = scatter(
+        lambda zz: R.dw2.at[zz, y], lambda zz: R.dw2.at[zz, yo], R.r2y, R.r2z, R.r2v, "s2"
+    )
+    two_begin()
+
+    for k in range(4):
+        net.arrive(R.w2.at[order[k], yo], w2y + order[k])
+
+    def narrow_back_rows(which):
+        def narrow_back(j, _):
+            where = pl.ds(pl.multiple_of(j * 256, 256), 256)
+            made = nt(R.dyx[which], R.w2[j].reshape(256, 1024)) * R.gp[which, :, where].astype(f32)
+            R.gp[which, :, where] = made.astype(bf16)
+            return 0
+
+        loop(4, narrow_back)
+
+    def group_reduce(product, sent, landing, landing_x):
+        slot_s, slot_x = net.slots(2), net.slots(1)
+        for which, where in ((members[3], xo), (members[2], None), (members[1], x), (members[0], None)):
+            if which is members[0]:
+                product(which, R.own)
+            else:
+                product(which, sent.at[which])
+            if where is not None:
+                net.send(sent.at[which], landing.at[where], sib, slot_s + where)
+            elif which is members[2]:
+                net.arrive(landing.at[xo], slot_s + xo)
+                sent[which] = (sent[which].astype(f32) + landing[xo].astype(f32)).astype(bf16)
+                net.send(sent.at[which], landing_x, xn, slot_x)
+        net.arrive(landing.at[x], slot_s + x)
+        net.arrive(landing_x, slot_x)
+
+    def grad_norm_part(which, out):
+        narrow_back_rows(which)
+
+        def back(n, _):
+            made = nt(R.gp[which], R.w1[n].reshape(256, 1024))
+            out[:, pl.ds(pl.multiple_of(n * 256, 256), 256)] = made.astype(out.dtype)
+            return 0
+
+        loop(4, back)
+
+    group_reduce(grad_norm_part, R.gps, R.gpr, R.gpx)
+    sums = [jnp.zeros((1, 1024), f32) for _ in range(3)]
+
+    def norm_two_back():
+        for k in range(4):
+            where = slice(k * 64, k * 64 + 64)
+            grad = R.own[where, :] + R.gpr[x, where, :].astype(f32) + R.gpx[where, :].astype(f32)
+            scaled, inverse = row_stats(R.mid[where, :])
+            flow = dy_in[k // 2, (k % 2) * 64:(k % 2) * 64 + 64, :].astype(f32)
+            sums[0] = sums[0] + column_sum(grad * scaled)
+            sums[1] = sums[1] + column_sum(grad)
+            sums[2] = sums[2] + column_sum(flow)
+            total = flow + norm_pullback(grad, scaled, inverse, R.vec[2:3, :])
+            R.gm[where, :] = total
+            R.gb[where, :] = total.astype(bf16)
+
+    norm_two_back()
+
+    do_r = net.slots(8)
+
+    def outflow_back(h, _):
+        made = nt(R.gb[...], R.wo[h].reshape(256, 1024)).astype(bf16)
+        R.da[:, h] = made.reshape(2, 128, 256)
+        return 0
+
+    loop(4, outflow_back)
+    for b in range(2):
+        for xx in (x, xo):
+            for cc in (c, flip):
+                zt = 2 * c + b
+                net.send(
+                    R.da.at[b, 2 * xx + cc],
+                    R.do.at[s],
+                    at(zt, xx, y, cc),
+                    do_r + s,
+                    is_self=jnp.logical_and(zt == z, jnp.logical_and(xx == x, cc == c)),
+                )
+
+    net.settle("w")
+
+    def outer_one(n, _):
+        left = R.nt2[:, :, pl.ds(pl.multiple_of(n * 256, 256), 256)].reshape(1024, 256)
+        made = tn(left, R.gp[...].reshape(1024, 1024)).astype(bf16)
+        R.w1[n] = made.reshape(2, 2, 2, 32, 1024)
+        return 0
+
+    loop(4, outer_one)
+    one_begin, one_take, one_along, one_final = scatter(
+        w1_piece, lambda zz: R.w1.at[zz, :, yo], R.r1y, R.r1z, R.r1v, "s1"
+    )
+    one_begin()
+
+    def outer_flow():
+        for h in range(4):
+            made = tn(R.att[:, h].reshape(256, 256), R.gb[...]).astype(bf16)
+            R.wo[h] = made.reshape(2, 2, 2, 32, 1024)
+
+    outer_flow()
+    ros_s = net.slots(1)
+    net.send(R.wo.at[:, :, :, flip], R.ros, sib, ros_s)
+    for k in (3, 2, 1, 0):
+        two_take(k)
+        if k:
+            two_along(k)
+
+    R.dk[...] = jnp.zeros((1024, 256), f32)
+    R.dv[...] = jnp.zeros((1024, 256), f32)
+
+    def attend_back_tile(step, _):
+        t = (z + step) % NZ
+        where = pl.ds(pl.multiple_of(t * 256, 256), 256)
+        two = pl.ds(2 * t, 2)
+        for k in range(2):
+            net.arrive(R.do.at[2 * t + k], do_r + 2 * t + k)
+        for pair in range(2):
+            cols = slice(pair * 128, pair * 128 + 128)
+            kcols = slice(256 + pair * 128, 256 + pair * 128 + 128)
+            vcols = slice(512 + pair * 128, 512 + pair * 128 + 128)
+            q = R.qkv[where, cols]
+            grad = R.do[two, :, cols].reshape(256, 128)
+            prod = grad.astype(f32) * R.at[two, :, cols].reshape(256, 128).astype(f32)
+            query = None
+            for e in range(2):
+                h = pair * 2 + e
+                qe, ge = only(q, e), only(grad, e)
+                scores = nt(qe, R.qkv[:, kcols])
+                scores = (scores.reshape(4, 64, 1024) + R.bias[h * 4 + t][:, None, :]).reshape(256, 1024)
+                chances = jnp.exp(scores - R.lse[where, h:h + 1])
+                central = jnp.sum(only(prod, e), axis=-1, keepdims=True)
+                moved = nt(ge, R.qkv[:, vcols])
+                back = (chances * (moved - central)).astype(bf16)
+                R.dv[:, cols] += tn(chances.astype(bf16), ge)
+                R.dk[:, cols] += tn(back, qe)
+                got = nn(back, R.qkv[:, kcols])
+                query = got if e == 0 else jnp.where(low_lane, query, got)
+            R.qkv[where, cols] = (query * 0.125).astype(bf16)
+        return 0
+
+    def attend_back(low, high):
+        lax.fori_loop(low, high, attend_back_tile, 0)
+
+    attend_back(0, 2)
+    for k in (3, 2, 1, 0):
+        one_take(k)
+        if k:
+            one_along(k)
+    net.arrive(R.ros, ros_s)
+    for k in range(4):
+        R.wo[k, :, :, c] = (R.wo[k, :, :, c].astype(f32) + R.ros[k].astype(f32)).astype(bf16)
+    roa_s, rob_s, rof_s, roz_s, rov_s = net.slots(1), net.slots(1), net.slots(1), net.slots(4), net.slots(1)
+    net.send(wo_column(xo, yo), R.roa, far, roa_s)
+    net.send(wo_column(bx, by), R.rob, far, rob_s)
+    attend_back(2, 4)
+    R.qkv[:, 256:512] = R.dk[...].astype(bf16)
+    R.qkv[:, 512:768] = R.dv[...].astype(bf16)
+
+    net.settle("xr")
+
+    def unproject(step, _):
+        t = (z + 1 + step) % NZ
+        where = pl.ds(pl.multiple_of(t * 256, 256), 256)
+        made = nt(R.qkv[where, :], R.wq[...].reshape(1024, 768)).astype(bf16)
+        R.xr[pl.ds(2 * t, 2)] = made.reshape(2, 2, 64, 1024)
+        gs_start(t)
+        return 0
+
+    rgs_s, rgx_s, gnr_s = net.slots(4), net.slots(4), net.slots(4)
+    gs_start = net.series(
+        4,
+        lambda t: (
+            R.xr.at[pl.ds(2 * t, 2), flip], R.rgs.at[pl.ds(2 * t, 2)], sib, rgs_s + t, None, None
+        ),
+    )
+    loop(4, unproject)
+
+    def outer_in(n, _):
+        cols = pl.ds(pl.multiple_of(n * 256, 256), 256)
+        made = tn(R.n1[:, :, cols].reshape(1024, 256), R.qkv[...]).astype(bf16)
+        R.wq[n] = made.reshape(2, 2, 2, 32, 768)
+        return 0
+
+    loop(4, outer_in)
+    q_begin, q_take, q_along, q_final = scatter(
+        wq_piece, lambda zz: R.wq.at[zz, :, yo], R.rqy, R.rqz, R.rqv, "sq"
+    )
+    q_begin()
+    for k in (3, 2, 1, 0):
+        zt = order[k]
+        i = zt * 2 + xo
+        net.arrive(R.rgs.at[pl.ds(2 * zt, 2)], rgs_s + zt)
+        R.xr[i, c] = (R.xr[i, c].astype(f32) + R.rgs[i].astype(f32)).astype(bf16)
+        net.send(R.xr.at[i, c], R.rgx.at[zt], xn, rgx_s + zt)
+    net.arrive(R.roa, roa_s)
+    part = wo_column(ax, ay)
+    part[...] = (part[...].astype(f32) + R.roa[...].astype(f32)).astype(bf16)
+    net.send(part, R.rof, near, rof_s)
+    for k in (3, 2, 1, 0):
+        zt = order[k]
+        i = zt * 2 + x
+        net.arrive(R.rgx.at[zt], rgx_s + zt)
+        R.xr[i, c] = (
+            R.xr[i, c].astype(f32) + R.rgs[i].astype(f32) + R.rgx[zt].astype(f32)
+        ).astype(bf16)
+        net.send(
+            R.xr.at[i, c],
+            R.gnr.at[z % 2, c],
+            at(zt, x, y, back_c),
+            gnr_s + 2 * (z % 2) + c,
+            is_self=jnp.logical_and(zt == z, c == back_c),
+        )
+    for k in (3, 2, 1, 0):
+        q_take(k)
+        if k:
+            q_along(k)
+
+    net.arrive(R.rob, rob_s)
+    net.arrive(R.rof, rof_s)
+    part = wo_column(x, y)
+    part[...] = (part[...].astype(f32) + R.rob[...].astype(f32) + R.rof[...].astype(f32)).astype(bf16)
+    for k in (1, 2, 3):
+        net.send(wo_piece(order[k]), R.roz.at[z], at(order[k], x, y, c), roz_s + z)
+
+    def contract_part(which, out):
+        def forth(n, _):
+            cols = pl.ds(pl.multiple_of(n * 256, 256), 256)
+            made = nn(R.act[which], R.w2[:, :, :, cols].reshape(1024, 256))
+            out[:, cols] = made.astype(out.dtype)
+            return 0
+
+        loop(4, forth)
+
+    group_reduce(contract_part, R.ops, R.opr, R.opx)
+    for k in range(2):
+        where = slice(k * 128, k * 128 + 128)
+        total = R.mid[where, :] + R.own[where, :] + R.opr[x, where, :].astype(f32)
+        out_ref[k] = (total + R.opx[where, :].astype(f32) + R.vec[4:5, :]).astype(bf16)
+
+    def note(which, row, line):
+        for r in range(8):
+            R.sg[which, r, row:row + 1, :] = line[:, r * 128:(r + 1) * 128]
+
+    def small_begin(which):
+        base = net.slots(8)
+        for k in (3, 2, 1, 0):
+            for xx in (xo, x):
+                if k == 0 and xx is x:
+                    continue
+                zt = order[k]
+                net.send(R.sg.at[which, zt * 2 + xx], R.rsg.at[which, s], at(zt, xx, y, c), base + s)
+        return base
+
+    def small_middle(which, base):
+        total = R.sg[which, s]
+        for k in (1, 2, 3, 0):
+            for xx in (x, xo):
+                if k == 0 and xx is x:
+                    continue
+                i = order[k] * 2 + xx
+                net.arrive(R.rsg.at[which, i], base + i)
+                total = total + R.rsg[which, i]
+        R.sgt[which] = total
+        slot = net.slots(4)
+        for yy, cc in ((y, flip), (yo, c), (yo, flip)):
+            net.send(R.sgt.at[which], R.rst.at[which, 2 * y + c], at(z, x, yy, cc), slot + 2 * y + c)
+        return slot
+
+    def small_end(which, slot):
+        row = lax.broadcasted_iota(jnp.int32, (8, 128), 0)
+        total = R.sgt[which]
+        for yy, cc in ((y, flip), (yo, c), (yo, flip)):
+            i = 2 * yy + cc
+            net.arrive(R.rst.at[which, i], slot + i)
+            got = R.rst[which, i]
+            total = total + (got if cc is c else jnp.where(row < 5, got, 0.0))
+        return total
+
+    R.sg[...] = jnp.zeros((2, 8, 8, 128), f32)
+    for k in range(3):
+        note(0, 2 + k, sums[k])
+    up = [jnp.zeros((1, 1024), f32)]
+
+    def up_sum():
+        for k in range(16):
+            rows = slice((k % 4) * 64, (k % 4) * 64 + 64)
+            up[0] = up[0] + column_sum(R.gp[k // 4, rows, :].astype(f32))
+
+    up_sum()
+    for q in range(8):
+        R.sg[0, 2 * (q // 2) + x, 5 + q % 2:6 + q % 2, :] = up[0][:, q * 128:(q + 1) * 128]
+    early = small_begin(0)
+    two_final(dw2_ref)
+    early = small_middle(0, early)
+
+    for b in range(2):
+        for cc in range(2):
+            net.arrive(R.gnr.at[b, cc], gnr_s + 2 * b + cc)
+    sums = [jnp.zeros((1, 1024), f32) for _ in range(2)]
+    for k in range(4):
+        rows = slice((k % 2) * 64, (k % 2) * 64 + 64)
+        grad = R.gnr[k // 2, k % 2].astype(f32)
+        scaled, inverse = row_stats(x_in[k // 2, k % 2].astype(f32))
+        sums[0] = sums[0] + column_sum(grad * scaled)
+        sums[1] = sums[1] + column_sum(grad)
+        gx_ref[k // 2, rows, :] = R.gm[k * 64:(k + 1) * 64, :] + norm_pullback(
+            grad, scaled, inverse, R.vec[0:1, :]
+        )
+    for k in range(2):
+        note(1, k, sums[k])
+    late = small_begin(1)
+
+    r1f_s, rqf_s = net.slots(4), net.slots(4)
+    one_final(R.f1)
+    for xx, cc, dev in group:
+        net.send(R.f1.at[xx, cc], R.r1f.at[g], dev, r1f_s + g)
+    R.r1f[g] = R.f1[x, c]
+    q_final(R.fq)
+    for xx, cc, dev in group:
+        net.send(R.fq.at[xx, cc], R.rqf.at[g], dev, rqf_s + g)
+    R.rqf[g] = R.fq[x, c]
+    late = small_middle(1, late)
+
+    dwo_ref[...] = wo_piece(z)[...].astype(f32)
+    for k in (1, 2, 3):
+        net.arrive(R.roz.at[order[k]], roz_s + order[k])
+        dwo_ref[...] += R.roz[order[k]].astype(f32)
+    for xx, cc, dev in group:
+        net.arrive(R.r1f.at[2 * xx + cc], r1f_s + 2 * xx + cc)
+    for h in range(4):
+        for q in range(8):
+            block = 8 * (q // 2) + 4 * (h // 2) + 2 * (q % 2) + h % 2
+            dw1_ref[:, block * 128:(block + 1) * 128] = R.r1f[h, :, q * 128:(q + 1) * 128]
+    for xx, cc, dev in group:
+        net.arrive(R.rqf.at[2 * xx + cc], rqf_s + 2 * xx + cc)
+    for h in range(4):
+        for t in range(3):
+            dwq_ref[:, t * 1024 + h * 256:t * 1024 + (h + 1) * 256] = R.rqf[h, :, t * 256:(t + 1) * 256]
+    sg_ref[...] = small_end(0, early) + small_end(1, late)
+    net.settle(everything=True)
+
+
+def local_fused(
+    arriving_features,
+    valid_extents,
+    sampled_target_tiles,
+    query_context_mapping,
+    attention_outflow_weights,
+    expansion_weights,
+    contraction_weights,
+    opening_scale_vector,
+    opening_shift_vector,
+    closing_scale_vector,
+    closing_shift_vector,
+    expansion_shift,
+    contraction_shift,
+    output_sensitivity,
+):
+    docs, heads, blocks, count = sampled_target_tiles.shape
+    tiles = sampled_target_tiles.reshape(docs, heads * blocks, count)
+    extents = jnp.broadcast_to(valid_extents[:, None, None], (docs, heads * blocks, 1))
+    aux = jnp.concatenate([tiles, extents], axis=2)
+    aux = jnp.pad(aux, ((0, 0), (0, 0), (0, 124))).reshape(docs, 4, 64, 128)
+    line_one = jnp.concatenate(
+        [opening_scale_vector, opening_shift_vector, closing_scale_vector, closing_shift_vector]
+    )
+    line_two = jnp.pad(contraction_shift, (0, 96))
+    small = jnp.pad(jnp.stack([line_one, line_two, expansion_shift]), ((0, 5), (0, 0))).astype(f32)
+    shapes = (
+        (arriving_features.shape, bf16),
+        (arriving_features.shape, f32),
+        (query_context_mapping.shape, f32),
+        (attention_outflow_weights.shape, f32),
+        (expansion_weights.shape, f32),
+        (contraction_weights.shape, f32),
+        ((8, 128), f32),
+    )
+    whole = pl.BlockSpec(memory_space=pltpu.VMEM)
+    made = pl.pallas_call(
+        layer_kernel,
+        name="layer",
+        out_shape=[jax.ShapeDtypeStruct(a, b) for a, b in shapes],
+        in_specs=[whole] * 8,
+        out_specs=[whole] * 7,
+        scratch_shapes=[pltpu.VMEM(a, b) for a, b in SCRATCH.values()]
+        + [
+            pltpu.SemaphoreType.DMA((SENDS,)),
+            pltpu.SemaphoreType.DMA((RECVS,)),
+        ],
+        compiler_params=pltpu.CompilerParams(
+            collective_id=0, has_side_effects=True, vmem_limit_bytes=VMEM_BYTES
+        ),
+    )(
+        arriving_features.reshape(2, 2, 64, 1024),
+        output_sensitivity,
+        aux,
+        query_context_mapping,
+        attention_outflow_weights,
+        expansion_weights,
+        contraction_weights,
+        small,
+    )
+    sums = made[6]
+    doc = lax.axis_index("doc")
+    narrow = lax.dynamic_slice(sums, (0, doc * 32), (5, 32))
+    up = lax.dynamic_slice(sums, (5 + doc // 2, 0), (1, 128))
+    return tuple(made[:6]) + (narrow[0], narrow[1], narrow[2], narrow[3], up[0], narrow[4])
+
+
+def fits_fused(mesh, arguments):
+    features, tiles, expand = arguments[0], arguments[2], arguments[5]
+    return (
+        dict(mesh.shape) == {"seq": 8, "doc": 4}
+        and features.shape == (8, 1024, 1024)
+        and tiles.shape == (8, 16, 16, 3)
+        and expand.shape == (1024, 4096)
+    )
+
+
 def solution(mesh):
-    return jax.shard_map(
-        local,
-        mesh=mesh,
-        in_specs=(
-            P("doc", "seq", None),
-            P("doc"),
-            P("doc", None, None, None),
-            P(("seq", "doc"), None),
-            P(("seq", "doc"), None),
-            P(("seq", "doc"), None),
-            P(("seq", "doc"), None),
-            P(("seq", "doc")),
-            P(("seq", "doc")),
-            P(("seq", "doc")),
-            P(("seq", "doc")),
-            P(("seq", "doc")),
-            P(("seq", "doc")),
-            P("doc", "seq", None),
-        ),
-        out_specs=(
-            P("doc", "seq", None),
-            P("doc", "seq", None),
-            P(("seq", "doc"), None),
-            P(("seq", "doc"), None),
-            P(("seq", "doc"), None),
-            P(("seq", "doc"), None),
-            P(("seq", "doc")),
-            P(("seq", "doc")),
-            P(("seq", "doc")),
-            P(("seq", "doc")),
-            P(("seq", "doc")),
-            P(("seq", "doc")),
-        ),
-        check_vma=False,
-    )
+    in_specs = (
+        P("doc", "seq", None),
+        P("doc"),
+        P("doc", None, None, None),
+        P(("seq", "doc"), None),
+        P(("seq", "doc"), None),
+        P(("seq", "doc"), None),
+        P(("seq", "doc"), None),
+        P(("seq", "doc")),
+        P(("seq", "doc")),
+        P(("seq", "doc")),
+        P(("seq", "doc")),
+        P(("seq", "doc")),
+        P(("seq", "doc")),
+        P("doc", "seq", None),
+    )
+    out_specs = (
+        P("doc", "seq", None),
+        P("doc", "seq", None),
+        P(("seq", "doc"), None),
+        P(("seq", "doc"), None),
+        P(("seq", "doc"), None),
+        P(("seq", "doc"), None),
+        P(("seq", "doc")),
+        P(("seq", "doc")),
+        P(("seq", "doc")),
+        P(("seq", "doc")),
+        P(("seq", "doc")),
+        P(("seq", "doc")),
+    )
+
+    def run(*arguments):
+        body = local_fused if fits_fused(mesh, arguments) else local
+        mapped = jax.shard_map(
+            body, mesh=mesh, in_specs=in_specs, out_specs=out_specs, check_vma=False
+        )
+        return mapped(*arguments)
+
+    return run

time: 1750 us -> 260 us (0.15)
  waiting for transfers between devices: 864 us -> 0 us
  local copies, waits for them, and re-layouts: 377 us -> 12.3 us
  matrix products: 262 us -> 0 us
  Pallas kernels: 0 us -> 246 us
  blocking collectives: 123 us -> 0 us
  other arithmetic: 83.9 us -> 0.68 us
    reduce_scatter x4 -> x0, waiting for transfers between devices: 577 us -> none  [the longest x1 188 us: local(): lax.psum_scatter(contract_grad, ('seq', 'doc'), scatter_dimension=0, tile...]
    dot_general x100 -> x0, matrix products: 262 us -> none  [the longest x8 23.7 us: sparse_backward(): jnp.einsum('hitd,hickd->hitck', query_group, key_group, preferred_element...]
    pallas_call x0 -> x1, Pallas kernels: none -> 246 us  [local_fused(): pl.pallas_call(layer_kernel, name='layer', out_shape=[jax.ShapeDtypeStruc...]
    while x4 -> x0, waiting for transfers between devices: 170 us -> none
    reshape x28 -> x2, local copies, waits for them, and re-layouts: 164 us -> 0.1 us  [local_fused(): tiles = sampled_target_tiles.reshape(docs, heads * blocks, count)]
    all_gather x5 -> x0, waiting for transfers between devices: 113 us -> none  [the longest x1 73.5 us: local(): pair_full = lax.all_gather(pair_local, 'seq', axis=1, tiled=True)]
    unnamed x2 -> x0, blocking collectives: 83.8 us -> none
    while x82 -> x0, local copies, waits for them, and re-layouts: 68.9 us -> none
  transfers between devices with their start and end apart: 11 -> 0, of which waited for: 9 -> 0; matrix products, arithmetic and copies ran while one was open for 15% -> 0% of each run, Pallas kernels for 0% -> 0%
where the time goes in v2:
time: 260 us; the launch traced here: 259 us
  Pallas kernels  246 us (95%)
  local copies, waits for them, and re-layouts  12.3 us (5%)
    pallas_call x1, Pallas kernels, local_fused(): pl.pallas_call(layer_kernel, name='layer', out_shape=[jax.ShapeDtypeStruc...  246 us
    unnamed x33, local copies, waits for them, and re-layouts  8.85 us

profile of v2, /device:TPU:0, one launch (start us, length us, event | category | flops | bytes accessed | tf_op | source)
XLA Modules:
  0.0 259.4 jit_solution(4219926830425652105)
XLA Ops:
  0.6 0.0 copy-start.5
  0.7 0.0 copy-start.9
  0.7 0.0 copy-start.10
  0.7 0.0 copy-start.6
  0.7 0.0 copy-start.7
  0.7 0.0 copy-start.8
  0.7 0.6 copy-done.9
  1.3 0.0 copy-done.10
  1.3 0.0 copy-done.6
  1.4 0.0 copy-done.7
  1.4 0.0 copy-done.8
  1.4 0.1 maximum_bitcast_fusion
  1.5 0.0 copy-start.11
  1.5 0.7 copy-done.11
  2.1 0.0 copy-start.12
  2.1 0.1 broadcast_in_dim.2
  2.2 0.6 copy-done.12
  2.8 0.6 fusion.5.sv_in
  3.4 0.0 copy-done.5
  3.4 0.1 reshape.39
  3.5 0.1 copy.30
  3.7 0.7 pad.12.clone
  4.4 245.6 %layer.1 = (bf16[2,128,1024]{2,1,0:T(8,128)(2,1)}, f32[2,128,1024]{2,1,0:T(8,128)}, f32[32,3072]{1,0:T(8,128)}, f32[32,1024]{1,0:T(8,128)}, f32[32,4096]{1,0:T(8...) custom-call(bf16[2,2,64,1024]{3,2,1,0:T(8,128)(2,1)} %bitcast.24, bf16[2,128,1024]{2,1,0:T(8,128)(2,1)} %dy_in.1, ...), custom_call_target="tpu_custom_call" | custom-call | tf_op jit(solution)/shard_map/layer/pallas_call | solution.py:1499
  250.0 0.0 copy-start
  250.0 1.3 dynamic-slice_bitcast_fusion
  251.3 0.8 constant_dynamic-slice_fusion
  252.1 0.5 slice_bitcast_fusion
  252.6 1.9 copy.37
  254.5 0.0 copy-done
  254.5 0.0 copy-start.3
  254.5 1.0 copy.38
  255.4 0.3 copy-done.3
  255.7 0.0 copy-start.4
  255.7 0.0 copy-start.2
  255.7 0.7 copy.39
  256.4 0.2 copy-done.4
  256.7 0.7 copy.40
  257.4 0.0 copy-done.2
  257.4 0.0 copy-start.1
  257.4 0.8 copy.41
  258.1 0.4 copy-done.1
  258.6 0.8 copy.42
  (2 shorter events, 0.0 us)
Async XLA Ops:
  0.6 2.7 %copy-start.5 = (s32[2,16,16,3]{2,1,3,0:T(8,128)S(1)}, s32[2,16,16,3]{2,1,3,0:T(8,128)}, u32[]{:S(2)}) copy-start(s32[2,16,16,3]{2,1,3,0:T(8,128)} %param.16) | copy-start | bytes 18436
  0.7 0.7 copy-start.9
  0.7 0.7 copy-start.10
  0.7 0.7 copy-start.6
  0.7 0.7 copy-start.7
  0.7 0.7 copy-start.8
  1.5 0.7 copy-start.11
  2.1 0.7 copy-start.12
  250.0 4.5 %copy-start = (f32[2,128,1024]{2,1,0:T(8,128)S(1)}, f32[2,128,1024]{2,1,0:T(8,128)}, u32[]{:S(2)}) copy-start(f32[2,128,1024]{2,1,0:T(8,128)} %get-tuple-element.46) | copy-start | bytes 3145732
  254.5 1.2 copy-start.3
  255.7 1.0 copy-start.4
  255.7 1.7 copy-start.2
  257.4 1.2 copy-start.1

commit v3 on v2

--- a/solution.py
+++ b/solution.py
@@ -655,6 +655,8 @@
     xr=((8, 2, 64, 1024), bf16),
     n1=((8, 128, 1024), bf16),
     aux=((64, 128), jnp.int32),
+    aux2=((4, 16, 128), jnp.int32),
+    table=((16, 16, 128), jnp.int32),
     bias=((16, 4, 1024), f32),
     sv=((4, 2, 2, 2, 8, 128), f32),
     vec=((8, 1024), f32),
@@ -686,8 +688,9 @@
     gm=((256, 1024), f32),
     da=((2, 4, 128, 256), bf16),
     do=((8, 128, 256), bf16),
-    dk=((1024, 256), f32),
-    dv=((1024, 256), f32),
+    dk=((1024, 128), f32),
+    dv=((1024, 128), f32),
+    dwq=((2, 4, 2, 2, 2, 32, 384), bf16),
     rgs=((8, 64, 1024), bf16),
     rgx=((4, 64, 1024), bf16),
     gnr=((2, 2, 64, 1024), bf16),
@@ -705,9 +708,9 @@
     rof=((4, 32, 1024), bf16),
     roz=((4, 32, 1024), bf16),
     rov=((32, 1024), bf16),
-    rqy=((4, 2, 2, 32, 768), bf16),
-    rqz=((4, 2, 2, 32, 768), bf16),
-    rqv=((2, 2, 32, 768), bf16),
+    rqy=((2, 4, 2, 2, 32, 384), bf16),
+    rqz=((2, 4, 2, 2, 32, 384), bf16),
+    rqv=((2, 2, 2, 32, 384), bf16),
     fq=((2, 2, 32, 768), f32),
     rqf=((4, 32, 768), f32),
     sg=((2, 8, 8, 128), f32),
@@ -720,7 +723,8 @@
 
 
 def layer_kernel(
-    x_in, dy_in, aux_in, wq_in, wo_in, w1_in, w2_in, sv_in,
+    x_in, dy_in, extent_in, tiles_in, wq_in, wo_in, w1_in, w2_in,
+    gain_one, shift_one, gain_two, shift_two, shift_up, shift_down,
     out_ref, gx_ref, dwq_ref, dwo_ref, dw1_ref, dw2_ref, sg_ref,
     *rest,
 ):
@@ -754,6 +758,38 @@
     lax.fori_loop(1, 16, greet, 0)
     for cc in (c, flip):
         pl.semaphore_signal(barrier, inc=1, device_id=at(z, x, yo, cc), device_id_type=ROUTE)
+    for h in range(4):
+        for t in range(3):
+            for pair in range(2):
+                src = t * 1024 + h * 256 + pair * 128
+                dst = pair * 384 + t * 128
+                R.wqs[h, :, dst:dst + 128] = wq_in[:, src:src + 128]
+    R.wq[z, x, y, c] = R.wqs[g]
+    small = R.sv.at[z, x, y, c]
+    small[...] = jnp.zeros((8, 128), f32)
+    for k, vector in enumerate((gain_one, shift_one, gain_two, shift_two)):
+        small[0:1, k * 32:(k + 1) * 32] = vector[...].astype(f32)
+    small[1:2, 0:32] = shift_down[...].astype(f32)
+    small[2:3, :] = shift_up[...].astype(f32)
+    for h in range(4):
+        for q in range(8):
+            block = 8 * (q // 2) + 4 * (h // 2) + 2 * (q % 2) + h % 2
+            R.w1s[h, :, q * 128:(q + 1) * 128] = w1_in[:, block * 128:(block + 1) * 128]
+    R.w1[z, x, y, c] = R.w1s[g]
+    R.wo[z, x, y, c] = wo_in[...]
+    R.w2[z, y] = w2_in[...]
+    R.dyx[g] = dy_in[...].reshape(256, 1024)
+    R.sg[...] = jnp.zeros((2, 8, 8, 128), f32)
+    has_table = c == z // 2
+
+    for h in range(16):
+        R.table[h, :, 0:3] = tiles_in[z % 2, h]
+    R.table[:, :, 3:4] = jnp.full((16, 16, 1), extent_in[z % 2], jnp.int32)
+
+    @pl.when(has_table)
+    def table():
+        R.aux[...] = R.table[pl.ds(4 * g, 4)].reshape(64, 128)
+
     pl.semaphore_wait(barrier, 17)
 
     def z_start(piece, base, name):
@@ -783,38 +819,19 @@
                 is_self=jnp.logical_and(zt == z, c == ch),
             )
 
-    for h in range(4):
-        for t in range(3):
-            R.wqs[h, :, t * 256:(t + 1) * 256] = wq_in[:, t * 1024 + h * 256:t * 1024 + (h + 1) * 256]
-    R.wq[z, x, y, c] = R.wqs[g]
     wqa = net.slots(4)
     for xx, cc, dev in group:
         net.send(R.wqs.at[2 * xx + cc], R.wq.at[z, x, y, c], dev, wqa + g)
 
     sv_s, sv_z, sv_x, sv_y = net.slots(1), net.slots(4), net.slots(1), net.slots(1)
-    R.sv[z, x, y, c] = sv_in[...]
     net.send(R.sv.at[z, x, y, c], R.sv.at[z, x, y, c], sib, sv_s)
 
     aux_s = net.slots(1)
-    has_table = c == z // 2
-
-    @pl.when(has_table)
-    def table():
-        R.aux[...] = aux_in[z % 2, g]
-
-    net.send(aux_in.at[z % 2, 2 * x + flip], R.aux, sib, aux_s, made=has_table)
-
-    for h in range(4):
-        for q in range(8):
-            block = 8 * (q // 2) + 4 * (h // 2) + 2 * (q % 2) + h % 2
-            R.w1s[h, :, q * 128:(q + 1) * 128] = w1_in[:, block * 128:(block + 1) * 128]
-    R.w1[z, x, y, c] = R.w1s[g]
+    net.send(R.table.at[pl.ds(4 * (2 * x + flip), 4)], R.aux2, sib, aux_s, made=has_table)
+
     w1a = net.slots(4)
     for xx, cc, dev in group:
         net.send(R.w1s.at[2 * xx + cc], R.w1.at[z, x, y, c], dev, w1a + g)
-    R.wo[z, x, y, c] = wo_in[...]
-    R.w2[z, y] = w2_in[...]
-    R.dyx[g] = dy_in[...].reshape(256, 1024)
 
     def wq_piece(zz):
         return R.wq.at[zz, :, y]
@@ -833,34 +850,33 @@
     for xx, cc, dev in group:
         net.arrive(R.wq.at[z, xx, y, cc], wqa + 2 * xx + cc)
     z_start(wq_piece, wqz, "w")
-    net.send(wq_piece(z), wq_piece(z), yn, wqy + z, "w")
+    net.send(wq_piece(z), wq_piece(z), yn, wqy + 0, "w")
     net.arrive(R.sv.at[z, x, y, flip], sv_s)
     z_start(lambda zz: R.sv.at[zz, x, y], sv_z, None)
     for xx, cc, dev in group:
         net.arrive(R.w1.at[z, xx, y, cc], w1a + 2 * xx + cc)
-    net.send(w1_piece(z), w1_piece(z), yn, w1y + z, "w")
-    net.send(w2_piece(z), w2_piece(z), yn, w2y + z, "w")
-
-    xx_r, xs_r = net.slots(4), net.slots(8)
+    net.send(w1_piece(z), w1_piece(z), yn, w1y + 0, "w")
+
+    xx_r, xs_a, xs_b = net.slots(4), net.slots(4), net.slots(4)
     for k in range(4):
         zt = order[k]
         part = R.xr.at[zt * 2 + x, :, :, half]
         net.arrive(part, xz + zt)
-        net.send(part, part, xn, xx_r + zt, "xr")
-        net.send(part, part, sib, xs_r + zt * 2 + x, "xr")
+        net.send(part, part, xn, xx_r + k, "xr")
+        net.send(part, part, sib, xs_a + k, "xr")
         if k:
             part = z_take(wq_piece, wqz, "w", k)
-            net.send(part, part, yn, wqy + zt, "w")
+            net.send(part, part, yn, wqy + k, "w")
+    z_start(wo_piece, woz, "w")
     z_start(w1_piece, w1z, "w")
-    z_start(wo_piece, woz, "w")
     for k in (1, 2, 3):
         z_take(lambda zz: R.sv.at[zz, x, y], sv_z, None, k)
     net.send(R.sv.at[:, x, y], R.sv.at[:, x, y], xn, sv_x)
     for k in range(4):
         zt = order[k]
         part = R.xr.at[zt * 2 + xo, :, :, half]
-        net.arrive(part, xx_r + zt)
-        net.send(part, part, sib, xs_r + zt * 2 + xo, "xr")
+        net.arrive(part, xx_r + k)
+        net.send(part, part, sib, xs_b + k, "xr")
         if k == 0:
             net.arrive(R.sv.at[:, xo, y], sv_x)
             net.send(R.sv.at[:, :, y], R.sv.at[:, :, y], yn, sv_y)
@@ -890,7 +906,8 @@
 
     @pl.when(jnp.logical_not(has_table))
     def table_here():
-        net.arrive(R.aux, aux_s)
+        net.arrive(R.aux2, aux_s)
+        R.aux[...] = R.aux2[...].reshape(64, 128)
 
     for i in range(16):
         tiles = R.aux[i * 4:(i + 1) * 4, :]
@@ -921,34 +938,48 @@
     for q in range(8):
         R.b1[:, q * 128:(q + 1) * 128] = R.sv[q // 2, x, q % 2, c, 2:3, :]
 
-    def first_norm(step, _):
-        zt = (z + step) % NZ
-        for k in range(2):
+    def first_norm(zt):
+        def rows(k, _):
             i = 2 * zt + k
-            net.arrive(R.xr.at[i, :, :, other_half], xs_r + i)
             scaled, _inverse = row_stats(R.xr[i].reshape(128, 1024).astype(f32))
             R.n1[i] = (scaled * R.vec[0:1, :] + R.vec[1:2, :]).astype(bf16)
-        return 0
-
-    loop(4, first_norm)
+            return 0
+
+        loop(2, rows)
+
     for k in range(4):
-        net.arrive(R.wq.at[order[k], :, yo], wqy + order[k])
+        zt = order[k]
+        net.arrive(R.xr.at[zt * 2 + x, :, :, other_half], xs_a + k)
+        net.arrive(R.xr.at[zt * 2 + xo, :, :, other_half], xs_b + k)
+        first_norm(zt)
+    for k in range(4):
+        net.arrive(R.wq.at[order[k], :, yo], wqy + k)
 
     def project(step, _):
         rows = R.n1[pl.ds(2 * step, 2)].reshape(256, 1024)
         made = nn(rows, R.wq[...].reshape(1024, 768)).astype(bf16)
         where = pl.ds(pl.multiple_of(step * 256, 256), 256)
-        R.qkv[where, :] = jnp.concatenate([made[:, :256] * jnp.asarray(0.125, bf16), made[:, 256:]], axis=1)
+        eighth = jnp.asarray(0.125, bf16)
+        R.qkv[where, :] = jnp.concatenate(
+            [made[:, :128] * eighth, made[:, 128:384], made[:, 384:512] * eighth, made[:, 512:]], axis=1
+        )
         return 0
 
     loop(4, project)
-    dy_begin()
-    z_start(w2_piece, w2z, "w")
 
     low_lane = lax.broadcasted_iota(jnp.int32, (1, 128), 1) < 64
 
     def only(values, e):
         return jnp.where(low_lane if e == 0 else jnp.logical_not(low_lane), values, jnp.zeros_like(values))
+
+    def pair_columns(pair):
+        first = pair * 384
+        return (
+            slice(pair * 128, pair * 128 + 128),
+            slice(first, first + 128),
+            slice(first + 128, first + 256),
+            slice(first + 256, first + 384),
+        )
 
     at_r = net.slots(8)
     back_c = z // 2
@@ -964,10 +995,8 @@
         t = (z + step) % NZ
         where = pl.ds(pl.multiple_of(t * 256, 256), 256)
         for pair in range(2):
-            cols = slice(pair * 128, pair * 128 + 128)
-            kcols = slice(256 + pair * 128, 256 + pair * 128 + 128)
-            vcols = slice(512 + pair * 128, 512 + pair * 128 + 128)
-            q = R.qkv[where, cols]
+            cols, qcols, kcols, vcols = pair_columns(pair)
+            q = R.qkv[where, qcols]
             mixed = None
             for e in range(2):
                 h = pair * 2 + e
@@ -988,34 +1017,37 @@
     def attend(low, high):
         lax.fori_loop(low, high, attend_tile, 0)
 
-    attend(1, 3)
-    for k in (1, 2):
-        part = z_take(w1_piece, w1z, "w", k)
-        net.send(part, part, yn, w1y + order[k], "w")
-    attend(3, 5)
-    part = z_take(w1_piece, w1z, "w", 3)
-    net.send(part, part, yn, w1y + order[3], "w")
-
     ax, ay = (x + flip) % 2, (y + c) % 2
     bx, by = (x + c) % 2, (y + flip) % 2
     near, far = at(z, ax, ay, c), at(z, bx, by, c)
     wo_a, wo_b, wo_d, wo_s = net.slots(1), net.slots(1), net.slots(1), net.slots(1)
+
+    def wo_column(xx, yy):
+        return R.wo.at[:, xx, yy, c]
+
+    def w1_step(k):
+        part = z_take(w1_piece, w1z, "w", k)
+        net.send(part, part, yn, w1y + k, "w")
+
+    def w2_step(k):
+        part = z_take(w2_piece, w2z, "w", k)
+        net.send(part, part, yn, w2y + k, "w")
+
     for k in (1, 2, 3):
         z_take(wo_piece, woz, "w", k)
-
-    def wo_column(xx, yy):
-        return R.wo.at[:, xx, yy, c]
-
     net.send(wo_column(x, y), wo_column(x, y), near, wo_a, "w")
     net.send(wo_column(x, y), wo_column(x, y), far, wo_b, "w")
-    dy_step()
-    part = z_take(w2_piece, w2z, "w", 1)
-    net.send(part, part, yn, w2y + order[1], "w")
+    attend(1, 2)
     net.arrive(wo_column(ax, ay), wo_a)
     net.send(wo_column(ax, ay), wo_column(ax, ay), far, wo_d, "w")
-    for k in (2, 3):
-        part = z_take(w2_piece, w2z, "w", k)
-        net.send(part, part, yn, w2y + order[k], "w")
+    w1_step(1)
+    attend(2, 3)
+    dy_begin()
+    w1_step(2)
+    attend(3, 4)
+    w1_step(3)
+    attend(4, 5)
+    dy_step()
     net.arrive(wo_column(bx, by), wo_b)
     net.arrive(wo_column(xo, yo), wo_d)
     net.send(R.wo.at[:, :, :, c], R.wo.at[:, :, :, c], sib, wo_s, "w")
@@ -1023,6 +1055,8 @@
     for b in range(2):
         for h in range(4):
             net.arrive(R.att.at[b, h], at_r + b * 4 + h)
+    z_start(w2_piece, w2z, "w")
+    net.send(w2_piece(z), w2_piece(z), yn, w2y + 0, "w")
 
     def outflow():
         for n in range(4):
@@ -1043,7 +1077,7 @@
     nt_begin()
 
     for k in range(4):
-        net.arrive(R.w1.at[order[k], :, yo], w1y + order[k])
+        net.arrive(R.w1.at[order[k], :, yo], w1y + k)
 
     def widen_rows(which):
         def widen(j, _):
@@ -1059,11 +1093,14 @@
         loop(4, widen)
 
     widen_rows(members[0])
+    w2_step(1)
     nt_take(1)
     widen_rows(members[1])
     nt_step()
+    w2_step(2)
     widen_rows(members[2])
     nt_take(3)
+    w2_step(3)
     widen_rows(members[3])
     dy_take(1)
     dy_take(3)
@@ -1081,13 +1118,13 @@
 
         def begin(ks=(3, 2, 1, 0)):
             for k in ks:
-                net.send(away(order[k]), landing_y.at[order[k]], yn, base_y + order[k], name)
+                net.send(away(order[k]), landing_y.at[order[k]], yn, base_y + k, name)
 
         def add(ref, other):
             ref[...] = (ref[...].astype(f32) + other[...].astype(f32)).astype(bf16)
 
         def take(k):
-            net.arrive(landing_y.at[order[k]], base_y + order[k])
+            net.arrive(landing_y.at[order[k]], base_y + k)
             add(piece(order[k]), landing_y.at[order[k]])
 
         def along(k):
@@ -1123,7 +1160,7 @@
     two_begin()
 
     for k in range(4):
-        net.arrive(R.w2.at[order[k], yo], w2y + order[k])
+        net.arrive(R.w2.at[order[k], yo], w2y + k)
 
     def narrow_back_rows(which):
         def narrow_back(j, _):
@@ -1134,11 +1171,11 @@
 
         loop(4, narrow_back)
 
-    def group_reduce(product, sent, landing, landing_x):
+    def group_reduce(product, sent, landing, landing_x, kept):
         slot_s, slot_x = net.slots(2), net.slots(1)
         for which, where in ((members[3], xo), (members[2], None), (members[1], x), (members[0], None)):
             if which is members[0]:
-                product(which, R.own)
+                product(which, kept)
             else:
                 product(which, sent.at[which])
             if where is not None:
@@ -1147,8 +1184,12 @@
                 net.arrive(landing.at[xo], slot_s + xo)
                 sent[which] = (sent[which].astype(f32) + landing[xo].astype(f32)).astype(bf16)
                 net.send(sent.at[which], landing_x, xn, slot_x)
-        net.arrive(landing.at[x], slot_s + x)
-        net.arrive(landing_x, slot_x)
+
+        def finish():
+            net.arrive(landing.at[x], slot_s + x)
+            net.arrive(landing_x, slot_x)
+
+        return finish
 
     def grad_norm_part(which, out):
         narrow_back_rows(which)
@@ -1160,7 +1201,22 @@
 
         loop(4, back)
 
-    group_reduce(grad_norm_part, R.gps, R.gpr, R.gpx)
+    gn_finish = group_reduce(grad_norm_part, R.gps, R.gpr, R.gpx, R.own)
+    net.settle("w")
+
+    def outer_one(n, _):
+        left = R.nt2[:, :, pl.ds(pl.multiple_of(n * 256, 256), 256)].reshape(1024, 256)
+        made = tn(left, R.gp[...].reshape(1024, 1024)).astype(bf16)
+        R.w1[n] = made.reshape(2, 2, 2, 32, 1024)
+        return 0
+
+    loop(4, outer_one)
+    one_begin, one_take, one_along, one_final = scatter(
+        w1_piece, lambda zz: R.w1.at[zz, :, yo], R.r1y, R.r1z, R.r1v, "s1"
+    )
+    one_begin()
+
+    gn_finish()
     sums = [jnp.zeros((1, 1024), f32) for _ in range(3)]
 
     def norm_two_back():
@@ -1198,19 +1254,6 @@
                     is_self=jnp.logical_and(zt == z, jnp.logical_and(xx == x, cc == c)),
                 )
 
-    net.settle("w")
-
-    def outer_one(n, _):
-        left = R.nt2[:, :, pl.ds(pl.multiple_of(n * 256, 256), 256)].reshape(1024, 256)
-        made = tn(left, R.gp[...].reshape(1024, 1024)).astype(bf16)
-        R.w1[n] = made.reshape(2, 2, 2, 32, 1024)
-        return 0
-
-    loop(4, outer_one)
-    one_begin, one_take, one_along, one_final = scatter(
-        w1_piece, lambda zz: R.w1.at[zz, :, yo], R.r1y, R.r1z, R.r1v, "s1"
-    )
-    one_begin()
 
     def outer_flow():
         for h in range(4):
@@ -1220,127 +1263,6 @@
     outer_flow()
     ros_s = net.slots(1)
     net.send(R.wo.at[:, :, :, flip], R.ros, sib, ros_s)
-    for k in (3, 2, 1, 0):
-        two_take(k)
-        if k:
-            two_along(k)
-
-    R.dk[...] = jnp.zeros((1024, 256), f32)
-    R.dv[...] = jnp.zeros((1024, 256), f32)
-
-    def attend_back_tile(step, _):
-        t = (z + step) % NZ
-        where = pl.ds(pl.multiple_of(t * 256, 256), 256)
-        two = pl.ds(2 * t, 2)
-        for k in range(2):
-            net.arrive(R.do.at[2 * t + k], do_r + 2 * t + k)
-        for pair in range(2):
-            cols = slice(pair * 128, pair * 128 + 128)
-            kcols = slice(256 + pair * 128, 256 + pair * 128 + 128)
-            vcols = slice(512 + pair * 128, 512 + pair * 128 + 128)
-            q = R.qkv[where, cols]
-            grad = R.do[two, :, cols].reshape(256, 128)
-            prod = grad.astype(f32) * R.at[two, :, cols].reshape(256, 128).astype(f32)
-            query = None
-            for e in range(2):
-                h = pair * 2 + e
-                qe, ge = only(q, e), only(grad, e)
-                scores = nt(qe, R.qkv[:, kcols])
-                scores = (scores.reshape(4, 64, 1024) + R.bias[h * 4 + t][:, None, :]).reshape(256, 1024)
-                chances = jnp.exp(scores - R.lse[where, h:h + 1])
-                central = jnp.sum(only(prod, e), axis=-1, keepdims=True)
-                moved = nt(ge, R.qkv[:, vcols])
-                back = (chances * (moved - central)).astype(bf16)
-                R.dv[:, cols] += tn(chances.astype(bf16), ge)
-                R.dk[:, cols] += tn(back, qe)
-                got = nn(back, R.qkv[:, kcols])
-                query = got if e == 0 else jnp.where(low_lane, query, got)
-            R.qkv[where, cols] = (query * 0.125).astype(bf16)
-        return 0
-
-    def attend_back(low, high):
-        lax.fori_loop(low, high, attend_back_tile, 0)
-
-    attend_back(0, 2)
-    for k in (3, 2, 1, 0):
-        one_take(k)
-        if k:
-            one_along(k)
-    net.arrive(R.ros, ros_s)
-    for k in range(4):
-        R.wo[k, :, :, c] = (R.wo[k, :, :, c].astype(f32) + R.ros[k].astype(f32)).astype(bf16)
-    roa_s, rob_s, rof_s, roz_s, rov_s = net.slots(1), net.slots(1), net.slots(1), net.slots(4), net.slots(1)
-    net.send(wo_column(xo, yo), R.roa, far, roa_s)
-    net.send(wo_column(bx, by), R.rob, far, rob_s)
-    attend_back(2, 4)
-    R.qkv[:, 256:512] = R.dk[...].astype(bf16)
-    R.qkv[:, 512:768] = R.dv[...].astype(bf16)
-
-    net.settle("xr")
-
-    def unproject(step, _):
-        t = (z + 1 + step) % NZ
-        where = pl.ds(pl.multiple_of(t * 256, 256), 256)
-        made = nt(R.qkv[where, :], R.wq[...].reshape(1024, 768)).astype(bf16)
-        R.xr[pl.ds(2 * t, 2)] = made.reshape(2, 2, 64, 1024)
-        gs_start(t)
-        return 0
-
-    rgs_s, rgx_s, gnr_s = net.slots(4), net.slots(4), net.slots(4)
-    gs_start = net.series(
-        4,
-        lambda t: (
-            R.xr.at[pl.ds(2 * t, 2), flip], R.rgs.at[pl.ds(2 * t, 2)], sib, rgs_s + t, None, None
-        ),
-    )
-    loop(4, unproject)
-
-    def outer_in(n, _):
-        cols = pl.ds(pl.multiple_of(n * 256, 256), 256)
-        made = tn(R.n1[:, :, cols].reshape(1024, 256), R.qkv[...]).astype(bf16)
-        R.wq[n] = made.reshape(2, 2, 2, 32, 768)
-        return 0
-
-    loop(4, outer_in)
-    q_begin, q_take, q_along, q_final = scatter(
-        wq_piece, lambda zz: R.wq.at[zz, :, yo], R.rqy, R.rqz, R.rqv, "sq"
-    )
-    q_begin()
-    for k in (3, 2, 1, 0):
-        zt = order[k]
-        i = zt * 2 + xo
-        net.arrive(R.rgs.at[pl.ds(2 * zt, 2)], rgs_s + zt)
-        R.xr[i, c] = (R.xr[i, c].astype(f32) + R.rgs[i].astype(f32)).astype(bf16)
-        net.send(R.xr.at[i, c], R.rgx.at[zt], xn, rgx_s + zt)
-    net.arrive(R.roa, roa_s)
-    part = wo_column(ax, ay)
-    part[...] = (part[...].astype(f32) + R.roa[...].astype(f32)).astype(bf16)
-    net.send(part, R.rof, near, rof_s)
-    for k in (3, 2, 1, 0):
-        zt = order[k]
-        i = zt * 2 + x
-        net.arrive(R.rgx.at[zt], rgx_s + zt)
-        R.xr[i, c] = (
-            R.xr[i, c].astype(f32) + R.rgs[i].astype(f32) + R.rgx[zt].astype(f32)
-        ).astype(bf16)
-        net.send(
-            R.xr.at[i, c],
-            R.gnr.at[z % 2, c],
-            at(zt, x, y, back_c),
-            gnr_s + 2 * (z % 2) + c,
-            is_self=jnp.logical_and(zt == z, c == back_c),
-        )
-    for k in (3, 2, 1, 0):
-        q_take(k)
-        if k:
-            q_along(k)
-
-    net.arrive(R.rob, rob_s)
-    net.arrive(R.rof, rof_s)
-    part = wo_column(x, y)
-    part[...] = (part[...].astype(f32) + R.rob[...].astype(f32) + R.rof[...].astype(f32)).astype(bf16)
-    for k in (1, 2, 3):
-        net.send(wo_piece(order[k]), R.roz.at[z], at(order[k], x, y, c), roz_s + z)
 
     def contract_part(which, out):
         def forth(n, _):
@@ -1351,11 +1273,11 @@
 
         loop(4, forth)
 
-    group_reduce(contract_part, R.ops, R.opr, R.opx)
-    for k in range(2):
-        where = slice(k * 128, k * 128 + 128)
-        total = R.mid[where, :] + R.own[where, :] + R.opr[x, where, :].astype(f32)
-        out_ref[k] = (total + R.opx[where, :].astype(f32) + R.vec[4:5, :]).astype(bf16)
+    out_finish = group_reduce(contract_part, R.ops, R.opr, R.opx, R.own)
+    for k in (3, 2, 1, 0):
+        two_take(k)
+        if k:
+            two_along(k)
 
     def note(which, row, line):
         for r in range(8):
@@ -1396,7 +1318,6 @@
             total = total + (got if cc is c else jnp.where(row < 5, got, 0.0))
         return total
 
-    R.sg[...] = jnp.zeros((2, 8, 8, 128), f32)
     for k in range(3):
         note(0, 2 + k, sums[k])
     up = [jnp.zeros((1, 1024), f32)]
@@ -1410,14 +1331,147 @@
     for q in range(8):
         R.sg[0, 2 * (q // 2) + x, 5 + q % 2:6 + q % 2, :] = up[0][:, q * 128:(q + 1) * 128]
     early = small_begin(0)
+
+    def attend_back(pair):
+        cols, qcols, kcols, vcols = pair_columns(pair)
+        R.dk[...] = jnp.zeros((1024, 128), f32)
+        R.dv[...] = jnp.zeros((1024, 128), f32)
+
+        def tile(step, _):
+            t = (z + step) % NZ
+            where = pl.ds(pl.multiple_of(t * 256, 256), 256)
+            two = pl.ds(2 * t, 2)
+            if pair == 0:
+                for k in range(2):
+                    net.arrive(R.do.at[2 * t + k], do_r + 2 * t + k)
+            q = R.qkv[where, qcols]
+            grad = R.do[two, :, cols].reshape(256, 128)
+            prod = grad.astype(f32) * R.at[two, :, cols].reshape(256, 128).astype(f32)
+            query = None
+            for e in range(2):
+                h = pair * 2 + e
+                qe, ge = only(q, e), only(grad, e)
+                scores = nt(qe, R.qkv[:, kcols])
+                scores = (scores.reshape(4, 64, 1024) + R.bias[h * 4 + t][:, None, :]).reshape(256, 1024)
+                chances = jnp.exp(scores - R.lse[where, h:h + 1])
+                central = jnp.sum(only(prod, e), axis=-1, keepdims=True)
+                moved = nt(ge, R.qkv[:, vcols])
+                back = (chances * (moved - central)).astype(bf16)
+                R.dv[...] += tn(chances.astype(bf16), ge)
+                R.dk[...] += tn(back, qe)
+                got = nn(back, R.qkv[:, kcols])
+                query = got if e == 0 else jnp.where(low_lane, query, got)
+            R.qkv[where, qcols] = (query * 0.125).astype(bf16)
+            return 0
+
+        lax.fori_loop(0, 4, tile, 0)
+        R.qkv[:, kcols] = R.dk[...].astype(bf16)
+        R.qkv[:, vcols] = R.dv[...].astype(bf16)
+
+    def outer_in_pair(pair):
+        def outer_in(n, _):
+            rows = pl.ds(pl.multiple_of(n * 256, 256), 256)
+            made = tn(R.n1[:, :, rows].reshape(1024, 256), R.qkv[:, pair * 384:pair * 384 + 384])
+            R.dwq[pair, n] = made.astype(bf16).reshape(2, 2, 2, 32, 384)
+            return 0
+
+        loop(4, outer_in)
+        steps = scatter(
+            lambda zz: R.dwq.at[pair, zz, :, y],
+            lambda zz: R.dwq.at[pair, zz, :, yo],
+            R.rqy.at[pair],
+            R.rqz.at[pair],
+            R.rqv.at[pair],
+            None,
+        )
+        steps[0]()
+        return steps
+
+    attend_back(0)
+    for k in (3, 2, 1, 0):
+        one_take(k)
+        if k:
+            one_along(k)
+    net.arrive(R.ros, ros_s)
+    for k in range(4):
+        R.wo[k, :, :, c] = (R.wo[k, :, :, c].astype(f32) + R.ros[k].astype(f32)).astype(bf16)
+    roa_s, rob_s, rof_s, roz_s = net.slots(1), net.slots(1), net.slots(1), net.slots(4)
+    net.send(wo_column(xo, yo), R.roa, far, roa_s)
+    net.send(wo_column(bx, by), R.rob, far, rob_s)
+    q0_begin, q0_take, q0_along, q0_final = outer_in_pair(0)
+    early = small_middle(0, early)
+    out_finish()
+    for k in range(2):
+        where = slice(k * 128, k * 128 + 128)
+        total = R.mid[where, :] + R.own[where, :] + R.opr[x, where, :].astype(f32)
+        out_ref[k] = (total + R.opx[where, :].astype(f32) + R.vec[4:5, :]).astype(bf16)
+    attend_back(1)
+
+    net.settle("xr")
+
+    def unproject(step, _):
+        t = (z + 1 + step) % NZ
+        where = pl.ds(pl.multiple_of(t * 256, 256), 256)
+        made = nt(R.qkv[where, :], R.wq[...].reshape(1024, 768)).astype(bf16)
+        R.xr[pl.ds(2 * t, 2)] = made.reshape(2, 2, 64, 1024)
+        gs_start(t)
+        return 0
+
+    rgs_s, rgx_s, gnr_s = net.slots(4), net.slots(4), net.slots(4)
+    gs_start = net.series(
+        4,
+        lambda t: (
+            R.xr.at[pl.ds(2 * t, 2), flip], R.rgs.at[pl.ds(2 * t, 2)], sib, rgs_s + t, None, None
+        ),
+    )
+    loop(4, unproject)
+
+    for k in (3, 2, 1, 0):
+        q0_take(k)
+        if k:
+            q0_along(k)
+    q1_begin, q1_take, q1_along, q1_final = outer_in_pair(1)
+    for k in (3, 2, 1, 0):
+        zt = order[k]
+        i = zt * 2 + xo
+        net.arrive(R.rgs.at[pl.ds(2 * zt, 2)], rgs_s + zt)
+        R.xr[i, c] = (R.xr[i, c].astype(f32) + R.rgs[i].astype(f32)).astype(bf16)
+        net.send(R.xr.at[i, c], R.rgx.at[zt], xn, rgx_s + k)
+    net.arrive(R.roa, roa_s)
+    part = wo_column(ax, ay)
+    part[...] = (part[...].astype(f32) + R.roa[...].astype(f32)).astype(bf16)
+    net.send(part, R.rof, near, rof_s)
+    for k in (3, 2, 1, 0):
+        zt = order[k]
+        i = zt * 2 + x
+        net.arrive(R.rgx.at[zt], rgx_s + k)
+        R.xr[i, c] = (
+            R.xr[i, c].astype(f32) + R.rgs[i].astype(f32) + R.rgx[zt].astype(f32)
+        ).astype(bf16)
+        net.send(
+            R.xr.at[i, c],
+            R.gnr.at[z % 2, c],
+            at(zt, x, y, back_c),
+            gnr_s + 2 * (z % 2) + c,
+            is_self=jnp.logical_and(zt == z, c == back_c),
+        )
+    for k in (3, 2, 1, 0):
+        q1_take(k)
+        if k:
+            q1_along(k)
+
+    net.arrive(R.rob, rob_s)
+    net.arrive(R.rof, rof_s)
+    part = wo_column(x, y)
+    part[...] = (part[...].astype(f32) + R.rob[...].astype(f32) + R.rof[...].astype(f32)).astype(bf16)
+    for k in (1, 2, 3):
+        net.send(wo_piece(order[k]), R.roz.at[z], at(order[k], x, y, c), roz_s + z)
+
+
     two_final(dw2_ref)
-    early = small_middle(0, early)
-
-    for b in range(2):
-        for cc in range(2):
-            net.arrive(R.gnr.at[b, cc], gnr_s + 2 * b + cc)
     sums = [jnp.zeros((1, 1024), f32) for _ in range(2)]
     for k in range(4):
+        net.arrive(R.gnr.at[k // 2, k % 2], gnr_s + k)
         rows = slice((k % 2) * 64, (k % 2) * 64 + 64)
         grad = R.gnr[k // 2, k % 2].astype(f32)
         scaled, inverse = row_stats(x_in[k // 2, k % 2].astype(f32))
@@ -1435,7 +1489,8 @@
     for xx, cc, dev in group:
         net.send(R.f1.at[xx, cc], R.r1f.at[g], dev, r1f_s + g)
     R.r1f[g] = R.f1[x, c]
-    q_final(R.fq)
+    q0_final(R.fq.at[:, :, :, 0:384])
+    q1_final(R.fq.at[:, :, :, 384:768])
     for xx, cc, dev in group:
         net.send(R.fq.at[xx, cc], R.rqf.at[g], dev, rqf_s + g)
     R.rqf[g] = R.fq[x, c]
@@ -1455,8 +1510,13 @@
         net.arrive(R.rqf.at[2 * xx + cc], rqf_s + 2 * xx + cc)
     for h in range(4):
         for t in range(3):
-            dwq_ref[:, t * 1024 + h * 256:t * 1024 + (h + 1) * 256] = R.rqf[h, :, t * 256:(t + 1) * 256]
-    sg_ref[...] = small_end(0, early) + small_end(1, late)
+            for pair in range(2):
+                src = pair * 384 + t * 128
+                dst = t * 1024 + h * 256 + pair * 128
+                dwq_ref[:, dst:dst + 128] = R.rqf[h, :, src:src + 128]
+    total = small_end(0, early) + small_end(1, late)
+    sg_ref[...] = pltpu.roll(total, (128 - 32 * d) % 128, 1)
+    sg_ref[5:6, :] = jnp.where(y == 0, total[5:6, :], total[6:7, :])
     net.settle(everything=True)
 
 
@@ -1476,16 +1536,6 @@
     contraction_shift,
     output_sensitivity,
 ):
-    docs, heads, blocks, count = sampled_target_tiles.shape
-    tiles = sampled_target_tiles.reshape(docs, heads * blocks, count)
-    extents = jnp.broadcast_to(valid_extents[:, None, None], (docs, heads * blocks, 1))
-    aux = jnp.concatenate([tiles, extents], axis=2)
-    aux = jnp.pad(aux, ((0, 0), (0, 0), (0, 124))).reshape(docs, 4, 64, 128)
-    line_one = jnp.concatenate(
-        [opening_scale_vector, opening_shift_vector, closing_scale_vector, closing_shift_vector]
-    )
-    line_two = jnp.pad(contraction_shift, (0, 96))
-    small = jnp.pad(jnp.stack([line_one, line_two, expansion_shift]), ((0, 5), (0, 0))).astype(f32)
     shapes = (
         (arriving_features.shape, bf16),
         (arriving_features.shape, f32),
@@ -1496,11 +1546,12 @@
         ((8, 128), f32),
     )
     whole = pl.BlockSpec(memory_space=pltpu.VMEM)
+    scalars = pl.BlockSpec(memory_space=pltpu.SMEM)
     made = pl.pallas_call(
         layer_kernel,
         name="layer",
         out_shape=[jax.ShapeDtypeStruct(a, b) for a, b in shapes],
-        in_specs=[whole] * 8,
+        in_specs=[whole] * 2 + [scalars] + [whole] * 11,
         out_specs=[whole] * 7,
         scratch_shapes=[pltpu.VMEM(a, b) for a, b in SCRATCH.values()]
         + [
@@ -1513,18 +1564,42 @@
     )(
         arriving_features.reshape(2, 2, 64, 1024),
         output_sensitivity,
-        aux,
+        valid_extents,
+        sampled_target_tiles,
         query_context_mapping,
         attention_outflow_weights,
         expansion_weights,
         contraction_weights,
-        small,
-    )
-    sums = made[6]
-    doc = lax.axis_index("doc")
-    narrow = lax.dynamic_slice(sums, (0, doc * 32), (5, 32))
-    up = lax.dynamic_slice(sums, (5 + doc // 2, 0), (1, 128))
-    return tuple(made[:6]) + (narrow[0], narrow[1], narrow[2], narrow[3], up[0], narrow[4])
+        opening_scale_vector.reshape(1, 32),
+        opening_shift_vector.reshape(1, 32),
+        closing_scale_vector.reshape(1, 32),
+        closing_shift_vector.reshape(1, 32),
+        expansion_shift.reshape(1, 128),
+        contraction_shift.reshape(1, 32),
+    )
+    place = pl.BlockSpec(memory_space=pl.ANY)
+    rows = ((1, 32), (1, 32), (1, 32), (1, 32), (1, 128), (1, 32))
+    done = pl.pallas_call(
+        leave_kernel,
+        name="leave",
+        out_shape=[jax.ShapeDtypeStruct(a, b) for a, b in shapes[:6]]
+        + [jax.ShapeDtypeStruct(a, f32) for a in rows],
+        in_specs=[place] * 6 + [whole],
+        out_specs=[place] * 6 + [whole] * 6,
+        scratch_shapes=[pltpu.SemaphoreType.DMA((6,))],
+    )(*made)
+    return tuple(done[:6]) + tuple(line.reshape(-1) for line in done[6:])
+
+
+def leave_kernel(*refs):
+    large, small, out, rows, sems = refs[:6], refs[6], refs[7:13], refs[13:19], refs[19]
+    copies = [pltpu.make_async_copy(large[k], out[k], sems.at[k]) for k in range(6)]
+    for copy in copies:
+        copy.start()
+    for k, row in enumerate((0, 1, 2, 3, 5, 4)):
+        rows[k][...] = small[row:row + 1, :rows[k].shape[1]]
+    for copy in copies:
+        copy.wait()
 
 
 def fits_fused(mesh, arguments):

time: 260 us -> 321 us (1.23)
  Pallas kernels: 246 us -> 318 us
  local copies, waits for them, and re-layouts: 12.3 us -> 1.76 us
    pallas_call x0 -> x1, Pallas kernels: none -> 97.7 us  [local_fused(): pl.pallas_call(leave_kernel, name='leave', out_shape=[jax.ShapeDtypeStruc...]
    pallas_call x1, Pallas kernels: 246 us -> 220 us  [local_fused(): pl.pallas_call(layer_kernel, name='layer', out_shape=[jax.ShapeDtypeStruc...]
    unnamed x33 -> x1, local copies, waits for them, and re-layouts: 8.85 us -> 1.76 us
where the time goes in v3:
time: 321 us; the launch traced here: 320 us
  Pallas kernels  318 us (99%)
    pallas_call x1, Pallas kernels, local_fused(): pl.pallas_call(layer_kernel, name='layer', out_shape=[jax.ShapeDtypeStruc...  220 us
    pallas_call x1, Pallas kernels, local_fused(): pl.pallas_call(leave_kernel, name='leave', out_shape=[jax.ShapeDtypeStruc...  97.7 us

profile of v3, /device:TPU:0, one launch (start us, length us, event | category | flops | bytes accessed | tf_op | source)
XLA Modules:
  0.0 320.4 jit_solution(15960856711261455294)
XLA Ops:
  0.6 1.8 copy.26.tiles_in
  2.4 220.2 %layer.1 = (bf16[2,128,1024]{2,1,0:T(8,128)(2,1)}, f32[2,128,1024]{2,1,0:T(8,128)}, f32[32,3072]{1,0:T(8,128)}, f32[32,1024]{1,0:T(8,128)}, f32[32,4096]{1,0:T(8...) custom-call(bf16[2,2,64,1024]{3,2,1,0:T(8,128)(2,1)} %bitcast.13, bf16[2,128,1024]{2,1,0:T(8,128)(2,1)} %dy_in.1, ...), custom_call_target="tpu_custom_call" | custom-call | tf_op jit(solution)/shard_map/layer/pallas_call | solution.py:1550
  222.6 97.7 %leave.1 = (bf16[2,128,1024]{2,1,0:T(8,128)(2,1)}, f32[2,128,1024]{2,1,0:T(8,128)}, f32[32,3072]{1,0:T(8,128)}, f32[32,1024]{1,0:T(8,128)}, f32[32,4096]{1,0:T(8...) custom-call(bf16[2,128,1024]{2,1,0:T(8,128)(2,1)} %get-tuple-element, ...), custom_call_target="tpu_custom_call" | custom-call | tf_op jit(solution)/shard_map/leave/pallas_call | solution.py:1582

commit v4 on v3

--- a/solution.py
+++ b/solution.py
@@ -1586,20 +1586,24 @@
         + [jax.ShapeDtypeStruct(a, f32) for a in rows],
         in_specs=[place] * 6 + [whole],
         out_specs=[place] * 6 + [whole] * 6,
-        scratch_shapes=[pltpu.SemaphoreType.DMA((6,))],
+        scratch_shapes=[pltpu.VMEM(a, b) for a, b in shapes[:6]]
+        + [pltpu.SemaphoreType.DMA((6,)), pltpu.SemaphoreType.DMA((6,))],
     )(*made)
     return tuple(done[:6]) + tuple(line.reshape(-1) for line in done[6:])
 
 
 def leave_kernel(*refs):
-    large, small, out, rows, sems = refs[:6], refs[6], refs[7:13], refs[13:19], refs[19]
-    copies = [pltpu.make_async_copy(large[k], out[k], sems.at[k]) for k in range(6)]
-    for copy in copies:
-        copy.start()
+    large, small, out, rows, held = refs[:6], refs[6], refs[7:13], refs[13:19], refs[19:25]
+    come, go = refs[25:]
+    for k in range(6):
+        pltpu.make_async_copy(large[k], held[k], come.at[k]).start()
     for k, row in enumerate((0, 1, 2, 3, 5, 4)):
         rows[k][...] = small[row:row + 1, :rows[k].shape[1]]
-    for copy in copies:
-        copy.wait()
+    for k in range(6):
+        pltpu.make_async_copy(large[k], held[k], come.at[k]).wait()
+        pltpu.make_async_copy(held[k], out[k], go.at[k]).start()
+    for k in range(6):
+        pltpu.make_async_copy(held[k], out[k], go.at[k]).wait()
 
 
 def fits_fused(mesh, arguments):

time: 321 us -> 227 us (0.71)
  Pallas kernels: 318 us -> 224 us
    pallas_call x1, Pallas kernels: 97.7 us -> 4.2 us  [local_fused(): pl.pallas_call(leave_kernel, name='leave', out_shape=[jax.ShapeDtypeStruc...]
where the time goes in v4:
time: 227 us
  Pallas kernels  224 us (99%)
    pallas_call x1, Pallas kernels, local_fused(): pl.pallas_call(layer_kernel, name='layer', out_shape=[jax.ShapeDtypeStruc...  220 us

profile of v4, /device:TPU:0, one launch (start us, length us, event | category | flops | bytes accessed | tf_op | source)
XLA Modules:
  0.0 227.0 jit_solution(10622862004161842126)
XLA Ops:
  0.6 1.8 copy.26.tiles_in
  2.4 220.2 %layer.1 = (bf16[2,128,1024]{2,1,0:T(8,128)(2,1)}, f32[2,128,1024]{2,1,0:T(8,128)}, f32[32,3072]{1,0:T(8,128)}, f32[32,1024]{1,0:T(8,128)}, f32[32,4096]{1,0:T(8...) custom-call(bf16[2,2,64,1024]{3,2,1,0:T(8,128)(2,1)} %bitcast.13, bf16[2,128,1024]{2,1,0:T(8,128)(2,1)} %dy_in.1, ...), custom_call_target="tpu_custom_call" | custom-call | tf_op jit(solution)/shard_map/layer/pallas_call | solution.py:1550
  222.6 4.2 %leave.1 = (bf16[2,128,1024]{2,1,0:T(8,128)(2,1)}, f32[2,128,1024]{2,1,0:T(8,128)}, f32[32,3072]{1,0:T(8,128)}, f32[32,1024]{1,0:T(8,128)}, f32[32,4096]{1,0:T(8...) custom-call(bf16[2,128,1024]{2,1,0:T(8,128)(2,1)} %get-tuple-element, ...), custom_call_target="tpu_custom_call" | custom-call | tf_op jit(solution)/shard_map/leave/pallas_call | solution.py:1582

commit v5 on v4

--- a/solution.py
+++ b/solution.py
@@ -652,6 +652,18 @@
 
 
 SCRATCH = dict(
+    x_in=((2, 2, 64, 1024), bf16),
+    dy_in=((2, 128, 1024), bf16),
+    wq_in=((32, 3072), bf16),
+    wo_in=((32, 1024), bf16),
+    w1_in=((32, 4096), bf16),
+    w2_in=((128, 1024), bf16),
+    out=((2, 128, 1024), bf16),
+    gx=((2, 128, 1024), f32),
+    dwq_out=((32, 3072), f32),
+    dwo=((32, 1024), f32),
+    dw1=((32, 4096), f32),
+    dw2_out=((128, 1024), f32),
     xr=((8, 2, 64, 1024), bf16),
     n1=((8, 128, 1024), bf16),
     aux=((64, 128), jnp.int32),
@@ -698,7 +710,8 @@
     r1z=((4, 2, 2, 32, 1024), bf16),
     r1v=((2, 2, 32, 1024), bf16),
     f1=((2, 2, 32, 1024), f32),
-    r1f=((4, 32, 1024), f32),
+    f1b=((2, 2, 32, 1024), bf16),
+    r1f=((4, 32, 1024), bf16),
     r2y=((4, 128, 1024), bf16),
     r2z=((4, 128, 1024), bf16),
     r2v=((128, 1024), bf16),
@@ -712,7 +725,8 @@
     rqz=((2, 4, 2, 2, 32, 384), bf16),
     rqv=((2, 2, 2, 32, 384), bf16),
     fq=((2, 2, 32, 768), f32),
-    rqf=((4, 32, 768), f32),
+    fqb=((2, 2, 32, 768), bf16),
+    rqf=((4, 32, 768), bf16),
     sg=((2, 8, 8, 128), f32),
     rsg=((2, 8, 8, 128), f32),
     sgt=((2, 8, 128), f32),
@@ -723,14 +737,36 @@
 
 
 def layer_kernel(
-    x_in, dy_in, extent_in, tiles_in, wq_in, wo_in, w1_in, w2_in,
+    x_arg, dy_arg, extent_in, tiles_in, wq_arg, wo_arg, w1_arg, w2_arg,
     gain_one, shift_one, gain_two, shift_two, shift_up, shift_down,
-    out_ref, gx_ref, dwq_ref, dwo_ref, dw1_ref, dw2_ref, sg_ref,
+    out_arg, gx_arg, dwq_arg, dwo_arg, dw1_arg, dw2_arg, sg_ref,
     *rest,
 ):
     names = list(SCRATCH)
     R = types.SimpleNamespace(**dict(zip(names, rest[: len(names)])))
-    send_sems, recv_sems = rest[len(names):]
+    send_sems, recv_sems, local_sems = rest[len(names):]
+    x_in, dy_in, wq_in, wo_in, w1_in, w2_in = R.x_in, R.dy_in, R.wq_in, R.wo_in, R.w1_in, R.w2_in
+    out_ref, gx_ref, dwq_ref, dwo_ref, dw1_ref, dw2_ref = R.out, R.gx, R.dwq_out, R.dwo, R.dw1, R.dw2_out
+    arrivals = [
+        pltpu.make_async_copy(src, dst, local_sems.at[k])
+        for k, (src, dst) in enumerate(
+            (
+                (wq_arg, wq_in), (x_arg, x_in), (w1_arg, w1_in),
+                (wo_arg, wo_in), (w2_arg, w2_in), (dy_arg, dy_in),
+            )
+        )
+    ]
+    for copy in arrivals:
+        copy.start()
+    leaving = [
+        pltpu.make_async_copy(src, dst, local_sems.at[6 + k])
+        for k, (src, dst) in enumerate(
+            (
+                (out_ref, out_arg), (gx_ref, gx_arg), (dwq_ref, dwq_arg),
+                (dwo_ref, dwo_arg), (dw1_ref, dw1_arg), (dw2_ref, dw2_arg),
+            )
+        )
+    ]
     s, d = lax.axis_index("seq"), lax.axis_index("doc")
     z, x, y, c = s // NX, s % NX, d // NC, d % NC
     g = 2 * x + c
@@ -758,6 +794,8 @@
     lax.fori_loop(1, 16, greet, 0)
     for cc in (c, flip):
         pl.semaphore_signal(barrier, inc=1, device_id=at(z, x, yo, cc), device_id_type=ROUTE)
+    for copy in arrivals:
+        copy.wait()
     for h in range(4):
         for t in range(3):
             for pair in range(2):
@@ -793,16 +831,14 @@
     pl.semaphore_wait(barrier, 17)
 
     def z_start(piece, base, name):
-        for k in (1, 2, 3):
-            net.send(
-                piece(z), piece(z), at(order[k], x, y, c), base + z, name, made=middle if k == 3 else None
-            )
+        for k in (1, 2):
+            net.send(piece(z), piece(z), at(order[k], x, y, c), base + z, name)
 
     def z_take(piece, base, name, k):
         part = piece(order[k])
         net.arrive(part, base + order[k])
-        if k == 3:
-            net.send(part, part, at(order[2], x, y, c), base + order[3], name, made=middle)
+        if k != 2:
+            net.send(part, part, at(order[2], x, y, c), base + order[k], name, made=middle)
         return part
 
     half = pl.ds(pl.multiple_of(c * 512, 512), 512)
@@ -1157,10 +1193,10 @@
     two_begin, two_take, two_along, two_final = scatter(
         lambda zz: R.dw2.at[zz, y], lambda zz: R.dw2.at[zz, yo], R.r2y, R.r2z, R.r2v, "s2"
     )
-    two_begin()
 
     for k in range(4):
         net.arrive(R.w2.at[order[k], yo], w2y + k)
+    two_begin()
 
     def narrow_back_rows(which):
         def narrow_back(j, _):
@@ -1405,6 +1441,7 @@
         where = slice(k * 128, k * 128 + 128)
         total = R.mid[where, :] + R.own[where, :] + R.opr[x, where, :].astype(f32)
         out_ref[k] = (total + R.opx[where, :].astype(f32) + R.vec[4:5, :]).astype(bf16)
+    leaving[0].start()
     attend_back(1)
 
     net.settle("xr")
@@ -1468,7 +1505,14 @@
         net.send(wo_piece(order[k]), R.roz.at[z], at(order[k], x, y, c), roz_s + z)
 
 
+    r1f_s, rqf_s = net.slots(4), net.slots(4)
+    one_final(R.f1)
+    R.f1b[...] = R.f1[...].astype(bf16)
+    for xx, cc, dev in group:
+        net.send(R.f1b.at[xx, cc], R.r1f.at[g], dev, r1f_s + g)
+    R.r1f[g] = R.f1b[x, c]
     two_final(dw2_ref)
+    leaving[5].start()
     sums = [jnp.zeros((1, 1024), f32) for _ in range(2)]
     for k in range(4):
         net.arrive(R.gnr.at[k // 2, k % 2], gnr_s + k)
@@ -1480,32 +1524,31 @@
         gx_ref[k // 2, rows, :] = R.gm[k * 64:(k + 1) * 64, :] + norm_pullback(
             grad, scaled, inverse, R.vec[0:1, :]
         )
+    leaving[1].start()
     for k in range(2):
         note(1, k, sums[k])
     late = small_begin(1)
 
-    r1f_s, rqf_s = net.slots(4), net.slots(4)
-    one_final(R.f1)
-    for xx, cc, dev in group:
-        net.send(R.f1.at[xx, cc], R.r1f.at[g], dev, r1f_s + g)
-    R.r1f[g] = R.f1[x, c]
     q0_final(R.fq.at[:, :, :, 0:384])
     q1_final(R.fq.at[:, :, :, 384:768])
+    R.fqb[...] = R.fq[...].astype(bf16)
     for xx, cc, dev in group:
-        net.send(R.fq.at[xx, cc], R.rqf.at[g], dev, rqf_s + g)
-    R.rqf[g] = R.fq[x, c]
+        net.send(R.fqb.at[xx, cc], R.rqf.at[g], dev, rqf_s + g)
+    R.rqf[g] = R.fqb[x, c]
     late = small_middle(1, late)
 
     dwo_ref[...] = wo_piece(z)[...].astype(f32)
     for k in (1, 2, 3):
         net.arrive(R.roz.at[order[k]], roz_s + order[k])
         dwo_ref[...] += R.roz[order[k]].astype(f32)
+    leaving[3].start()
     for xx, cc, dev in group:
         net.arrive(R.r1f.at[2 * xx + cc], r1f_s + 2 * xx + cc)
     for h in range(4):
         for q in range(8):
             block = 8 * (q // 2) + 4 * (h // 2) + 2 * (q % 2) + h % 2
-            dw1_ref[:, block * 128:(block + 1) * 128] = R.r1f[h, :, q * 128:(q + 1) * 128]
+            dw1_ref[:, block * 128:(block + 1) * 128] = R.r1f[h, :, q * 128:(q + 1) * 128].astype(f32)
+    leaving[4].start()
     for xx, cc, dev in group:
         net.arrive(R.rqf.at[2 * xx + cc], rqf_s + 2 * xx + cc)
     for h in range(4):
@@ -1513,11 +1556,14 @@
             for pair in range(2):
                 src = pair * 384 + t * 128
                 dst = t * 1024 + h * 256 + pair * 128
-                dwq_ref[:, dst:dst + 128] = R.rqf[h, :, src:src + 128]
+                dwq_ref[:, dst:dst + 128] = R.rqf[h, :, src:src + 128].astype(f32)
+    leaving[2].start()
     total = small_end(0, early) + small_end(1, late)
     sg_ref[...] = pltpu.roll(total, (128 - 32 * d) % 128, 1)
     sg_ref[5:6, :] = jnp.where(y == 0, total[5:6, :], total[6:7, :])
     net.settle(everything=True)
+    for copy in leaving:
+        copy.wait()
 
 
 def local_fused(
@@ -1547,16 +1593,18 @@
     )
     whole = pl.BlockSpec(memory_space=pltpu.VMEM)
     scalars = pl.BlockSpec(memory_space=pltpu.SMEM)
+    place = pl.BlockSpec(memory_space=pl.ANY)
     made = pl.pallas_call(
         layer_kernel,
         name="layer",
         out_shape=[jax.ShapeDtypeStruct(a, b) for a, b in shapes],
-        in_specs=[whole] * 2 + [scalars] + [whole] * 11,
-        out_specs=[whole] * 7,
+        in_specs=[place] * 2 + [scalars, whole] + [place] * 4 + [whole] * 6,
+        out_specs=[place] * 6 + [whole],
         scratch_shapes=[pltpu.VMEM(a, b) for a, b in SCRATCH.values()]
         + [
             pltpu.SemaphoreType.DMA((SENDS,)),
             pltpu.SemaphoreType.DMA((RECVS,)),
+            pltpu.SemaphoreType.DMA((12,)),
         ],
         compiler_params=pltpu.CompilerParams(
             collective_id=0, has_side_effects=True, vmem_limit_bytes=VMEM_BYTES
@@ -1577,7 +1625,6 @@
         expansion_shift.reshape(1, 128),
         contraction_shift.reshape(1, 32),
     )
-    place = pl.BlockSpec(memory_space=pl.ANY)
     rows = ((1, 32), (1, 32), (1, 32), (1, 32), (1, 128), (1, 32))
     done = pl.pallas_call(
         leave_kernel,

time: 227 us -> 225 us (level)
    pallas_call x1, Pallas kernels: 220 us -> 218 us  [local_fused(): pl.pallas_call(layer_kernel, name='layer', out_shape=[jax.ShapeDtypeStruc...]
where the time goes in v5:
time: 225 us; the launch traced here: 224 us
  Pallas kernels  222 us (99%)
    pallas_call x1, Pallas kernels, local_fused(): pl.pallas_call(layer_kernel, name='layer', out_shape=[jax.ShapeDtypeStruc...  218 us

profile of v5, /device:TPU:0, one launch (start us, length us, event | category | flops | bytes accessed | tf_op | source)
XLA Modules:
  0.0 224.5 jit_solution(8791780244490711214)
XLA Ops:
  0.6 1.8 copy.26.tiles_in
  2.4 217.7 %layer.1 = (bf16[2,128,1024]{2,1,0:T(8,128)(2,1)}, f32[2,128,1024]{2,1,0:T(8,128)}, f32[32,3072]{1,0:T(8,128)}, f32[32,1024]{1,0:T(8,128)}, f32[32,4096]{1,0:T(8...) custom-call(bf16[2,2,64,1024]{3,2,1,0:T(8,128)(2,1)} %bitcast.13, bf16[2,128,1024]{2,1,0:T(8,128)(2,1)} %dy_arg.1, ...), custom_call_target="tpu_custom_call" | custom-call | tf_op jit(solution)/shard_map/layer/pallas_call | solution.py:1597
  220.1 4.2 %leave.1 = (bf16[2,128,1024]{2,1,0:T(8,128)(2,1)}, f32[2,128,1024]{2,1,0:T(8,128)}, f32[32,3072]{1,0:T(8,128)}, f32[32,1024]{1,0:T(8,128)}, f32[32,4096]{1,0:T(8...) custom-call(bf16[2,128,1024]{2,1,0:T(8,128)(2,1)} %get-tuple-element, ...), custom_call_target="tpu_custom_call" | custom-call | tf_op jit(solution)/shard_map/leave/pallas_call | solution.py:1629

commit v6 on v5

--- a/solution.py
+++ b/solution.py
@@ -1530,12 +1530,12 @@
     late = small_begin(1)
 
     q0_final(R.fq.at[:, :, :, 0:384])
+    late = small_middle(1, late)
     q1_final(R.fq.at[:, :, :, 384:768])
     R.fqb[...] = R.fq[...].astype(bf16)
     for xx, cc, dev in group:
         net.send(R.fqb.at[xx, cc], R.rqf.at[g], dev, rqf_s + g)
     R.rqf[g] = R.fqb[x, c]
-    late = small_middle(1, late)
 
     dwo_ref[...] = wo_piece(z)[...].astype(f32)
     for k in (1, 2, 3):

time: 225 us -> 228 us (1.013)
  Pallas kernels: 222 us -> 225 us
    pallas_call x1, Pallas kernels: 218 us -> 221 us  [local_fused(): pl.pallas_call(layer_kernel, name='layer', out_shape=[jax.ShapeDtypeStruc...]
where the time goes in v6:
time: 228 us
  Pallas kernels  225 us (99%)
    pallas_call x1, Pallas kernels, local_fused(): pl.pallas_call(layer_kernel, name='layer', out_shape=[jax.ShapeDtypeStruc...  221 us

profile of v6, /device:TPU:0, one launch (start us, length us, event | category | flops | bytes accessed | tf_op | source)
XLA Modules:
  0.0 227.5 jit_solution(9993679535048131345)
XLA Ops:
  0.6 1.8 copy.26.tiles_in
  2.4 220.7 %layer.1 = (bf16[2,128,1024]{2,1,0:T(8,128)(2,1)}, f32[2,128,1024]{2,1,0:T(8,128)}, f32[32,3072]{1,0:T(8,128)}, f32[32,1024]{1,0:T(8,128)}, f32[32,4096]{1,0:T(8...) custom-call(bf16[2,2,64,1024]{3,2,1,0:T(8,128)(2,1)} %bitcast.13, bf16[2,128,1024]{2,1,0:T(8,128)(2,1)} %dy_arg.1, ...), custom_call_target="tpu_custom_call" | custom-call | tf_op jit(solution)/shard_map/layer/pallas_call | solution.py:1597
  223.1 4.2 %leave.1 = (bf16[2,128,1024]{2,1,0:T(8,128)(2,1)}, f32[2,128,1024]{2,1,0:T(8,128)}, f32[32,3072]{1,0:T(8,128)}, f32[32,1024]{1,0:T(8,128)}, f32[32,4096]{1,0:T(8...) custom-call(bf16[2,128,1024]{2,1,0:T(8,128)(2,1)} %get-tuple-element, ...), custom_call_target="tpu_custom_call" | custom-call | tf_op jit(solution)/shard_map/leave/pallas_call | solution.py:1629
